TPU v7x, 32 devices: a whole 2x2x4 slice. The times are simulated.
32 devices in a mesh: ctx: 8 (over z, core), ch: 4 (over y, x).
Axes of the slice: x: 2, y: 2, z: 4, core: 2. Of those that a mesh axis runs over, the one named last changes fastest.
Arguments:
- tokens: bfloat16 [1024, 8192], P('ctx', 'ch'), may hold values from -6 to 6
- w_in: bfloat16 [8192, 3, 4096], P('ctx', None, 'ch'), may hold values from -0.0625 to 0.0625
- short_filter: float32 [3, 3, 4096], P(None, None, 'ch'), may hold values from -3 to 3
- decay_rate: float32 [256, 16], P('ch'), may hold values from 0.00048828125 to 0.1
- residue: float32 [256, 16], P('ch'), may hold values from -1.5 to 1.5
- skip: float32 [4096], P('ch'), may hold values from -6 to 6
Outputs:
- block_out: bfloat16 [1024, 4096], P('ctx', 'ch')
All inputs are finite; a program needn't handle non-finite values.
Results may differ from a plain program's by a relative error of at most 0.011.
Values may be sent and summed in bfloat16 or wider, within the bound.
No kernel may reach another device: no remote copies, remote signals or barrier semaphores. Data moves between devices by JAX's collectives and lax.ppermute only.
A program may use at most 128 MiB of HBM per device.

v0:
```python
import math

import jax
import jax.numpy as jnp
from jax import lax
from jax.sharding import PartitionSpec as P

GROUP = 16


def shifted(block, axis, distance):
    devices = range(lax.axis_size(axis))
    route = [(i - distance, i) for i in devices if i - distance in devices]
    return lax.ppermute(block, axis, route)


def short_mix(projected, short_filter_taps, block_len, local_width):
    rounded = lax.optimization_barrier(projected.astype(jnp.bfloat16))
    proj_rows = rounded.astype(jnp.float32).reshape(
        block_len + 2, short_filter_taps.shape[1], local_width
    )
    return (
        short_filter_taps[0] * proj_rows[2:]
        + short_filter_taps[1] * proj_rows[1:-1]
        + short_filter_taps[2] * proj_rows[:-2]
    )


def split_parts(weight_full):
    upper_triangle_part = weight_full.astype(jnp.bfloat16)
    lower_triangle_part = (weight_full - upper_triangle_part.astype(jnp.float32)).astype(
        jnp.bfloat16
    )
    return (upper_triangle_part, lower_triangle_part)


def decay_sum(weight_full, input_half_rows):
    upper_triangle_part, lower_triangle_part = split_parts(weight_full)
    first_sum = jnp.einsum(
        "lbu,lvu->lbv", upper_triangle_part, input_half_rows, preferred_element_type=jnp.float32
    )
    second_partial_sum = jnp.einsum(
        "lbu,lvu->lbv", lower_triangle_part, input_half_rows, preferred_element_type=jnp.float32
    )
    return first_sum + second_partial_sum


def local(tokens, w_in, short_filter, decay_rate, residue, skip):
    block_len = tokens.shape[0]
    local_width = w_in.shape[2]
    group_count = local_width // GROUP
    gathered = lax.all_gather(tokens, "ch", axis=1, tiled=True)
    previous = shifted(gathered[block_len - 2 :], "ctx", 1)
    extended = jnp.concatenate([previous, gathered], axis=0)
    shard_piece = lax.all_gather(w_in, "ctx", axis=0, tiled=True)
    flat_piece = shard_piece.reshape(shard_piece.shape[0], -1)
    proj_all = jnp.dot(extended, flat_piece, preferred_element_type=jnp.float32)
    short_mixed = short_mix(proj_all, short_filter, block_len, local_width)
    query_part = short_mixed[:, 0]
    key_part = short_mixed[:, 1]
    value_part = short_mixed[:, 2]
    gated_input = (key_part * value_part).astype(jnp.bfloat16)
    input_t = gated_input.T
    columns_t = input_t.reshape(group_count, GROUP, block_len)
    pole_weight = residue * jnp.sqrt(2.0 * decay_rate)
    positions = jnp.arange(block_len).astype(jnp.float32)
    near_filter = jnp.einsum(
        "gr,grl->gl",
        pole_weight,
        jnp.exp(-decay_rate[:, :, None] * positions[None, None, :]),
        precision=lax.Precision.HIGHEST,
    )
    padded_filter = jnp.concatenate(
        [
            jnp.zeros((group_count, block_len - 1), jnp.float32),
            near_filter,
            jnp.zeros((group_count, 1), jnp.float32),
        ],
        axis=1,
    )

    def near_one(item_pair):
        filter_row, tok_block = item_pair
        span_len = 2 * block_len - 1
        tiled_rows = jnp.tile(filter_row, block_len)[: block_len * span_len].reshape(
            block_len, span_len
        )
        toeplitz = tiled_rows[:, block_len - 1 :]
        upper_triangle_part, lower_triangle_part = split_parts(toeplitz)
        return jnp.dot(
            tok_block, upper_triangle_part, preferred_element_type=jnp.float32
        ) + jnp.dot(tok_block, lower_triangle_part, preferred_element_type=jnp.float32)

    near_field = lax.map(near_one, (padded_filter, columns_t), batch_size=2)
    my_start = lax.axis_index("ctx") * block_len
    empty_state = jnp.zeros((group_count, decay_rate.shape[1], GROUP), jnp.float32)
    shard_piece = lax.all_gather(input_t, "ctx", axis=1, tiled=True)
    piece_len = shard_piece.shape[1]
    sub_len = math.gcd(piece_len, block_len)

    def sub_step(turn_index, carried):
        part_cols = lax.dynamic_slice_in_dim(shard_piece, turn_index * sub_len, sub_len, 1)
        distance = (my_start - 1 - turn_index * sub_len - jnp.arange(sub_len)).astype(jnp.float32)
        decay_factor_weight = jnp.where(
            distance[None, None, :] >= 0.0,
            jnp.exp(-decay_rate[:, :, None] * jnp.maximum(distance, 0.0)[None, None, :]),
            0.0,
        )
        part_input = part_cols.reshape(group_count, GROUP, sub_len)
        return carried + decay_sum(decay_factor_weight, part_input)

    past_state = lax.fori_loop(0, piece_len // sub_len, sub_step, empty_state)
    far_weight = pole_weight[:, :, None] * jnp.exp(
        -decay_rate[:, :, None] * (positions + 1.0)[None, None, :]
    )
    distant_field_output = jnp.einsum(
        "grc,gri->gci", past_state, far_weight, precision=lax.Precision.HIGHEST
    )
    long_out = (near_field + distant_field_output).reshape(local_width, block_len).T
    return (query_part * (long_out + skip * gated_input.astype(jnp.float32))).astype(jnp.bfloat16)


def solution(mesh):
    return jax.shard_map(
        local,
        mesh=mesh,
        in_specs=(
            P("ctx", "ch"),
            P("ctx", None, "ch"),
            P(None, None, "ch"),
            P("ch", None),
            P("ch", None),
            P("ch"),
        ),
        out_specs=P("ctx", "ch"),
        check_vma=False,
    )
```

profile of v0, /device:TPU:0, one launch (start us, length us, event | category | flops | bytes accessed | tf_op | source)
XLA Modules:
  0.0 593.6 jit_solution(9194431997208698956)
XLA Ops:
  6.5 0.7 all-gather.4.cloned.1.call-update
  7.3 8.7 %copy.16 = bf16[1024,3,1024]{0,2,1:T(8,128)(2,1)} copy(bf16[1024,3,1024]{2,0,1:T(8,128)(2,1)} %param.11) | data formatting | bytes 12582912 | tf_op args[1]
  16.0 0.6 copy-done.4
  16.9 0.6 slice_bitcast_fusion.3
  17.6 0.7 fusion.32
  18.3 28.9 %all-gather.4.cloned.1.call-done = bf16[128,8192]{1,0:T(8,128)(2,1)} async-done(((bf16[128,2048]{1,0:T(8,128)(2,1)}), bf16[128,8192]{1,0:T(8,128)(2,1)}) %all-gather.4.cloned.1.call-update) | async-done | bytes 2097168 | tf_op jit(solution)/shard_map/all_gather | solution.py:52
  47.3 0.9 slice.60
  48.2 1.7 collective-permute-start
  49.9 0.5 broadcast_add_fusion
  50.5 0.7 reshape.64
  51.2 425.1 %all-gather.6.cloned.1.call-done = bf16[8192,3,1024]{0,2,1:T(8,128)(2,1)} async-done(((bf16[1024,3,1024]{0,2,1:T(8,128)(2,1)}), bf16[8192,3,1024]{0,2,1:T(8,128)(2,1)}) %all-gather.6.cloned.1.call-update) | async-done | bytes 50331664 | tf_op jit(solution)/shard_map/all_gather | solution.py:55
  476.3 22.6 %convolution_convert_fusion = bf16[130,3072]{1,0:T(8,128)(2,1)S(1)} fusion(bf16[8192,3072]{0,1:T(8,128)(2,1)} %bitcast.89, bf16[128,8192]{1,0:T(8,128)(2,1)} %all-gather.4.cloned.1.call-done, bf16[2,8192]{1,0:T(2,128)(2,1)S(1)} %collective-permute-done), kind=kOutput, calls=%fused_computation.34 | convolution fusion | flops 6547773440 | bytes 53260288 | tf_op jit(solution)/shard_map/dot_general | solution.py:57
  498.9 2.2 fusion.41
  501.1 3.0 copy.19
  504.2 3.0 copy.18
  507.2 1.6 copy.17
  508.8 3.7 multiply_add_fusion
  512.6 0.8 fusion.47
  513.4 56.9 %while.26 = (s32[]{:T(128)}, f32[32,2,16,128]{3,2,1,0:T(8,128)S(1)}, bf16[32,2,16,128]{3,2,1,0:T(8,128)(2,1)S(1)}, f32[32,2,256]{2,1,0:T(2,128)}, s32[]{:T(128)}) while((s32[]{:T(128)}, f32[32,2,16,128]{3,2,1,0:T(8,128)S(1)}, bf16[32,2,16,128]{3,2,1,0:T(8,128)(2,1)S(1)}, f32[32,2,256]{2,1,0:T(2,128)}, s32[]{:T(128)}) %tuple.71), condition=%wide.region_1.2_spmd, body=%wide.region_0.1_spmd.sunk | while | flops 2232322 | bytes 2100301 | solution.py:94
  513.4 0.7 dynamic-slice_bitcast_fusion.2
  515.2 0.7 dynamic-slice_bitcast_fusion.2
  517.0 0.7 dynamic-slice_bitcast_fusion.2
  518.7 0.7 dynamic-slice_bitcast_fusion.2
  519.7 0.4 reshape.72
  520.5 0.7 dynamic-slice_bitcast_fusion.2
  522.3 0.7 dynamic-slice_bitcast_fusion.2
  524.1 0.7 dynamic-slice_bitcast_fusion.2
  525.9 0.7 dynamic-slice_bitcast_fusion.2
  527.7 0.7 dynamic-slice_bitcast_fusion.2
  528.6 0.4 reshape.72
  529.4 0.7 dynamic-slice_bitcast_fusion.2
  531.2 0.6 dynamic-slice_bitcast_fusion.2
  533.0 0.7 dynamic-slice_bitcast_fusion.2
  534.7 0.7 dynamic-slice_bitcast_fusion.2
  536.5 0.7 dynamic-slice_bitcast_fusion.2
  538.3 0.7 dynamic-slice_bitcast_fusion.2
  540.1 0.7 dynamic-slice_bitcast_fusion.2
  541.8 0.6 dynamic-slice_bitcast_fusion.2
  543.6 0.7 dynamic-slice_bitcast_fusion.2
  545.4 0.7 dynamic-slice_bitcast_fusion.2
  547.1 0.7 dynamic-slice_bitcast_fusion.2
  548.9 0.7 dynamic-slice_bitcast_fusion.2
  550.7 0.6 dynamic-slice_bitcast_fusion.2
  552.4 0.7 dynamic-slice_bitcast_fusion.2
  554.2 0.6 dynamic-slice_bitcast_fusion.2
  556.0 0.7 dynamic-slice_bitcast_fusion.2
  557.8 0.7 dynamic-slice_bitcast_fusion.2
  559.5 0.7 dynamic-slice_bitcast_fusion.2
  561.3 0.7 dynamic-slice_bitcast_fusion.2
  563.1 0.7 dynamic-slice_bitcast_fusion.2
  564.9 0.7 dynamic-slice_bitcast_fusion.2
  566.7 0.7 dynamic-slice_bitcast_fusion.2
  568.4 0.7 dynamic-slice_bitcast_fusion.2
  570.2 14.4 %while.27 = (s32[]{:T(128)}, f32[64,16,16]{2,1,0:T(8,128)S(1)}, s32[]{:T(128)}, f32[64,16,1]{1,0,2:T(8,128)S(1)}, bf16[1024,1024]{1,0:T(8,128)(2,1)}, /*index=5*/s32[]{:T(128)}, s32[]{:T(128)}, s32[]{:T(128)}, s32[]{:T(128)}) while((s32[]{:T(128)}, f32[64,16,16]{2,1,0:T(8,128)S(1)}, s32[]{:T(128)}, f32[64,16,1]{1,0,2:T(8,128)S(1)}, ...), condition=%wide.region_3.4_spmd.clone, body=%wide.region_2.3_spmd.clone.sunk | while | flops 9618184 | bytes 1321013 | solution.py:112
  570.2 1.0 constant_dynamic-slice_fusion.2
  572.1 1.0 constant_dynamic-slice_fusion.2
  573.8 1.0 constant_dynamic-slice_fusion.2
  575.7 1.0 constant_dynamic-slice_fusion.2
  577.5 1.0 constant_dynamic-slice_fusion.2
  579.3 1.0 constant_dynamic-slice_fusion.2
  581.1 1.0 constant_dynamic-slice_fusion.2
  582.9 1.0 constant_dynamic-slice_fusion.2
  584.7 1.3 convolution_add_fusion.2
  586.2 0.9 copy.23
  (258 shorter events, 40.7 us)
Async XLA Ops:
  6.5 40.7 %all-gather.4.cloned.1.call-start = ((), (), s32[]{:S(2)}) async-start(), calls=%async_computation | async-start | bytes 2621440 | tf_op jit(solution)/shard_map/all_gather | solution.py:52
  7.3 469.0 %all-gather.6.cloned.1.call-start = ((), (), s32[]{:S(2)}) async-start(), calls=%async_computation.1 | async-start | bytes 56623104 | tf_op jit(solution)/shard_map/all_gather | solution.py:55
  16.0 0.7 copy-start.4
  16.0 0.8 copy-start.5
  16.0 1.0 copy-start.3
  16.0 554.2 %all-gather.8.cloned.1.call-start = ((), (), s32[]{:S(2)}) async-start(), calls=%async_computation.2 | async-start | bytes 2359296 | tf_op jit(solution)/shard_map/all_gather | solution.py:97
  48.2 3.0 collective-permute-start
  507.2 1.6 copy-start
  507.2 1.6 copy-start.1
  507.2 1.6 copy-start.2
  570.2 14.4 %copy-start.7 = (f32[128]{0:T(128)S(1)}, f32[128]{0:T(128)}, u32[]{:S(2)}) copy-start(f32[128]{0:T(128)} %broadcast_add_fusion) | copy-start | bytes 1540
  584.6 1.3 copy-start.6
Sparse Core Ops, SparseCore 0:
  9.2 38.0 all-gather.3
  48.9 427.3 all-gather.5
  513.5 29.1 all-gather.7
where the time goes:
time: 595 us; the launch traced here: 594 us
  waiting for transfers between devices  455 us (76%)
  local copies, waits for them, and re-layouts  72.8 us (12%)
  matrix products  44.3 us (7%)
  between operations  13.2 us (2%)
    all_gather x1, waiting for transfers between devices, local(): shard_piece = lax.all_gather(w_in, 'ctx', axis=0, tiled=True)  425 us
    all_gather x1, waiting for transfers between devices, local(): gathered = lax.all_gather(tokens, 'ch', axis=1, tiled=True)  28.9 us
    dot_general x1, matrix products, local(): proj_all = jnp.dot(extended, flat_piece, preferred_element_type=jnp.float32)  22.6 us
    another operation x32, local copies, waits for them, and re-layouts, near_one(): jnp.tile(filter_row, block_len)[:block_len * span_len]  21.6 us
    reshape x32, local copies, waits for them, and re-layouts, near_one(): jnp.tile(filter_row, block_len)[:block_len * span_len]  13 us
  transfers between devices with their start and end apart: 4, of which 2 were waited for; matrix products, arithmetic and copies ran while one was open for 12% of the time, Pallas kernels for 0%

commit v1 on v0

v1 whole, which is shorter than its diff:
```python
import jax
import jax.numpy as jnp
from jax import lax
from jax.experimental import pallas as pl
from jax.experimental.pallas import tpu as pltpu
from jax.sharding import PartitionSpec as P

GROUP = 16
CHUNK = 128
F32 = jnp.float32
BF16 = jnp.bfloat16


def pick(blocks, index):
    chosen = blocks[0]
    for i in range(1, len(blocks)):
        chosen = jnp.where(index == i, blocks[i], chosen)
    return chosen


def swap_cores(block, n_ctx):
    return lax.ppermute(block, "ctx", [(i, i ^ 1) for i in range(n_ctx)])


def to_plane(block, distance, planes):
    route = [(2 * z + c, 2 * (z ^ distance) + c) for z in range(planes) for c in range(2)]
    return lax.ppermute(block, "ctx", route)


def to_column(block, distance, n_ch):
    return lax.ppermute(block, "ch", [(j, j ^ distance) for j in range(n_ch)])


def spread_tokens(tokens, z, me, planes, n_ch):
    rows = tokens.shape[0] // n_ch
    pieces = tokens.reshape(n_ch, rows, tokens.shape[1])
    got = []
    for s in range(n_ch):
        piece = lax.dynamic_index_in_dim(pieces, me ^ s, 0, keepdims=False)
        got.append(to_column(piece, s, n_ch) if s else piece)
    came = []
    for u in range(planes):
        piece = pick(got, me ^ z ^ u)
        came.append(to_plane(piece, u, planes) if u else piece)
    return jnp.concatenate([pick(came, z ^ k) for k in range(planes)], axis=0)


def project_kernel(planes, where_ref, x_own, x_sib, w_own, w_sib, *outs):
    turn = pl.program_id(0)
    sums = jnp.dot(x_own[...], w_own[0], preferred_element_type=F32)
    sums += jnp.dot(x_sib[...], w_sib[0], preferred_element_type=F32)
    sums = sums.astype(BF16)
    lanes = sums.shape[1] // 2
    for r in range(planes):

        @pl.when(turn == r)
        def _():
            outs[r][0, 0] = sums[:, :lanes]
            outs[r][1, 0] = sums[:, lanes:]


def project(x, w_own, w_sib, z, core, planes):
    rows, wide = x.shape
    depth, width = w_own.shape[1:]
    across = width // planes
    lanes = across // 2
    if lanes % 128:
        halves = x.reshape(rows, 2, depth)
        x_own = lax.dynamic_index_in_dim(halves, core, 1, keepdims=False)
        x_sib = lax.dynamic_index_in_dim(halves, 1 - core, 1, keepdims=False)
        sums = jnp.einsum("tk,jkc->tjc", x_own, w_own, preferred_element_type=F32)
        sums += jnp.einsum("tk,jkc->tjc", x_sib, w_sib, preferred_element_type=F32)
        sums = sums.astype(BF16).reshape(rows, 3, planes, 2, lanes).transpose(2, 3, 1, 0, 4)
        return [
            lax.dynamic_index_in_dim(sums, (z + r) % planes, 0, keepdims=False)
            for r in range(planes)
        ]

    def out_at(r):
        def at(turn, j, where):
            return 0, jnp.where(turn == r, j, jnp.where(turn < r, 0, 2)), 0, 0

        return at

    def w_at(turn, j, where):
        return j, 0, (where[0] + turn) % planes

    return pl.pallas_call(
        lambda *refs: project_kernel(planes, *refs),
        grid_spec=pltpu.PrefetchScalarGridSpec(
            num_scalar_prefetch=1,
            grid=(planes, 3),
            in_specs=[
                pl.BlockSpec((rows, depth), lambda turn, j, where: (0, where[1])),
                pl.BlockSpec((rows, depth), lambda turn, j, where: (0, 1 - where[1])),
                pl.BlockSpec((1, depth, across), w_at),
                pl.BlockSpec((1, depth, across), w_at),
            ],
            out_specs=[pl.BlockSpec((2, 1, rows, lanes), out_at(r)) for r in range(planes)],
        ),
        out_shape=[jax.ShapeDtypeStruct((2, 3, rows, lanes), BF16)] * planes,
        compiler_params=pltpu.CompilerParams(vmem_limit_bytes=32 << 20),
        cost_estimate=pl.CostEstimate(
            flops=2 * rows * wide * 3 * width,
            bytes_accessed=2 * (wide * 3 * width + rows * wide + rows * 3 * width),
            transcendentals=0,
        ),
        name="project",
    )(jnp.stack([z, core]).astype(jnp.int32), x, x, w_own, w_sib)


def add(*blocks):
    total = blocks[0].astype(F32)
    for block in blocks[1:]:
        total = total + block.astype(F32)
    return total.astype(BF16)


def reduce_planes(streams, planes):
    last = planes - 1
    up, down = [None] * len(streams), [None] * len(streams)
    for t in range(last):
        up_route = [(2 * z + c, 2 * z + 2 + c) for z in range(min(t + 1, last)) for c in range(2)]
        down_route = [(2 * (last - z) + c, 2 * (last - z) - 2 + c) for z in range(min(t + 1, last)) for c in range(2)]
        for i, blocks in enumerate(streams):
            sent_up, sent_down = blocks[last - t], blocks[t + 1]
            if t:
                sent_up, sent_down = add(sent_up, up[i]), add(sent_down, down[i])
            up[i] = lax.ppermute(sent_up, "ctx", up_route)
            down[i] = lax.ppermute(sent_down, "ctx", down_route)
    return [add(blocks[0], up[i], down[i]) for i, blocks in enumerate(streams)]


def long_filters(decay, weight):
    lag = jnp.arange(CHUNK)
    apart = lag[:, None] - lag[None, :]
    away = jnp.maximum(apart, 0).astype(F32)
    near = jnp.sum(
        weight[:, :, None, None] * jnp.exp(-decay[:, :, None, None] * away[None, None]), axis=1
    )
    near = jnp.where(apart[None] >= 0, near, 0.0)
    poles = decay.reshape(-1)
    position = lag.astype(F32)
    collect = jnp.exp(-poles[:, None] * (CHUNK - 1 - position)[None, :])
    emit = weight.reshape(-1)[None, :] * jnp.exp(-poles[None, :] * (position + 1.0)[:, None])
    return near, collect, emit, jnp.exp(-CHUNK * poles)[:, None]


def halves_of(value):
    high = value.astype(BF16)
    return high, (value - high.astype(F32)).astype(BF16)


def mix_kernel(order, parts, planes, n_ch, where_ref, *refs):
    data, (taps, skip, near, collect, emit, keep), refs = refs[:parts], refs[parts : parts + 6], refs[parts + 6 :]
    outs, (proj, long_in, done) = refs[:planes], refs[planes:]
    core, me, z = where_ref[0], where_ref[1], where_ref[2]
    lanes = skip.shape[1]
    groups = near.shape[0]
    proj[:, 0:8] = jnp.zeros((3, 8, lanes), F32)
    rows = CHUNK // n_ch
    for (side, first, pieces), ref in zip(order, data, strict=True):
        owner = core if side == 0 else 1 - core
        for s in range(pieces):
            for k in range(planes):
                at = (2 * k + owner) * CHUNK + (me ^ (first + s)) * rows + 8
                start = (s * planes + k) * rows
                for j in range(3):
                    proj[j, pl.ds(pl.multiple_of(at, 8), rows)] = ref[j, start : start + rows].astype(F32)

    lane_group = lax.broadcasted_iota(jnp.int32, (1, lanes), 1) // GROUP
    pole_group = lax.broadcasted_iota(jnp.int32, (collect.shape[0], lanes), 0) // (collect.shape[0] // groups)
    same = pole_group == lane_group
    collect2 = jnp.concatenate(halves_of(collect[...]), axis=1)
    emit_high, emit_low = halves_of(emit[...])
    emit3 = jnp.concatenate([emit_high, emit_low, emit_high], axis=1)
    state = jnp.zeros(same.shape, F32)
    chunks = 2 * planes
    for n in range(chunks):
        mixed = []
        for j in range(3):
            total = 0.0
            for lag in range(3):
                total += taps[lag, j : j + 1] * proj[j, 8 - lag + n * CHUNK : 8 - lag + (n + 1) * CHUNK]
            mixed.append(total)
        gated = (mixed[1] * mixed[2]).astype(BF16)
        gated2 = jnp.concatenate([gated, gated], axis=0)
        long_out = skip[...] * gated.astype(F32)
        if n:
            state_high, state_low = halves_of(state)
            long_out += jnp.dot(
                emit3, jnp.concatenate([state_high, state_high, state_low], axis=0), preferred_element_type=F32
            )
        if n < chunks - 1:
            fresh = jnp.dot(collect2, gated2, preferred_element_type=F32)
            state = keep[...] * state + jnp.where(same, fresh, 0.0)
        long_in[n // 2, n % 2] = gated2
        done[n * CHUNK : (n + 1) * CHUNK] = long_out
        proj[0, 8 + n * CHUNK - 8 : n * CHUNK + CHUNK] = mixed[0]
    for g in range(groups):
        near2 = jnp.concatenate(halves_of(near[g]), axis=1)
        mine = lane_group == g
        for k in range(planes):
            pair = jnp.concatenate([long_in[k, 0], long_in[k, 1]], axis=1)
            both = jnp.dot(near2, pair, preferred_element_type=F32)
            for c in range(2):
                at = slice((2 * k + c) * CHUNK, (2 * k + c + 1) * CHUNK)
                done[at] += jnp.where(mine, both[:, c * lanes : (c + 1) * lanes], 0.0)
    for u in range(planes):
        at = pl.multiple_of((z ^ u) * 2 * CHUNK, CHUNK)
        both = proj[0, pl.ds(at, 2 * CHUNK)] * done[pl.ds(at, 2 * CHUNK)]
        outs[u][...] = both.astype(BF16).reshape(2, CHUNK, lanes)


def mix(own, sib, pieces, taps, skip, filters, core, me, z, planes, n_ch):
    lanes = skip.shape[0]
    if lanes % 128:
        return mix_plainly(own, sib, taps, skip, filters, core, me, z, planes, n_ch)
    order, data, first = [], [], 0
    for i, count in enumerate(pieces):
        order += [(0, first, count), (1, first, count)]
        data += [own[i], sib[i]]
        first += count
    poles = filters[1].shape[0]
    length = 2 * planes * CHUNK
    vmem = pl.BlockSpec(memory_space=pltpu.VMEM)
    return pl.pallas_call(
        lambda *refs: mix_kernel(order, len(data), planes, n_ch, *refs),
        in_specs=[pl.BlockSpec(memory_space=pltpu.SMEM)] + [vmem] * (len(data) + 6),
        out_specs=[vmem] * planes,
        out_shape=[jax.ShapeDtypeStruct((2, CHUNK, lanes), BF16)] * planes,
        scratch_shapes=[
            pltpu.VMEM((3, length + 8, lanes), F32),
            pltpu.VMEM((planes, 2, 2 * CHUNK, lanes), BF16),
            pltpu.VMEM((length, lanes), F32),
        ],
        compiler_params=pltpu.CompilerParams(vmem_limit_bytes=32 << 20),
        cost_estimate=pl.CostEstimate(
            flops=2 * length * lanes * (2 * CHUNK * filters[0].shape[0] + 5 * poles),
            bytes_accessed=2 * 4 * length * lanes,
            transcendentals=0,
        ),
        name="mix",
    )(
        jnp.stack([core, me, z]).astype(jnp.int32), *data, taps, skip[None], *filters
    )


def mix_plainly(own, sib, taps, skip, filters, core, me, z, planes, n_ch):
    lanes = skip.shape[0]
    near, collect, emit, keep = filters
    groups, rows = near.shape[0], CHUNK // n_ch
    sides = []
    for side in (own, sib):
        blocks = jnp.concatenate(side, axis=1).reshape(3, n_ch, planes, rows, lanes)
        sides.append(jnp.stack([lax.dynamic_index_in_dim(blocks, me ^ s, 1, keepdims=False) for s in range(n_ch)], 2))
    both = jnp.stack([pick(sides, core), pick(sides, 1 - core)], axis=2)
    proj = both.reshape(3, -1, lanes).astype(F32)
    length = proj.shape[1]
    padded = jnp.pad(proj, ((0, 0), (2, 0), (0, 0)))
    mixed = sum(taps[lag][:, None] * padded[:, 2 - lag : 2 - lag + length] for lag in range(3))
    gated = lax.optimization_barrier((mixed[1] * mixed[2]).astype(BF16)).astype(F32)
    chunks = length // CHUNK
    columns = gated.reshape(chunks, CHUNK, groups, GROUP)
    high = lax.Precision.HIGHEST
    out = jnp.einsum("gij,njgc->nigc", near, columns, precision=high)
    fresh = jnp.einsum("grj,njgc->ngrc", collect.reshape(groups, -1, CHUNK), columns, precision=high)
    state, states = jnp.zeros_like(fresh[0]), []
    for n in range(chunks):
        states.append(state)
        state = keep.reshape(groups, -1, 1) * state + fresh[n]
    out += jnp.einsum("igr,ngrc->nigc", emit.reshape(CHUNK, groups, -1), jnp.stack(states), precision=high)
    out = (mixed[0] * (out.reshape(length, lanes) + skip * gated)).astype(BF16)
    out = out.reshape(planes, 2, CHUNK, lanes)
    return [lax.dynamic_index_in_dim(out, z ^ u, 0, keepdims=False) for u in range(planes)]


def local(tokens, w_in, short_filter, decay_rate, residue, skip):
    n_ctx, n_ch = lax.axis_size("ctx"), lax.axis_size("ch")
    planes = n_ctx // 2
    ctx, me = lax.axis_index("ctx"), lax.axis_index("ch")
    z, core = ctx // 2, ctx % 2
    lanes = w_in.shape[2] // n_ctx
    groups = lanes // GROUP

    w_own = w_in.transpose(1, 0, 2)
    w_sib = swap_cores(w_own, n_ctx)
    x = [spread_tokens(tokens, z, me, planes, n_ch)]
    for s in range(1, n_ch):
        x.append(to_column(x[0], s, n_ch))
    half = n_ch // 2
    streams = [
        project(jnp.concatenate(part, axis=0), w_own, w_sib, z, core, planes) for part in (x[:half], x[half:])
    ]
    summed = reduce_planes(streams, planes)
    own = [lax.dynamic_index_in_dim(block, core, 0, keepdims=False) for block in summed]
    sib = [
        swap_cores(lax.dynamic_index_in_dim(block, 1 - core, 0, keepdims=False), n_ctx) for block in summed
    ]

    mine = lambda a, count, axis: lax.dynamic_slice_in_dim(a, ctx * count, count, axis)
    decay = mine(decay_rate, groups, 0)
    weight = mine(residue, groups, 0) * jnp.sqrt(2.0 * decay)
    outs = mix(
        own,
        sib,
        [half, n_ch - half],
        mine(short_filter, lanes, 2),
        mine(skip, lanes, 0),
        long_filters(decay, weight),
        core,
        me,
        z,
        planes,
        n_ch,
    )
    came = jnp.stack([to_plane(block, u, planes) if u else block for u, block in enumerate(outs)])
    keep = lax.dynamic_index_in_dim(came, core, 1, keepdims=False)
    given = swap_cores(lax.dynamic_index_in_dim(came, 1 - core, 1, keepdims=False), n_ctx)
    pairs = [jnp.where(core == 0, keep, given), jnp.where(core == 0, given, keep)]
    columns = [pick([pairs[c][u] for u in range(planes)], z ^ k) for k in range(planes) for c in range(2)]
    return jnp.concatenate(columns, axis=1)


def solution(mesh):
    return jax.shard_map(
        local,
        mesh=mesh,
        in_specs=(
            P("ctx", "ch"),
            P("ctx", None, "ch"),
            P(None, None, "ch"),
            P("ch", None),
            P("ch", None),
            P("ch"),
        ),
        out_specs=P("ctx", "ch"),
        check_vma=False,
    )
```

time: 595 us -> 134 us (0.23)
  waiting for transfers between devices: 455 us -> 37.5 us
  local copies, waits for them, and re-layouts: 72.8 us -> 3.82 us
  starting transfers between devices: 1.82 us -> 50.6 us
  matrix products: 44.3 us -> 0 us
  Pallas kernels: 0 us -> 26.1 us
  between operations: 13.2 us -> 0.44 us
  other arithmetic: 5.42 us -> 14.1 us
    all_gather x3 -> x0, waiting for transfers between devices: 454 us -> none  [the longest x1 425 us: local(): shard_piece = lax.all_gather(w_in, 'ctx', axis=0, tiled=True)]
    ppermute x1 -> x28, starting transfers between devices: 1.74 us -> 50.6 us  [the longest x6 24 us: reduce_planes(): up[i] = lax.ppermute(sent_up, 'ctx', up_route)]
    dot_general x83 -> x0, matrix products: 44.3 us -> none  [the longest x1 22.6 us: local(): proj_all = jnp.dot(extended, flat_piece, preferred_element_type=jnp.float32)]
    ppermute x1 -> x28, waiting for transfers between devices: 0.01 us -> 37.5 us  [the longest x6 15.3 us: to_plane(): return lax.ppermute(block, 'ctx', route)]
    pallas_call x0 -> x3, Pallas kernels: none -> 26.1 us  [the longest x2 23.3 us: project(): pl.pallas_call(lambda *refs: project_kernel(planes, *refs), grid_spec=plt...]
    another operation x32 -> x0, local copies, waits for them, and re-layouts: 21.6 us -> none  [near_one(): jnp.tile(filter_row, block_len)[:block_len * span_len]]
    reshape x33 -> x0, local copies, waits for them, and re-layouts: 13.6 us -> none  [the longest x32 13 us: near_one(): jnp.tile(filter_row, block_len)[:block_len * span_len]]
    slice x37 -> x0, local copies, waits for them, and re-layouts: 11.5 us -> none  [the longest x2 3.85 us: short_mix(): proj_rows[2:]]
  transfers between devices with their start and end apart: 4 -> 28, of which waited for: 2 -> 14; matrix products, arithmetic and copies ran while one was open for 12% -> 12% of each run, Pallas kernels for 0% -> 18%
where the time goes in v1:
time: 134 us; the launch traced here: 133 us
  starting transfers between devices  50.6 us (38%)
  waiting for transfers between devices  37.5 us (28%)
  Pallas kernels  26.1 us (19%)
  other arithmetic  14.1 us (11%)
  local copies, waits for them, and re-layouts  3.82 us (3%)
    ppermute x6, starting transfers between devices, reduce_planes(): up[i] = lax.ppermute(sent_up, 'ctx', up_route)  24 us
    pallas_call x2, Pallas kernels, project(): pl.pallas_call(lambda *refs: project_kernel(planes, *refs), grid_spec=plt...  23.3 us
    ppermute x6, waiting for transfers between devices, to_plane(): return lax.ppermute(block, 'ctx', route)  15.3 us
    ppermute x6, waiting for transfers between devices, to_column(): return lax.ppermute(block, 'ch', [(j, j ^ distance) for j in range(n_ch)])  14.7 us
    ppermute x6, starting transfers between devices, to_plane(): return lax.ppermute(block, 'ctx', route)  11.4 us
    convert_element_type x8, other arithmetic, add(): return total.astype(BF16)  8.37 us
    ppermute x6, starting transfers between devices, to_column(): return lax.ppermute(block, 'ch', [(j, j ^ distance) for j in range(n_ch)])  7.8 us
    ppermute x6, starting transfers between devices, reduce_planes(): down[i] = lax.ppermute(sent_down, 'ctx', down_route)  6.77 us
  transfers between devices with their start and end apart: 28, of which 14 were waited for; matrix products, arithmetic and copies ran while one was open for 12% of the time, Pallas kernels for 18%

profile of v1, /device:TPU:0, one launch (start us, length us, event | category | flops | bytes accessed | tf_op | source)
XLA Modules:
  0.0 132.6 jit_solution(1617405905145627942)
XLA Ops:
  0.0 0.5 collective-permute-start.7
  0.5 1.1 dynamic-slice_bitcast_fusion.5
  1.5 3.5 %collective-permute-start = (bf16[32,2048]{1,0:T(8,128)(2,1)S(1)}, bf16[32,2048]{1,0:T(8,128)(2,1)S(1)}, u32[]{:S(2)}, u32[]{:S(2)}) collective-permute-start(bf16[32,2048]{1,0:T(8,128)(2,1)S(1)} %get-tuple-element.43), channel_id=1, source_target_pairs={{0,3},{1,2},{2,1},{3,0},{4,7},{5,6},{6,5},{7,4},{8,11},{9,10},{10,... | collective-permute-start | bytes 393224 | tf_op jit(solution)/shard_map/ppermute | solution.py:31
  5.1 0.5 collective-permute-start.1
  5.6 0.1 collective-permute-start.2
  5.7 0.8 constant_dynamic-slice_fusion
  6.7 2.6 %collective-permute-done = bf16[32,2048]{1,0:T(8,128)(2,1)S(1)} collective-permute-done((bf16[32,2048]{1,0:T(8,128)(2,1)S(1)}, bf16[32,2048]{1,0:T(8,128)(2,1)S(1)}, u32[]{:S(2)}, u32[]{:S(2)}) %collective-permute-start) | collective-permute-done | bytes 131104 | tf_op jit(solution)/shard_map/ppermute | solution.py:31
  9.3 2.7 %collective-permute-done.1 = bf16[32,2048]{1,0:T(8,128)(2,1)S(1)} collective-permute-done((bf16[32,2048]{1,0:T(8,128)(2,1)S(1)}, bf16[32,2048]{1,0:T(8,128)(2,1)S(1)}, u32[]{:S(2)}, u32[]{:S(2)}) %collective-permute-start.1) | collective-permute-done | bytes 131104 | tf_op jit(solution)/shard_map/ppermute | solution.py:31
  12.0 0.3 collective-permute-done.2
  12.3 1.0 fusion.9
  13.3 3.7 %collective-permute-start.3 = (bf16[32,2048]{1,0:T(8,128)(2,1)S(1)}, bf16[32,2048]{1,0:T(8,128)(2,1)S(1)}, u32[]{:S(2)}, u32[]{:S(2)}) collective-permute-start(bf16[32,2048]{1,0:T(8,128)(2,1)S(1)} %get-tuple-element.40), channel_id=1, source_target_pairs={{0,24},{4,28},{8,16},{12,20},{16,8},{20,12},{24,0},{28,4},{1,25},{... | collective-permute-start | bytes 393224 | tf_op jit(solution)/shard_map/ppermute | solution.py:27
  16.9 0.8 collective-permute-start.5
  17.7 0.1 pad_add_fusion.1.refs_0_
  17.8 3.8 %collective-permute-done.3 = bf16[32,2048]{1,0:T(8,128)(2,1)S(1)} collective-permute-done((bf16[32,2048]{1,0:T(8,128)(2,1)S(1)}, bf16[32,2048]{1,0:T(8,128)(2,1)S(1)}, u32[]{:S(2)}, u32[]{:S(2)}) %collective-permute-start.3) | collective-permute-done | bytes 131104 | tf_op jit(solution)/shard_map/ppermute | solution.py:27
  21.6 6.5 %collective-permute-done.4 = bf16[32,2048]{1,0:T(8,128)(2,1)S(1)} collective-permute-done((bf16[32,2048]{1,0:T(8,128)(2,1)S(1)}, bf16[32,2048]{1,0:T(8,128)(2,1)S(1)}, u32[]{:S(2)}, u32[]{:S(2)}) %collective-permute-start.4) | collective-permute-done | bytes 131104 | tf_op jit(solution)/shard_map/ppermute | solution.py:27
  28.1 1.0 constant_dynamic-update-slice_fusion.4
  29.3 0.1 constant_dynamic-update-slice_fusion.1
  29.4 1.6 %collective-permute-start.6 = (bf16[128,2048]{1,0:T(8,128)(2,1)S(1)}, bf16[128,2048]{1,0:T(8,128)(2,1)S(1)}, u32[]{:S(2)}, u32[]{:S(2)}) collective-permute-start(bf16[128,2048]{1,0:T(8,128)(2,1)S(1)} %pad_maximum_fusion.1), channel_id=1, source_target_pairs={{0,1},{1,0},{2,3},{3,2},{4,5},{5,4},{6,7},{7,6},{8,9},{9,8},{10,11... | collective-permute-start | bytes 1572872 | tf_op jit(solution)/shard_map/ppermute | solution.py:31
  31.0 2.1 %multiply_reduce_fusion = f32[8,128,128]{2,1,0:T(8,128)S(1)} fusion(f32[128,128]{1,0:T(8,128)S(1)} %maximum_convert_fusion, f32[8,16]{1,0:T(8,128)S(1)} %get-tuple-element.55, f32[8,16]{1,0:T(8,128)S(1)} %get-tuple-element.56), kind=kLoop, calls=%fused_computation | loop fusion | flops 6160384 | bytes 590848 | tf_op jit(solution)/shard_map/reduce_sum | solution.py:138
  33.2 1.6 %collective-permute-start.16 = (bf16[128,2048]{1,0:T(8,128)(2,1)S(1)}, bf16[128,2048]{1,0:T(8,128)(2,1)S(1)}, u32[]{:S(2)}, u32[]{:S(2)}) collective-permute-start(bf16[128,2048]{1,0:T(8,128)(2,1)S(1)} %pad_maximum_fusion.1), channel_id=1, source_target_pairs={{0,3},{1,2},{2,1},{3,0},{4,7},{5,6},{6,5},{7,4},{8,11},{9,10},{10,... | collective-permute-start | bytes 1572872 | tf_op jit(solution)/shard_map/ppermute | solution.py:31
  34.7 0.5 collective-permute-start.15
  35.3 9.1 %collective-permute-done.6 = bf16[128,2048]{1,0:T(8,128)(2,1)S(1)} collective-permute-done((bf16[128,2048]{1,0:T(8,128)(2,1)S(1)}, bf16[128,2048]{1,0:T(8,128)(2,1)S(1)}, u32[]{:S(2)}, u32[]{:S(2)}) %collective-permute-start.6) | collective-permute-done | bytes 524320 | tf_op jit(solution)/shard_map/ppermute | solution.py:31
  44.4 11.6 %project.2 = (bf16[2,3,256,128]{3,2,1,0:T(8,128)(2,1)S(1)}, bf16[2,3,256,128]{3,2,1,0:T(8,128)(2,1)S(1)}, bf16[2,3,256,128]{3,2,1,0:T(8,128)(2,1)S(1)}, bf16[2,3,256,128]{3,2,1,0:T(8,128)(2,1)S(1)}) custom-call(s32[2]{0:T(128)S(1)} %pad_add_fusion.1.refs_0_, bf16[256,2048]{1,0:T(8,128)(2,1)S(1)} %constant_dynamic-update-slice_fusion.refs_1_.refs_2_, ...), custom_call_target="tpu_custom_call" | custom-call | flops 3221225472 | bytes 15204352 | tf_op jit(solution)/shard_map/project/pallas_call | solution.py:88
  56.1 1.8 %collective-permute-start.8 = (bf16[2,3,256,128]{3,2,1,0:T(8,128)(2,1)S(1)}, bf16[2,3,256,128]{3,2,1,0:T(8,128)(2,1)S(1)}, u32[]{:S(2)}, u32[]{:S(2)}) collective-permute-start(bf16[2,3,256,128]{3,2,1,0:T(8,128)(2,1)S(1)} %get-tuple-element.20), channel_id=1, source_target_pairs={{0,8},{4,12},{1,9},{5,13},{2,10},{6,14},{3,11},{7,15}} | collective-permute-start | bytes 1179656 | tf_op jit(solution)/shard_map/ppermute | solution.py:129
  57.9 0.7 collective-permute-start.11
  58.6 0.1 pad_maximum_fusion.refs_1_.refs_2_
  58.7 11.6 %project.3 = (bf16[2,3,256,128]{3,2,1,0:T(8,128)(2,1)S(1)}, bf16[2,3,256,128]{3,2,1,0:T(8,128)(2,1)S(1)}, bf16[2,3,256,128]{3,2,1,0:T(8,128)(2,1)S(1)}, bf16[2,3,256,128]{3,2,1,0:T(8,128)(2,1)S(1)}) custom-call(s32[2]{0:T(128)S(1)} %pad_add_fusion.1.refs_0_, bf16[256,2048]{1,0:T(8,128)(2,1)S(1)} %pad_maximum_fusion.refs_1_.refs_2_, ...), custom_call_target="tpu_custom_call" | custom-call | flops 3221225472 | bytes 15204352 | tf_op jit(solution)/shard_map/project/pallas_call | solution.py:88
  70.3 2.4 %collective-permute-start.17 = (bf16[2,3,256,128]{3,2,1,0:T(8,128)(2,1)S(1)}, bf16[2,3,256,128]{3,2,1,0:T(8,128)(2,1)}, u32[]{:S(2)}, u32[]{:S(2)}) collective-permute-start(bf16[2,3,256,128]{3,2,1,0:T(8,128)(2,1)S(1)} %get-tuple-element.24), channel_id=1, source_target_pairs={{0,8},{4,12},{1,9},{5,13},{2,10},{6,14},{3,11},{7,15}} | collective-permute-start | bytes 1179656 | tf_op jit(solution)/shard_map/ppermute | solution.py:129
  72.7 1.4 %collective-permute-start.20 = (bf16[2,3,256,128]{3,2,1,0:T(8,128)(2,1)S(1)}, bf16[2,3,256,128]{3,2,1,0:T(8,128)(2,1)}, u32[]{:S(2)}, u32[]{:S(2)}) collective-permute-start(bf16[2,3,256,128]{3,2,1,0:T(8,128)(2,1)S(1)} %get-tuple-element.22), channel_id=1, source_target_pairs={{24,16},{28,20},{25,17},{29,21},{26,18},{30,22},{27,19},{31,23}} | collective-permute-start | bytes 1179656 | tf_op jit(solution)/shard_map/ppermute | solution.py:130
  74.1 1.1 fusion
  75.2 1.4 %collective-permute-start.12 = (bf16[2,3,256,128]{3,2,1,0:T(8,128)(2,1)}, bf16[2,3,256,128]{3,2,1,0:T(8,128)(2,1)}, u32[]{:S(2)}, u32[]{:S(2)}) collective-permute-start(bf16[2,3,256,128]{3,2,1,0:T(8,128)(2,1)} %get-tuple-element.53), channel_id=1, source_target_pairs={{24,16},{28,20},{16,8},{20,12},{25,17},{29,21},{17,9},{21,13},{26,... | collective-permute-start | bytes 1179656 | tf_op jit(solution)/shard_map/ppermute | solution.py:130
  76.6 0.1 pad_add_fusion.refs_0_
  76.7 1.3 collective-permute-start.9
  78.0 2.3 %collective-permute-done.17 = bf16[2,3,256,128]{3,2,1,0:T(8,128)(2,1)} collective-permute-done((bf16[2,3,256,128]{3,2,1,0:T(8,128)(2,1)S(1)}, bf16[2,3,256,128]{3,2,1,0:T(8,128)(2,1)}, u32[]{:S(2)}, u32[]{:S(2)}) %collective-permute-start.17) | collective-permute-done | bytes 393248 | tf_op jit(solution)/shard_map/ppermute | solution.py:129
  80.3 1.3 fusion.2
  81.6 0.7 collective-permute-start.21
  82.3 5.1 %collective-permute-start.18 = (bf16[2,3,256,128]{3,2,1,0:T(8,128)(2,1)S(1)}, bf16[2,3,256,128]{3,2,1,0:T(8,128)(2,1)S(1)}, u32[]{:S(2)}, u32[]{:S(2)}) collective-permute-start(bf16[2,3,256,128]{3,2,1,0:T(8,128)(2,1)S(1)} %get-tuple-element.48), channel_id=1, source_target_pairs={{0,8},{4,12},{8,16},{12,20},{1,9},{5,13},{9,17},{13,21},{2,10},{6,... | collective-permute-start | bytes 1179656 | tf_op jit(solution)/shard_map/ppermute | solution.py:129
  87.5 1.1 add_convert_fusion.4
  88.6 1.3 collective-permute-start.13
  89.9 0.9 add_convert_fusion.5
  90.7 7.6 %collective-permute-start.10 = (bf16[2,3,256,128]{3,2,1,0:T(8,128)(2,1)}, bf16[2,3,256,128]{3,2,1,0:T(8,128)(2,1)}, u32[]{:S(2)}, u32[]{:S(2)}) collective-permute-start(bf16[2,3,256,128]{3,2,1,0:T(8,128)(2,1)} %add_convert_fusion.5), channel_id=1, source_target_pairs={{0,8},{4,12},{8,16},{12,20},{16,24},{20,28},{1,9},{5,13},{9,17},{1... | collective-permute-start | bytes 1179656 | tf_op jit(solution)/shard_map/ppermute | solution.py:129
  98.4 0.8 add_convert_fusion.1
  99.2 1.3 collective-permute-start.22
  100.5 0.9 add_convert_fusion.2
  101.4 5.8 %collective-permute-start.19 = (bf16[2,3,256,128]{3,2,1,0:T(8,128)(2,1)}, bf16[2,3,256,128]{3,2,1,0:T(8,128)(2,1)}, u32[]{:S(2)}, u32[]{:S(2)}) collective-permute-start(bf16[2,3,256,128]{3,2,1,0:T(8,128)(2,1)} %add_convert_fusion.2), channel_id=1, source_target_pairs={{0,8},{4,12},{8,16},{12,20},{16,24},{20,28},{1,9},{5,13},{9,17},{1... | collective-permute-start | bytes 1179656 | tf_op jit(solution)/shard_map/ppermute | solution.py:129
  107.2 0.8 dynamic-slice_bitcast_fusion.8.refs_6_
  107.9 0.1 neg.20
  108.0 0.1 mul.101
  108.1 0.1 exp.27.refs_10_
  108.2 1.2 add_convert_fusion.3
  109.5 0.1 collective-permute-done.22
  109.6 2.4 %collective-permute-done.19 = bf16[2,3,256,128]{3,2,1,0:T(8,128)(2,1)} collective-permute-done((bf16[2,3,256,128]{3,2,1,0:T(8,128)(2,1)}, bf16[2,3,256,128]{3,2,1,0:T(8,128)(2,1)}, u32[]{:S(2)}, u32[]{:S(2)}) %collective-permute-start.19) | collective-permute-done | bytes 393248 | tf_op jit(solution)/shard_map/ppermute | solution.py:129
  112.0 1.2 add_convert_fusion
  113.3 0.1 exponential_multiply_fusion
  113.4 1.3 collective-permute-done.23.refs_4_
  114.7 2.8 %mix.1 = (bf16[2,128,128]{2,1,0:T(8,128)(2,1)S(1)}, bf16[2,128,128]{2,1,0:T(8,128)(2,1)S(1)}, bf16[2,128,128]{2,1,0:T(8,128)(2,1)S(1)}, bf16[2,128,128]{2,1,0:T(8,128)(2,1)S(1)}) custom-call(s32[3]{0:T(128)S(1)} %pad_add_fusion.refs_0_, bf16[3,256,128]{2,1,0:T(8,128)(2,1)S(1)} %get-tuple-element.51.refs_1_, ...), custom_call_target="tpu_custom_call" | custom-call | flops 704643072 | bytes 1048576 | tf_op jit(solution)/shard_map/mix/pallas_call | solution.py:227
  117.6 6.3 %collective-permute-start.26 = (bf16[2,128,128]{2,1,0:T(8,128)(2,1)S(1)}, bf16[2,128,128]{2,1,0:T(8,128)(2,1)S(1)}, u32[]{:S(2)}, u32[]{:S(2)}) collective-permute-start(bf16[2,128,128]{2,1,0:T(8,128)(2,1)S(1)} %get-tuple-element.28), channel_id=1, source_target_pairs={{0,24},{4,28},{8,16},{12,20},{16,8},{20,12},{24,0},{28,4},{1,25},{... | collective-permute-start | bytes 196616 | tf_op jit(solution)/shard_map/ppermute | solution.py:27
  123.9 0.6 collective-permute-start.24
  124.5 2.2 %collective-permute-done.26 = bf16[2,128,128]{2,1,0:T(8,128)(2,1)S(1)} collective-permute-done((bf16[2,128,128]{2,1,0:T(8,128)(2,1)S(1)}, bf16[2,128,128]{2,1,0:T(8,128)(2,1)S(1)}, u32[]{:S(2)}, u32[]{:S(2)}) %collective-permute-start.26) | collective-permute-done | bytes 65568 | tf_op jit(solution)/shard_map/ppermute | solution.py:27
  126.8 2.4 %collective-permute-done.25 = bf16[2,128,128]{2,1,0:T(8,128)(2,1)S(1)} collective-permute-done((bf16[2,128,128]{2,1,0:T(8,128)(2,1)S(1)}, bf16[2,128,128]{2,1,0:T(8,128)(2,1)S(1)}, u32[]{:S(2)}, u32[]{:S(2)}) %collective-permute-start.25) | collective-permute-done | bytes 65568 | tf_op jit(solution)/shard_map/ppermute | solution.py:27
  129.2 0.3 collective-permute-done.24
  129.7 1.3 %collective-permute-done.27 = bf16[4,128,128]{2,1,0:T(8,128)(2,1)S(1)} collective-permute-done((bf16[4,128,128]{2,1,0:T(8,128)(2,1)S(1)}, bf16[4,128,128]{2,1,0:T(8,128)(2,1)S(1)}, u32[]{:S(2)}, u32[]{:S(2)}) %collective-permute-start.27) | collective-permute-done | bytes 131104 | tf_op jit(solution)/shard_map/ppermute | solution.py:22
  131.3 0.7 copy-done.2
  132.0 0.6 bitcast_dynamic-update-slice_fusion
  (48 shorter events, 1.1 us)
Async XLA Ops:
  0.0 76.7 %copy-start = (f32[3,3,1024]{2,1,0:T(4,128)S(1)}, f32[3,3,1024]{2,1,0:T(4,128)}, u32[]{:S(2)}) copy-start(f32[3,3,1024]{2,1,0:T(4,128)} %param.8) | copy-start | bytes 110596
  0.0 44.4 %collective-permute-start.7 = (bf16[3,1024,1024]{2,1,0:T(8,128)(2,1)}, bf16[3,1024,1024]{2,1,0:T(8,128)(2,1)}, u32[]{:S(2)}, u32[]{:S(2)}) collective-permute-start(bf16[3,1024,1024]{2,1,0:T(8,128)(2,1)} %bitcast.68), channel_id=1, source_target_pairs={{0,4},{4,0},{8,12},{12,8},{16,20},{20,16},{24,28},{28,24},{1,5},{5... | collective-permute-start | bytes 18874376 | tf_op jit(solution)/shard_map/ppermute | solution.py:22
  1.5 7.8 %collective-permute-start = (bf16[32,2048]{1,0:T(8,128)(2,1)S(1)}, bf16[32,2048]{1,0:T(8,128)(2,1)S(1)}, u32[]{:S(2)}, u32[]{:S(2)}) collective-permute-start(bf16[32,2048]{1,0:T(8,128)(2,1)S(1)} %get-tuple-element.43), channel_id=1, source_target_pairs={{0,3},{1,2},{2,1},{3,0},{4,7},{5,6},{6,5},{7,4},{8,11},{9,10},{10,... | collective-permute-start | bytes 393224 | tf_op jit(solution)/shard_map/ppermute | solution.py:31
  5.1 6.9 %collective-permute-start.1 = (bf16[32,2048]{1,0:T(8,128)(2,1)S(1)}, bf16[32,2048]{1,0:T(8,128)(2,1)S(1)}, u32[]{:S(2)}, u32[]{:S(2)}) collective-permute-start(bf16[32,2048]{1,0:T(8,128)(2,1)S(1)} %get-tuple-element.42), channel_id=1, source_target_pairs={{0,2},{1,3},{2,0},{3,1},{4,6},{5,7},{6,4},{7,5},{8,10},{9,11},{10,... | collective-permute-start | bytes 393224 | tf_op jit(solution)/shard_map/ppermute | solution.py:31
  5.6 6.7 %collective-permute-start.2 = (bf16[32,2048]{1,0:T(8,128)(2,1)S(1)}, bf16[32,2048]{1,0:T(8,128)(2,1)S(1)}, u32[]{:S(2)}, u32[]{:S(2)}) collective-permute-start(bf16[32,2048]{1,0:T(8,128)(2,1)S(1)} %get-tuple-element.41), channel_id=1, source_target_pairs={{0,1},{1,0},{2,3},{3,2},{4,5},{5,4},{6,7},{7,6},{8,9},{9,8},{10,11... | collective-permute-start | bytes 393224 | tf_op jit(solution)/shard_map/ppermute | solution.py:31
  13.3 8.3 %collective-permute-start.3 = (bf16[32,2048]{1,0:T(8,128)(2,1)S(1)}, bf16[32,2048]{1,0:T(8,128)(2,1)S(1)}, u32[]{:S(2)}, u32[]{:S(2)}) collective-permute-start(bf16[32,2048]{1,0:T(8,128)(2,1)S(1)} %get-tuple-element.40), channel_id=1, source_target_pairs={{0,24},{4,28},{8,16},{12,20},{16,8},{20,12},{24,0},{28,4},{1,25},{... | collective-permute-start | bytes 393224 | tf_op jit(solution)/shard_map/ppermute | solution.py:27
  16.9 11.2 %collective-permute-start.4 = (bf16[32,2048]{1,0:T(8,128)(2,1)S(1)}, bf16[32,2048]{1,0:T(8,128)(2,1)S(1)}, u32[]{:S(2)}, u32[]{:S(2)}) collective-permute-start(bf16[32,2048]{1,0:T(8,128)(2,1)S(1)} %get-tuple-element.39), channel_id=1, source_target_pairs={{0,16},{4,20},{8,24},{12,28},{16,0},{20,4},{24,8},{28,12},{1,17},{... | collective-permute-start | bytes 393224 | tf_op jit(solution)/shard_map/ppermute | solution.py:27
  16.9 11.2 %collective-permute-start.5 = (bf16[32,2048]{1,0:T(8,128)(2,1)S(1)}, bf16[32,2048]{1,0:T(8,128)(2,1)S(1)}, u32[]{:S(2)}, u32[]{:S(2)}) collective-permute-start(bf16[32,2048]{1,0:T(8,128)(2,1)S(1)} %get-tuple-element.38), channel_id=1, source_target_pairs={{0,8},{4,12},{8,0},{12,4},{16,24},{20,28},{24,16},{28,20},{1,9},{5... | collective-permute-start | bytes 393224 | tf_op jit(solution)/shard_map/ppermute | solution.py:27
  17.8 26.6 %copy-start.1 = (bf16[1024,3,1024]{2,0,1:T(8,128)(2,1)S(1)}, bf16[1024,3,1024]{2,0,1:T(8,128)(2,1)}, u32[]{:S(2)}) copy-start(bf16[1024,3,1024]{2,0,1:T(8,128)(2,1)} %param.7) | copy-start | bytes 18874372
  29.4 14.9 %collective-permute-start.6 = (bf16[128,2048]{1,0:T(8,128)(2,1)S(1)}, bf16[128,2048]{1,0:T(8,128)(2,1)S(1)}, u32[]{:S(2)}, u32[]{:S(2)}) collective-permute-start(bf16[128,2048]{1,0:T(8,128)(2,1)S(1)} %pad_maximum_fusion.1), channel_id=1, source_target_pairs={{0,1},{1,0},{2,3},{3,2},{4,5},{5,4},{6,7},{7,6},{8,9},{9,8},{10,11... | collective-permute-start | bytes 1572872 | tf_op jit(solution)/shard_map/ppermute | solution.py:31
  33.2 25.4 %collective-permute-start.16 = (bf16[128,2048]{1,0:T(8,128)(2,1)S(1)}, bf16[128,2048]{1,0:T(8,128)(2,1)S(1)}, u32[]{:S(2)}, u32[]{:S(2)}) collective-permute-start(bf16[128,2048]{1,0:T(8,128)(2,1)S(1)} %pad_maximum_fusion.1), channel_id=1, source_target_pairs={{0,3},{1,2},{2,1},{3,0},{4,7},{5,6},{6,5},{7,4},{8,11},{9,10},{10,... | collective-permute-start | bytes 1572872 | tf_op jit(solution)/shard_map/ppermute | solution.py:31
  34.7 23.8 %collective-permute-start.15 = (bf16[128,2048]{1,0:T(8,128)(2,1)S(1)}, bf16[128,2048]{1,0:T(8,128)(2,1)S(1)}, u32[]{:S(2)}, u32[]{:S(2)}) collective-permute-start(bf16[128,2048]{1,0:T(8,128)(2,1)S(1)} %pad_maximum_fusion.1), channel_id=1, source_target_pairs={{0,2},{1,3},{2,0},{3,1},{4,6},{5,7},{6,4},{7,5},{8,10},{9,11},{10,... | collective-permute-start | bytes 1572872 | tf_op jit(solution)/shard_map/ppermute | solution.py:31
  56.1 18.0 %collective-permute-start.8 = (bf16[2,3,256,128]{3,2,1,0:T(8,128)(2,1)S(1)}, bf16[2,3,256,128]{3,2,1,0:T(8,128)(2,1)S(1)}, u32[]{:S(2)}, u32[]{:S(2)}) collective-permute-start(bf16[2,3,256,128]{3,2,1,0:T(8,128)(2,1)S(1)} %get-tuple-element.20), channel_id=1, source_target_pairs={{0,8},{4,12},{1,9},{5,13},{2,10},{6,14},{3,11},{7,15}} | collective-permute-start | bytes 1179656 | tf_op jit(solution)/shard_map/ppermute | solution.py:129
  57.9 16.3 %collective-permute-start.11 = (bf16[2,3,256,128]{3,2,1,0:T(8,128)(2,1)S(1)}, bf16[2,3,256,128]{3,2,1,0:T(8,128)(2,1)S(1)}, u32[]{:S(2)}, u32[]{:S(2)}) collective-permute-start(bf16[2,3,256,128]{3,2,1,0:T(8,128)(2,1)S(1)} %get-tuple-element.18), channel_id=1, source_target_pairs={{24,16},{28,20},{25,17},{29,21},{26,18},{30,22},{27,19},{31,23}} | collective-permute-start | bytes 1179656 | tf_op jit(solution)/shard_map/ppermute | solution.py:130
  70.3 10.0 %collective-permute-start.17 = (bf16[2,3,256,128]{3,2,1,0:T(8,128)(2,1)S(1)}, bf16[2,3,256,128]{3,2,1,0:T(8,128)(2,1)}, u32[]{:S(2)}, u32[]{:S(2)}) collective-permute-start(bf16[2,3,256,128]{3,2,1,0:T(8,128)(2,1)S(1)} %get-tuple-element.24), channel_id=1, source_target_pairs={{0,8},{4,12},{1,9},{5,13},{2,10},{6,14},{3,11},{7,15}} | collective-permute-start | bytes 1179656 | tf_op jit(solution)/shard_map/ppermute | solution.py:129
  72.7 7.6 %collective-permute-start.20 = (bf16[2,3,256,128]{3,2,1,0:T(8,128)(2,1)S(1)}, bf16[2,3,256,128]{3,2,1,0:T(8,128)(2,1)}, u32[]{:S(2)}, u32[]{:S(2)}) collective-permute-start(bf16[2,3,256,128]{3,2,1,0:T(8,128)(2,1)S(1)} %get-tuple-element.22), channel_id=1, source_target_pairs={{24,16},{28,20},{25,17},{29,21},{26,18},{30,22},{27,19},{31,23}} | collective-permute-start | bytes 1179656 | tf_op jit(solution)/shard_map/ppermute | solution.py:130
  75.2 12.2 %collective-permute-start.12 = (bf16[2,3,256,128]{3,2,1,0:T(8,128)(2,1)}, bf16[2,3,256,128]{3,2,1,0:T(8,128)(2,1)}, u32[]{:S(2)}, u32[]{:S(2)}) collective-permute-start(bf16[2,3,256,128]{3,2,1,0:T(8,128)(2,1)} %get-tuple-element.53), channel_id=1, source_target_pairs={{24,16},{28,20},{16,8},{20,12},{25,17},{29,21},{17,9},{21,13},{26,... | collective-permute-start | bytes 1179656 | tf_op jit(solution)/shard_map/ppermute | solution.py:130
  76.7 13.2 %collective-permute-start.9 = (bf16[2,3,256,128]{3,2,1,0:T(8,128)(2,1)}, bf16[2,3,256,128]{3,2,1,0:T(8,128)(2,1)S(1)}, u32[]{:S(2)}, u32[]{:S(2)}) collective-permute-start(bf16[2,3,256,128]{3,2,1,0:T(8,128)(2,1)} %get-tuple-element.52), channel_id=1, source_target_pairs={{0,8},{4,12},{8,16},{12,20},{1,9},{5,13},{9,17},{13,21},{2,10},{6,... | collective-permute-start | bytes 1179656 | tf_op jit(solution)/shard_map/ppermute | solution.py:129
  81.6 16.7 %collective-permute-start.21 = (bf16[2,3,256,128]{3,2,1,0:T(8,128)(2,1)S(1)}, bf16[2,3,256,128]{3,2,1,0:T(8,128)(2,1)S(1)}, u32[]{:S(2)}, u32[]{:S(2)}) collective-permute-start(bf16[2,3,256,128]{3,2,1,0:T(8,128)(2,1)S(1)} %get-tuple-element.49), channel_id=1, source_target_pairs={{24,16},{28,20},{16,8},{20,12},{25,17},{29,21},{17,9},{21,13},{26,... | collective-permute-start | bytes 1179656 | tf_op jit(solution)/shard_map/ppermute | solution.py:130
  82.3 18.2 %collective-permute-start.18 = (bf16[2,3,256,128]{3,2,1,0:T(8,128)(2,1)S(1)}, bf16[2,3,256,128]{3,2,1,0:T(8,128)(2,1)S(1)}, u32[]{:S(2)}, u32[]{:S(2)}) collective-permute-start(bf16[2,3,256,128]{3,2,1,0:T(8,128)(2,1)S(1)} %get-tuple-element.48), channel_id=1, source_target_pairs={{0,8},{4,12},{8,16},{12,20},{1,9},{5,13},{9,17},{13,21},{2,10},{6,... | collective-permute-start | bytes 1179656 | tf_op jit(solution)/shard_map/ppermute | solution.py:129
  88.6 19.6 %collective-permute-start.13 = (bf16[2,3,256,128]{3,2,1,0:T(8,128)(2,1)S(1)}, bf16[2,3,256,128]{3,2,1,0:T(8,128)(2,1)S(1)}, u32[]{:S(2)}, u32[]{:S(2)}) collective-permute-start(bf16[2,3,256,128]{3,2,1,0:T(8,128)(2,1)S(1)} %add_convert_fusion.4), channel_id=1, source_target_pairs={{24,16},{28,20},{16,8},{20,12},{8,0},{12,4},{25,17},{29,21},{17,9}... | collective-permute-start | bytes 1179656 | tf_op jit(solution)/shard_map/ppermute | solution.py:130
  90.7 17.5 %collective-permute-start.10 = (bf16[2,3,256,128]{3,2,1,0:T(8,128)(2,1)}, bf16[2,3,256,128]{3,2,1,0:T(8,128)(2,1)}, u32[]{:S(2)}, u32[]{:S(2)}) collective-permute-start(bf16[2,3,256,128]{3,2,1,0:T(8,128)(2,1)} %add_convert_fusion.5), channel_id=1, source_target_pairs={{0,8},{4,12},{8,16},{12,20},{16,24},{20,28},{1,9},{5,13},{9,17},{1... | collective-permute-start | bytes 1179656 | tf_op jit(solution)/shard_map/ppermute | solution.py:129
  99.2 10.4 %collective-permute-start.22 = (bf16[2,3,256,128]{3,2,1,0:T(8,128)(2,1)}, bf16[2,3,256,128]{3,2,1,0:T(8,128)(2,1)S(1)}, u32[]{:S(2)}, u32[]{:S(2)}) collective-permute-start(bf16[2,3,256,128]{3,2,1,0:T(8,128)(2,1)} %add_convert_fusion.1), channel_id=1, source_target_pairs={{24,16},{28,20},{16,8},{20,12},{8,0},{12,4},{25,17},{29,21},{17,9}... | collective-permute-start | bytes 1179656 | tf_op jit(solution)/shard_map/ppermute | solution.py:130
  101.4 10.6 %collective-permute-start.19 = (bf16[2,3,256,128]{3,2,1,0:T(8,128)(2,1)}, bf16[2,3,256,128]{3,2,1,0:T(8,128)(2,1)}, u32[]{:S(2)}, u32[]{:S(2)}) collective-permute-start(bf16[2,3,256,128]{3,2,1,0:T(8,128)(2,1)} %add_convert_fusion.2), channel_id=1, source_target_pairs={{0,8},{4,12},{8,16},{12,20},{16,24},{20,28},{1,9},{5,13},{9,17},{1... | collective-permute-start | bytes 1179656 | tf_op jit(solution)/shard_map/ppermute | solution.py:129
  109.4 4.0 %collective-permute-start.14 = (bf16[3,256,128]{2,1,0:T(8,128)(2,1)S(1)}, bf16[3,256,128]{2,1,0:T(8,128)(2,1)S(1)}, u32[]{:S(2)}, u32[]{:S(2)}) collective-permute-start(bf16[3,256,128]{2,1,0:T(8,128)(2,1)S(1)} %get-tuple-element.50), channel_id=1, source_target_pairs={{0,4},{4,0},{8,12},{12,8},{16,20},{20,16},{24,28},{28,24},{1,5},{5... | collective-permute-start | bytes 589832 | tf_op jit(solution)/shard_map/ppermute | solution.py:22
  113.2 1.5 %collective-permute-start.23 = (bf16[3,256,128]{2,1,0:T(8,128)(2,1)S(1)}, bf16[3,256,128]{2,1,0:T(8,128)(2,1)S(1)}, u32[]{:S(2)}, u32[]{:S(2)}) collective-permute-start(bf16[3,256,128]{2,1,0:T(8,128)(2,1)S(1)} %get-tuple-element.46), channel_id=1, source_target_pairs={{0,4},{4,0},{8,12},{12,8},{16,20},{20,16},{24,28},{28,24},{1,5},{5... | collective-permute-start | bytes 589832 | tf_op jit(solution)/shard_map/ppermute | solution.py:22
  117.6 9.2 %collective-permute-start.26 = (bf16[2,128,128]{2,1,0:T(8,128)(2,1)S(1)}, bf16[2,128,128]{2,1,0:T(8,128)(2,1)S(1)}, u32[]{:S(2)}, u32[]{:S(2)}) collective-permute-start(bf16[2,128,128]{2,1,0:T(8,128)(2,1)S(1)} %get-tuple-element.28), channel_id=1, source_target_pairs={{0,24},{4,28},{8,16},{12,20},{16,8},{20,12},{24,0},{28,4},{1,25},{... | collective-permute-start | bytes 196616 | tf_op jit(solution)/shard_map/ppermute | solution.py:27
  123.9 5.3 %collective-permute-start.25 = (bf16[2,128,128]{2,1,0:T(8,128)(2,1)S(1)}, bf16[2,128,128]{2,1,0:T(8,128)(2,1)S(1)}, u32[]{:S(2)}, u32[]{:S(2)}) collective-permute-start(bf16[2,128,128]{2,1,0:T(8,128)(2,1)S(1)} %get-tuple-element.27), channel_id=1, source_target_pairs={{0,16},{4,20},{8,24},{12,28},{16,0},{20,4},{24,8},{28,12},{1,17},{... | collective-permute-start | bytes 196616 | tf_op jit(solution)/shard_map/ppermute | solution.py:27
  123.9 5.7 %collective-permute-start.24 = (bf16[2,128,128]{2,1,0:T(8,128)(2,1)S(1)}, bf16[2,128,128]{2,1,0:T(8,128)(2,1)S(1)}, u32[]{:S(2)}, u32[]{:S(2)}) collective-permute-start(bf16[2,128,128]{2,1,0:T(8,128)(2,1)S(1)} %get-tuple-element.26), channel_id=1, source_target_pairs={{0,8},{4,12},{8,0},{12,4},{16,24},{20,28},{24,16},{28,20},{1,9},{5... | collective-permute-start | bytes 196616 | tf_op jit(solution)/shard_map/ppermute | solution.py:27
  129.6 1.4 %collective-permute-start.27 = (bf16[4,128,128]{2,1,0:T(8,128)(2,1)S(1)}, bf16[4,128,128]{2,1,0:T(8,128)(2,1)S(1)}, u32[]{:S(2)}, u32[]{:S(2)}) collective-permute-start(bf16[4,128,128]{2,1,0:T(8,128)(2,1)S(1)} %dynamic-slice_bitcast_fusion.4), channel_id=1, source_target_pairs={{0,4},{4,0},{8,12},{12,8},{16,20},{20,16},{24,28},{28,24},{1,5},{5... | collective-permute-start | bytes 393224 | tf_op jit(solution)/shard_map/ppermute | solution.py:22
  131.3 0.7 copy-start.2

commit v2 on v1

v2 whole, which is shorter than its diff:
```python
import jax
import jax.numpy as jnp
from jax import lax
from jax.experimental import pallas as pl
from jax.experimental.pallas import tpu as pltpu
from jax.sharding import PartitionSpec as P

GROUP = 16
CHUNK = 128
F32 = jnp.float32
BF16 = jnp.bfloat16


def pick(blocks, index):
    chosen = blocks[0]
    for i in range(1, len(blocks)):
        chosen = jnp.where(index == i, blocks[i], chosen)
    return chosen


def swap_cores(block, n_ctx):
    return lax.ppermute(block, "ctx", [(i, i ^ 1) for i in range(n_ctx)])


def to_plane(block, distance, planes):
    route = [(2 * z + c, 2 * (z ^ distance) + c) for z in range(planes) for c in range(2)]
    return lax.ppermute(block, "ctx", route)


def to_column(block, distance, n_ch):
    return lax.ppermute(block, "ch", [(j, j ^ distance) for j in range(n_ch)])


def trade_columns(tokens, me, n_ch):
    rows = tokens.shape[0] // n_ch
    pieces = tokens.reshape(n_ch, rows, tokens.shape[1])
    got = []
    for s in range(n_ch):
        piece = lax.dynamic_index_in_dim(pieces, me ^ s, 0, keepdims=False)
        got.append(to_column(piece, s, n_ch) if s else piece)
    return got


def trade_planes(got, z, me, planes):
    came = []
    for u in range(planes):
        piece = pick(got, me ^ z ^ u)
        came.append(to_plane(piece, u, planes) if u else piece)
    return came


def sending_order(planes):
    return [planes - 1, *range(1, planes - 1), 0]


def stage_kernel(planes, where_ref, w_own, w_sib, out_ref, sems):
    z, core = where_ref[0], where_ref[1]
    depth, half = w_own.shape[1], w_own.shape[2] // 2
    lanes = half // planes
    copies = []
    for side, w in enumerate((w_own, w_sib)):
        owner = core if side == 0 else 1 - core
        rows = pl.ds(pl.multiple_of(owner * depth, depth), depth)
        for i, r in enumerate(sending_order(planes)):
            columns = pl.ds(pl.multiple_of(core * half + (z + r) % planes * lanes, lanes), lanes)
            copy = pltpu.make_async_copy(
                w.at[:, :, columns], out_ref.at[:, rows, pl.ds(i * lanes, lanes)], sems.at[side, i]
            )
            copy.start()
            copies.append(copy)
    for copy in copies:
        copy.wait()


def stage(w_own, w_sib, z, core, planes):
    depth, half = w_own.shape[1], w_own.shape[2] // 2
    lanes = half // planes
    if lanes % 128:
        w = jnp.concatenate([pick([w_own, w_sib], core), pick([w_own, w_sib], 1 - core)], axis=1)
        w = lax.dynamic_slice_in_dim(w, core * half, half, 2).reshape(3, 2 * depth, planes, lanes)
        blocks = [lax.dynamic_index_in_dim(w, (z + r) % planes, 2, keepdims=False) for r in sending_order(planes)]
        return jnp.concatenate(blocks, axis=2)
    hbm = pl.BlockSpec(memory_space=pltpu.HBM)
    return pl.pallas_call(
        lambda *refs: stage_kernel(planes, *refs),
        in_specs=[pl.BlockSpec(memory_space=pltpu.SMEM), hbm, hbm],
        out_specs=pl.BlockSpec(memory_space=pltpu.VMEM),
        out_shape=jax.ShapeDtypeStruct((3, 2 * depth, half), BF16),
        scratch_shapes=[pltpu.SemaphoreType.DMA((2, planes))],
        compiler_params=pltpu.CompilerParams(vmem_limit_bytes=8 << 20),
        cost_estimate=pl.CostEstimate(flops=0, bytes_accessed=0, transcendentals=0),
        name="stage",
    )(jnp.stack([z, core]).astype(jnp.int32), w_own, w_sib)


def project_kernel(planes, pieces, *refs):
    x_refs, w_ref, outs, x_all = refs[:pieces], refs[pieces], refs[pieces + 1 : -1], refs[-1]
    lanes = w_ref.shape[2] // planes
    at = 0
    for ref in x_refs:
        x_all[at : at + ref.shape[0]] = ref[...]
        at += ref.shape[0]
    order = sending_order(planes)
    for i in range(0, planes, 2):

        @pl.loop(0, 3)
        def _(j):
            w = w_ref[j, :, i * lanes : (i + 2) * lanes]
            sums = jnp.dot(x_all[...], w, preferred_element_type=F32).astype(BF16)
            outs[order[i]][j] = sums[:, :lanes]
            outs[order[i + 1]][j] = sums[:, lanes:]


def project(xs, w, planes):
    rows = sum(x.shape[0] for x in xs)
    wide, half = w.shape[1:]
    lanes = half // planes
    if lanes % 128:
        x = jnp.concatenate(xs, axis=0)
        sums = jnp.einsum("tk,jkc->jtc", x, w, preferred_element_type=F32).astype(BF16)
        order = sending_order(planes)
        return [sums[:, :, order.index(r) * lanes : (order.index(r) + 1) * lanes] for r in range(planes)]
    vmem = pl.BlockSpec(memory_space=pltpu.VMEM)
    return pl.pallas_call(
        lambda *refs: project_kernel(planes, len(xs), *refs),
        in_specs=[vmem] * (len(xs) + 1),
        out_specs=[vmem] * planes,
        out_shape=[jax.ShapeDtypeStruct((3, rows, lanes), BF16)] * planes,
        scratch_shapes=[pltpu.VMEM((rows, wide), BF16)],
        compiler_params=pltpu.CompilerParams(vmem_limit_bytes=8 << 20),
        cost_estimate=pl.CostEstimate(flops=0, bytes_accessed=0, transcendentals=0),
        name="project",
    )(*xs, pltpu.with_memory_space_constraint(w, pltpu.VMEM))


def add(*blocks):
    total = blocks[0].astype(F32)
    for block in blocks[1:]:
        total = total + block.astype(F32)
    return total.astype(BF16)


class LineSum:
    def __init__(self, blocks):
        self.blocks, self.last = blocks, len(blocks) - 1
        self.step, self.came = 0, None

    def send(self):
        t, last = self.step, self.last
        up, down = self.blocks[last - t], self.blocks[t + 1]
        if t:
            up, down = add(up, self.came[0]), add(down, self.came[1])
        planes = range(min(t + 1, last))
        up_route = [(2 * z + c, 2 * z + 2 + c) for z in planes for c in range(2)]
        down_route = [(2 * (last - z) + c, 2 * (last - z) - 2 + c) for z in planes for c in range(2)]
        self.came = [lax.ppermute(up, "ctx", up_route), lax.ppermute(down, "ctx", down_route)]
        self.step += 1

    def after(self, value):
        *self.came, _ = lax.optimization_barrier((*self.came, value))

    def total(self):
        return add(self.blocks[0], *self.came)


def long_filters(decay, weight):
    lag = jnp.arange(CHUNK)
    apart = lag[:, None] - lag[None, :]
    away = jnp.maximum(apart, 0).astype(F32)
    near = jnp.sum(
        weight[:, :, None, None] * jnp.exp(-decay[:, :, None, None] * away[None, None]), axis=1
    )
    near = jnp.where(apart[None] >= 0, near, 0.0)
    poles = decay.reshape(-1)
    position = lag.astype(F32)
    collect = jnp.exp(-poles[:, None] * (CHUNK - 1 - position)[None, :])
    emit = weight.reshape(-1)[None, :] * jnp.exp(-poles[None, :] * (position + 1.0)[:, None])
    return near, collect, emit


def halves_of(value):
    high = value.astype(BF16)
    return high, (value - high.astype(F32)).astype(BF16)


def mix_kernel(order, parts, planes, n_ch, where_ref, *refs):
    data, (taps, skip, near, collect, emit), refs = refs[:parts], refs[parts : parts + 5], refs[parts + 5 :]
    outs, (proj, long_in, done) = refs[:planes], refs[planes:]
    core, me, z = where_ref[0], where_ref[1], where_ref[2]
    lanes = skip.shape[1]
    groups = near.shape[0]
    proj[:, 0:8] = jnp.zeros((3, 8, lanes), F32)
    rows = CHUNK // n_ch
    for pieces, ref in zip(order, data, strict=True):
        start = 0
        for side, s, first in pieces:
            owner = core if side == 0 else 1 - core
            for k in range(first, first + planes // 2):
                at = (2 * k + owner) * CHUNK + (me ^ s) * rows + 8
                for j in range(3):
                    proj[j, pl.ds(pl.multiple_of(at, 8), rows)] = ref[j, start : start + rows].astype(F32)
                start += rows

    lane_group = lax.broadcasted_iota(jnp.int32, (1, lanes), 1) // GROUP
    pole_group = lax.broadcasted_iota(jnp.int32, (collect.shape[0], lanes), 0) // (collect.shape[0] // groups)
    same = pole_group == lane_group
    keep = collect[:, 0:1] * collect[:, CHUNK - 2 : CHUNK - 1]
    collect2 = jnp.concatenate(halves_of(collect[...]), axis=1)
    emit_high, emit_low = halves_of(emit[...])
    emit3 = jnp.concatenate([emit_high, emit_low, emit_high], axis=1)
    state = jnp.zeros(same.shape, F32)
    chunks = 2 * planes
    for n in range(chunks):
        mixed = []
        for j in range(3):
            total = 0.0
            for lag in range(3):
                total += taps[lag, j : j + 1] * proj[j, 8 - lag + n * CHUNK : 8 - lag + (n + 1) * CHUNK]
            mixed.append(total)
        gated = (mixed[1] * mixed[2]).astype(BF16)
        gated2 = jnp.concatenate([gated, gated], axis=0)
        long_out = skip[...] * gated.astype(F32)
        if n:
            state_high, state_low = halves_of(state)
            long_out += jnp.dot(
                emit3, jnp.concatenate([state_high, state_high, state_low], axis=0), preferred_element_type=F32
            )
        if n < chunks - 1:
            fresh = jnp.dot(collect2, gated2, preferred_element_type=F32)
            state = keep * state + jnp.where(same, fresh, 0.0)
        long_in[n // 2, n % 2] = gated2
        done[n * CHUNK : (n + 1) * CHUNK] = long_out
        proj[0, 8 + n * CHUNK - 8 : n * CHUNK + CHUNK] = mixed[0]
    for g in range(groups):
        near2 = jnp.concatenate(halves_of(near[g]), axis=1)
        mine = lane_group == g
        for k in range(planes):
            pair = jnp.concatenate([long_in[k, 0], long_in[k, 1]], axis=1)
            both = jnp.dot(near2, pair, preferred_element_type=F32)
            for c in range(2):
                at = slice((2 * k + c) * CHUNK, (2 * k + c + 1) * CHUNK)
                done[at] += jnp.where(mine, both[:, c * lanes : (c + 1) * lanes], 0.0)
    for u in range(planes):
        at = pl.multiple_of((z ^ u) * 2 * CHUNK, CHUNK)
        both = proj[0, pl.ds(at, 2 * CHUNK)] * done[pl.ds(at, 2 * CHUNK)]
        outs[u][...] = both.astype(BF16).reshape(2, CHUNK, lanes)


def mix(data, order, taps, skip, filters, core, me, z, planes, n_ch):
    lanes = skip.shape[1]
    if lanes % 128:
        return mix_plainly(data, order, taps, skip, filters, core, me, z, planes, n_ch)
    poles = filters[1].shape[0]
    length = 2 * planes * CHUNK
    vmem = pl.BlockSpec(memory_space=pltpu.VMEM)
    return pl.pallas_call(
        lambda *refs: mix_kernel(order, len(data), planes, n_ch, *refs),
        in_specs=[pl.BlockSpec(memory_space=pltpu.SMEM)] + [vmem] * (len(data) + 5),
        out_specs=[vmem] * planes,
        out_shape=[jax.ShapeDtypeStruct((2, CHUNK, lanes), BF16)] * planes,
        scratch_shapes=[
            pltpu.VMEM((3, length + 8, lanes), F32),
            pltpu.VMEM((planes, 2, 2 * CHUNK, lanes), BF16),
            pltpu.VMEM((length, lanes), F32),
        ],
        compiler_params=pltpu.CompilerParams(vmem_limit_bytes=8 << 20),
        cost_estimate=pl.CostEstimate(flops=0, bytes_accessed=0, transcendentals=0),
        name="mix",
    )(
        jnp.stack([core, me, z]).astype(jnp.int32), *data, taps, skip, *filters
    )


def mix_plainly(data, order, taps, skip, filters, core, me, z, planes, n_ch):
    lanes = skip.shape[1]
    near, collect, emit = filters
    keep = collect[:, 0] * collect[:, CHUNK - 2]
    groups, rows = near.shape[0], CHUNK // n_ch
    sides = [[[None, None] for _ in range(n_ch)] for _ in range(2)]
    for pieces, block in zip(order, data, strict=True):
        cut = block.reshape(3, len(pieces), planes // 2, rows, lanes)
        for i, (side, s, first) in enumerate(pieces):
            sides[side][s][first > 0] = cut[:, i]
    sides = [[jnp.concatenate(halves, axis=1) for halves in side] for side in sides]
    sides = [jnp.stack([pick(side, me ^ p) for p in range(n_ch)], axis=2) for side in sides]
    both = jnp.stack([pick(sides, core), pick(sides, 1 - core)], axis=2)
    proj = both.reshape(3, -1, lanes).astype(F32)
    length = proj.shape[1]
    padded = jnp.pad(proj, ((0, 0), (2, 0), (0, 0)))
    mixed = sum(taps[lag][:, None] * padded[:, 2 - lag : 2 - lag + length] for lag in range(3))
    gated = lax.optimization_barrier((mixed[1] * mixed[2]).astype(BF16)).astype(F32)
    chunks = length // CHUNK
    columns = gated.reshape(chunks, CHUNK, groups, GROUP)
    high = lax.Precision.HIGHEST
    out = jnp.einsum("gij,njgc->nigc", near, columns, precision=high)
    fresh = jnp.einsum("grj,njgc->ngrc", collect.reshape(groups, -1, CHUNK), columns, precision=high)
    state, states = jnp.zeros_like(fresh[0]), []
    for n in range(chunks):
        states.append(state)
        state = keep.reshape(groups, -1, 1) * state + fresh[n]
    out += jnp.einsum("igr,ngrc->nigc", emit.reshape(CHUNK, groups, -1), jnp.stack(states), precision=high)
    out = (mixed[0] * (out.reshape(length, lanes) + skip * gated)).astype(BF16)
    out = out.reshape(planes, 2, CHUNK, lanes)
    return [lax.dynamic_index_in_dim(out, z ^ u, 0, keepdims=False) for u in range(planes)]


def local(tokens, w_in, short_filter, decay_rate, residue, skip):
    n_ctx, n_ch = lax.axis_size("ctx"), lax.axis_size("ch")
    planes = n_ctx // 2
    ctx, me = lax.axis_index("ctx"), lax.axis_index("ch")
    z, core = ctx // 2, ctx % 2
    half = w_in.shape[2] // 2
    lanes = half // planes
    groups = lanes // GROUP

    block = core * planes + z
    mine = lambda a, count, axis: lax.dynamic_slice_in_dim(a, block * count, count, axis)
    decay = mine(decay_rate, groups, 0)
    filters = long_filters(decay, mine(residue, groups, 0) * jnp.sqrt(2.0 * decay))

    w_own = w_in.transpose(1, 0, 2)
    w_sib = swap_cores(w_own, n_ctx)
    got = trade_columns(tokens, me, n_ch)
    came = trade_planes(got, z, me, planes)
    w_own, w_sib, _ = lax.optimization_barrier((w_own, w_sib, got[-1]))
    w = stage(w_own, w_sib, z, core, planes)
    taps, direct = mine(short_filter, lanes, 2), mine(skip, lanes, 0)[None]
    came, filters, w, taps, direct = lax.optimization_barrier((came, filters, w, taps, direct))
    by_plane = [pick(came, z ^ k) for k in range(planes)]
    middle = planes // 2
    x = [jnp.concatenate(by_plane[:middle], axis=0), jnp.concatenate(by_plane[middle:], axis=0)]

    order = []

    def project_pieces(pieces):
        xs = [y for piece, _, _ in pieces for y in (piece, swap_cores(piece, n_ctx))]
        order.append([(side, s, h * middle) for _, s, h in pieces for side in range(2)])
        return LineSum(project(xs, w, planes))

    near = [to_column(x[0], 1, n_ch), to_column(x[1], 2, n_ch), to_column(x[1], 1, n_ch), to_column(x[0], 2, n_ch)]
    a = project_pieces([(x[0], 0, 0), (x[1], 0, 1), (near[0], 1, 0), (near[1], 2, 1)])
    far = [to_column(near[0], 2, n_ch), to_column(near[1], 1, n_ch)]
    rest = [(near[2], 1, 1), (near[3], 2, 0), (far[0], 3, 0), (far[1], 3, 1)]
    rest += [(to_column(x[h], s, n_ch), s, h) for s in range(4, n_ch) for h in range(2)]
    b = project_pieces(rest)
    streams = [a, b]
    for step in range(planes - 1):
        for stream in streams:
            stream.send()
    data = [stream.total() for stream in streams]
    outs = mix(
        data,
        order,
        taps,
        direct,
        filters,
        core,
        me,
        z,
        planes,
        n_ch,
    )
    came = [to_plane(block, u, planes) if u else block for u, block in enumerate(outs)]
    came = jnp.stack(came)
    keep = lax.dynamic_index_in_dim(came, core, 1, keepdims=False)
    given = swap_cores(lax.dynamic_index_in_dim(came, 1 - core, 1, keepdims=False), n_ctx)
    sides = [jnp.where(core == 0, keep, given), jnp.where(core == 0, given, keep)]
    columns = [pick([sides[c][u] for u in range(planes)], z ^ k) for c in range(2) for k in range(planes)]
    return jnp.concatenate(columns, axis=1)


def solution(mesh):
    return jax.shard_map(
        local,
        mesh=mesh,
        in_specs=(
            P("ctx", "ch"),
            P("ctx", None, "ch"),
            P(None, None, "ch"),
            P("ch", None),
            P("ch", None),
            P("ch"),
        ),
        out_specs=P("ctx", "ch"),
        check_vma=False,
    )
```

time: 134 us -> 124 us (0.925)
  Pallas kernels: 26.1 us -> 15.3 us
  other arithmetic: 14.1 us -> 5.61 us
  waiting for transfers between devices: 37.5 us -> 44.7 us
  local copies, waits for them, and re-layouts: 3.82 us -> 6.41 us
    ppermute x12, waiting for transfers between devices: 4.84 us -> 22 us  [the longest x6 22 us: send(): lax.ppermute(up, 'ctx', up_route)]
    pallas_call x2 -> x3, Pallas kernels: 23.3 us -> 12.5 us  [the longest x2 9.08 us: project(): pl.pallas_call(lambda *refs: project_kernel(planes, len(xs), *refs), in_s...]
    ppermute x6, waiting for transfers between devices: 15.3 us -> 7.87 us  [to_plane(): return lax.ppermute(block, 'ctx', route)]
    convert_element_type x8, other arithmetic: 8.37 us -> 1.1 us  [add(): return total.astype(BF16)]
    ppermute x6 -> x9, waiting for transfers between devices: 14.7 us -> 11.8 us  [to_column(): return lax.ppermute(block, 'ch', [(j, j ^ distance) for j in range(n_ch)])]
    unnamed x8, local copies, waits for them, and re-layouts: 0.84 us -> 3.62 us
    ppermute x6 -> x9, starting transfers between devices: 7.8 us -> 10.1 us  [to_column(): return lax.ppermute(block, 'ch', [(j, j ^ distance) for j in range(n_ch)])]
    ppermute x12, starting transfers between devices: 30.8 us -> 28.6 us  [the longest x6 23.2 us: send(): lax.ppermute(up, 'ctx', up_route)]
  transfers between devices with their start and end apart: 28 -> 37, of which waited for: 14 -> 16; matrix products, arithmetic and copies ran while one was open for 12% -> 6% of each run, Pallas kernels for 18% -> 10%
where the time goes in v2:
time: 124 us; the launch traced here: 123 us
  starting transfers between devices  50.6 us (41%)
  waiting for transfers between devices  44.7 us (36%)
  Pallas kernels  15.3 us (12%)
  local copies, waits for them, and re-layouts  6.41 us (5%)
  other arithmetic  5.61 us (5%)
    ppermute x6, starting transfers between devices, send(): lax.ppermute(up, 'ctx', up_route)  23.2 us
    ppermute x6, waiting for transfers between devices, send(): lax.ppermute(up, 'ctx', up_route)  22 us
    ppermute x9, waiting for transfers between devices, to_column(): return lax.ppermute(block, 'ch', [(j, j ^ distance) for j in range(n_ch)])  11.8 us
    ppermute x6, starting transfers between devices, to_plane(): return lax.ppermute(block, 'ctx', route)  10.2 us
    ppermute x9, starting transfers between devices, to_column(): return lax.ppermute(block, 'ch', [(j, j ^ distance) for j in range(n_ch)])  10.1 us
    pallas_call x2, Pallas kernels, project(): pl.pallas_call(lambda *refs: project_kernel(planes, len(xs), *refs), in_s...  9.08 us
    ppermute x6, waiting for transfers between devices, to_plane(): return lax.ppermute(block, 'ctx', route)  7.87 us
    ppermute x6, starting transfers between devices, send(): lax.ppermute(down, 'ctx', down_route)  5.33 us
  transfers between devices with their start and end apart: 37, of which 16 were waited for; matrix products, arithmetic and copies ran while one was open for 6% of the time, Pallas kernels for 10%

profile of v2, /device:TPU:0, one launch (start us, length us, event | category | flops | bytes accessed | tf_op | source)
XLA Modules:
  0.0 123.1 jit_solution(8468044894650545479)
XLA Ops:
  0.0 0.5 collective-permute-start.6
  0.5 1.1 dynamic-slice_bitcast_fusion.1
  1.5 3.5 %collective-permute-start = (bf16[32,2048]{1,0:T(8,128)(2,1)S(1)}, bf16[32,2048]{1,0:T(8,128)(2,1)S(1)}, u32[]{:S(2)}, u32[]{:S(2)}) collective-permute-start(bf16[32,2048]{1,0:T(8,128)(2,1)S(1)} %get-tuple-element.63), channel_id=1, source_target_pairs={{0,3},{1,2},{2,1},{3,0},{4,7},{5,6},{6,5},{7,4},{8,11},{9,10},{10,... | collective-permute-start | bytes 393224 | tf_op jit(solution)/shard_map/ppermute | solution.py:31
  5.1 0.5 collective-permute-start.1
  5.6 0.1 collective-permute-start.2
  5.7 0.8 constant_dynamic-slice_fusion.1
  6.9 2.2 %multiply_reduce_fusion = f32[8,128,128]{2,1,0:T(8,128)S(1)} fusion(f32[128,128]{1,0:T(8,128)S(1)} %maximum_convert_fusion, f32[8,16]{1,0:T(8,128)S(1)} %get-tuple-element.71, f32[8,16]{1,0:T(8,128)S(1)} %get-tuple-element.70), kind=kLoop, calls=%fused_computation | loop fusion | flops 6160384 | bytes 590848 | tf_op jit(solution)/shard_map/reduce_sum | solution.py:170
  9.1 0.1 exponential_multiply_fusion
  9.3 2.7 %collective-permute-done.1 = bf16[32,2048]{1,0:T(8,128)(2,1)S(1)} collective-permute-done((bf16[32,2048]{1,0:T(8,128)(2,1)S(1)}, bf16[32,2048]{1,0:T(8,128)(2,1)S(1)}, u32[]{:S(2)}, u32[]{:S(2)}) %collective-permute-start.1) | collective-permute-done | bytes 131104 | tf_op jit(solution)/shard_map/ppermute | solution.py:31
  12.0 0.3 collective-permute-done.2
  12.3 1.0 fusion.11
  13.3 1.6 %collective-permute-start.3 = (bf16[32,2048]{1,0:T(8,128)(2,1)S(1)}, bf16[32,2048]{1,0:T(8,128)(2,1)S(1)}, u32[]{:S(2)}, u32[]{:S(2)}) collective-permute-start(bf16[32,2048]{1,0:T(8,128)(2,1)S(1)} %get-tuple-element.55), channel_id=1, source_target_pairs={{0,8},{4,12},{8,0},{12,4},{16,24},{20,28},{24,16},{28,20},{1,9},{5... | collective-permute-start | bytes 393224 | tf_op jit(solution)/shard_map/ppermute | solution.py:27
  14.9 2.6 %collective-permute-start.4 = (bf16[32,2048]{1,0:T(8,128)(2,1)S(1)}, bf16[32,2048]{1,0:T(8,128)(2,1)S(1)}, u32[]{:S(2)}, u32[]{:S(2)}) collective-permute-start(bf16[32,2048]{1,0:T(8,128)(2,1)S(1)} %get-tuple-element.54), channel_id=1, source_target_pairs={{0,16},{4,20},{8,24},{12,28},{16,0},{20,4},{24,8},{28,12},{1,17},{... | collective-permute-start | bytes 393224 | tf_op jit(solution)/shard_map/ppermute | solution.py:27
  17.5 0.2 collective-permute-start.5
  17.7 0.8 dynamic-slice_bitcast_fusion.4.refs_4_
  18.5 2.8 %copy-done.1 = bf16[1024,3,1024]{2,0,1:T(8,128)(2,1)S(1)} copy-done((bf16[1024,3,1024]{2,0,1:T(8,128)(2,1)S(1)}, bf16[1024,3,1024]{2,0,1:T(8,128)(2,1)}, u32[]{:S(2)}) %copy-start.1) | copy-done | bytes 6291480
  21.3 3.4 %stage.1.refs_8_ = bf16[3,2048,512]{2,1,0:T(8,128)(2,1)S(1)} custom-call(s32[2]{0:T(128)S(1)} %pad_add_fusion.1.refs_0_, bf16[3,1024,1024]{2,1,0:T(8,128)(2,1)S(1)} %bitcast.60, bf16[3,1024,1024]{2,1,0:T(8,128)(2,1)} %collective-permute-done.6.refs_2_), custom_call_target="tpu_custom_call" | custom-call | tf_op jit(solution)/shard_map/stage/pallas_call | solution.py:84
  24.7 3.1 %collective-permute-done.4 = bf16[32,2048]{1,0:T(8,128)(2,1)S(1)} collective-permute-done((bf16[32,2048]{1,0:T(8,128)(2,1)S(1)}, bf16[32,2048]{1,0:T(8,128)(2,1)S(1)}, u32[]{:S(2)}, u32[]{:S(2)}) %collective-permute-start.4) | collective-permute-done | bytes 131104 | tf_op jit(solution)/shard_map/ppermute | solution.py:27
  27.9 1.5 %collective-permute-start.11 = (bf16[64,2048]{1,0:T(8,128)(2,1)S(1)}, bf16[64,2048]{1,0:T(8,128)(2,1)S(1)}, u32[]{:S(2)}, u32[]{:S(2)}) collective-permute-start(bf16[64,2048]{1,0:T(8,128)(2,1)S(1)} %pad_maximum_fusion.1.refs_2_), channel_id=1, source_target_pairs={{0,2},{1,3},{2,0},{3,1},{4,6},{5,7},{6,4},{7,5},{8,10},{9,11},{10,... | collective-permute-start | bytes 786440 | tf_op jit(solution)/shard_map/ppermute | solution.py:31
  29.4 0.5 collective-permute-start.9
  30.0 1.6 %collective-permute-start.19 = (bf16[64,2048]{1,0:T(8,128)(2,1)S(1)}, bf16[64,2048]{1,0:T(8,128)(2,1)S(1)}, u32[]{:S(2)}, u32[]{:S(2)}) collective-permute-start(bf16[64,2048]{1,0:T(8,128)(2,1)S(1)} %pad_maximum_fusion.1.refs_2_), channel_id=1, source_target_pairs={{0,1},{1,0},{2,3},{3,2},{4,5},{5,4},{6,7},{7,6},{8,9},{9,8},{10,11... | collective-permute-start | bytes 786440 | tf_op jit(solution)/shard_map/ppermute | solution.py:31
  31.5 0.5 collective-permute-start.7
  32.1 2.3 %collective-permute-done.11.refs_6_ = bf16[64,2048]{1,0:T(8,128)(2,1)S(1)} collective-permute-done((bf16[64,2048]{1,0:T(8,128)(2,1)S(1)}, bf16[64,2048]{1,0:T(8,128)(2,1)S(1)}, u32[]{:S(2)}, u32[]{:S(2)}) %collective-permute-start.11) | collective-permute-done | bytes 262176 | tf_op jit(solution)/shard_map/ppermute | solution.py:31
  34.4 3.7 %collective-permute-done.9.refs_4_ = bf16[64,2048]{1,0:T(8,128)(2,1)S(1)} collective-permute-done((bf16[64,2048]{1,0:T(8,128)(2,1)S(1)}, bf16[64,2048]{1,0:T(8,128)(2,1)S(1)}, u32[]{:S(2)}, u32[]{:S(2)}) %collective-permute-start.9) | collective-permute-done | bytes 262176 | tf_op jit(solution)/shard_map/ppermute | solution.py:31
  38.1 2.8 %collective-permute-done.19.refs_0_ = bf16[64,2048]{1,0:T(8,128)(2,1)S(1)} collective-permute-done((bf16[64,2048]{1,0:T(8,128)(2,1)S(1)}, bf16[64,2048]{1,0:T(8,128)(2,1)S(1)}, u32[]{:S(2)}, u32[]{:S(2)}) %collective-permute-start.19) | collective-permute-done | bytes 262176 | tf_op jit(solution)/shard_map/ppermute | solution.py:31
  40.9 0.4 collective-permute-start.21
  41.3 1.5 %collective-permute-start.25 = (bf16[64,2048]{1,0:T(8,128)(2,1)S(1)}, bf16[64,2048]{1,0:T(8,128)(2,1)S(1)}, u32[]{:S(2)}, u32[]{:S(2)}) collective-permute-start(bf16[64,2048]{1,0:T(8,128)(2,1)S(1)} %collective-permute-done.11.refs_6_), channel_id=1, source_target_pairs={{0,1},{1,0},{2,3},{3,2},{4,5},{5,4},{6,7},{7,6},{8,9},{9,8},{10,11... | collective-permute-start | bytes 786440 | tf_op jit(solution)/shard_map/ppermute | solution.py:31
  42.8 0.5 collective-permute-start.23
  43.3 4.5 %project.2 = (bf16[3,512,128]{2,1,0:T(8,128)(2,1)S(1)}, bf16[3,512,128]{2,1,0:T(8,128)(2,1)S(1)}, bf16[3,512,128]{2,1,0:T(8,128)(2,1)S(1)}, bf16[3,512,128]{2,1,0:T(8,128)(2,1)S(1)}) custom-call(bf16[64,2048]{1,0:T(8,128)(2,1)S(1)} %pad_maximum_fusion.refs_0_, bf16[64,2048]{1,0:T(8,128)(2,1)S(1)} %collective-permute-done.7.refs_1_, ...), custom_call_target="tpu_custom_call" | custom-call | tf_op jit(solution)/shard_map/project/pallas_call | solution.py:124
  47.8 5.2 %collective-permute-start.13 = (bf16[3,512,128]{2,1,0:T(8,128)(2,1)S(1)}, bf16[3,512,128]{2,1,0:T(8,128)(2,1)S(1)}, u32[]{:S(2)}, u32[]{:S(2)}) collective-permute-start(bf16[3,512,128]{2,1,0:T(8,128)(2,1)S(1)} %get-tuple-element.39), channel_id=1, source_target_pairs={{0,8},{4,12},{1,9},{5,13},{2,10},{6,14},{3,11},{7,15}} | collective-permute-start | bytes 1179656 | tf_op jit(solution)/shard_map/ppermute | solution.py:156
  53.1 0.7 collective-permute-start.16
  53.8 0.5 collective-permute-start.26
  54.4 0.9 collective-permute-done.22.refs_3_
  55.4 0.4 collective-permute-done.26.refs_7_
  55.7 0.4 collective-permute-done.24.refs_5_
  56.1 4.5 %project.3 = (bf16[3,512,128]{2,1,0:T(8,128)(2,1)S(1)}, bf16[3,512,128]{2,1,0:T(8,128)(2,1)S(1)}, bf16[3,512,128]{2,1,0:T(8,128)(2,1)S(1)}, bf16[3,512,128]{2,1,0:T(8,128)(2,1)S(1)}) custom-call(bf16[64,2048]{1,0:T(8,128)(2,1)S(1)} %collective-permute-done.19.refs_0_, bf16[64,2048]{1,0:T(8,128)(2,1)S(1)} %collective-permute-done.20.refs_1_, ...), custom_call_target="tpu_custom_call" | custom-call | tf_op jit(solution)/shard_map/project/pallas_call | solution.py:124
  60.7 3.5 %collective-permute-start.27 = (bf16[3,512,128]{2,1,0:T(8,128)(2,1)S(1)}, bf16[3,512,128]{2,1,0:T(8,128)(2,1)S(1)}, u32[]{:S(2)}, u32[]{:S(2)}) collective-permute-start(bf16[3,512,128]{2,1,0:T(8,128)(2,1)S(1)} %get-tuple-element.43), channel_id=1, source_target_pairs={{0,8},{4,12},{1,9},{5,13},{2,10},{6,14},{3,11},{7,15}} | collective-permute-start | bytes 1179656 | tf_op jit(solution)/shard_map/ppermute | solution.py:156
  64.2 0.7 collective-permute-start.30
  64.9 0.2 fusion
  65.1 1.3 %collective-permute-start.14 = (bf16[3,512,128]{2,1,0:T(8,128)(2,1)S(1)}, bf16[3,512,128]{2,1,0:T(8,128)(2,1)S(1)}, u32[]{:S(2)}, u32[]{:S(2)}) collective-permute-start(bf16[3,512,128]{2,1,0:T(8,128)(2,1)S(1)} %get-tuple-element.68), channel_id=1, source_target_pairs={{0,8},{4,12},{8,16},{12,20},{1,9},{5,13},{9,17},{13,21},{2,10},{6,... | collective-permute-start | bytes 1179656 | tf_op jit(solution)/shard_map/ppermute | solution.py:156
  66.4 0.7 collective-permute-start.17
  67.1 6.5 %collective-permute-done.27 = bf16[3,512,128]{2,1,0:T(8,128)(2,1)S(1)} collective-permute-done((bf16[3,512,128]{2,1,0:T(8,128)(2,1)S(1)}, bf16[3,512,128]{2,1,0:T(8,128)(2,1)S(1)}, u32[]{:S(2)}, u32[]{:S(2)}) %collective-permute-start.27) | collective-permute-done | bytes 393248 | tf_op jit(solution)/shard_map/ppermute | solution.py:156
  73.6 0.2 fusion.2
  73.8 4.4 %collective-permute-start.28 = (bf16[3,512,128]{2,1,0:T(8,128)(2,1)S(1)}, bf16[3,512,128]{2,1,0:T(8,128)(2,1)S(1)}, u32[]{:S(2)}, u32[]{:S(2)}) collective-permute-start(bf16[3,512,128]{2,1,0:T(8,128)(2,1)S(1)} %get-tuple-element.66), channel_id=1, source_target_pairs={{0,8},{4,12},{8,16},{12,20},{1,9},{5,13},{9,17},{13,21},{2,10},{6,... | collective-permute-start | bytes 1179656 | tf_op jit(solution)/shard_map/ppermute | solution.py:156
  78.2 0.7 collective-permute-start.31
  78.9 3.1 %collective-permute-done.14 = bf16[3,512,128]{2,1,0:T(8,128)(2,1)S(1)} collective-permute-done((bf16[3,512,128]{2,1,0:T(8,128)(2,1)S(1)}, bf16[3,512,128]{2,1,0:T(8,128)(2,1)S(1)}, u32[]{:S(2)}, u32[]{:S(2)}) %collective-permute-start.14) | collective-permute-done | bytes 393248 | tf_op jit(solution)/shard_map/ppermute | solution.py:156
  82.1 4.4 %collective-permute-start.15 = (bf16[3,512,128]{2,1,0:T(8,128)(2,1)S(1)}, bf16[3,512,128]{2,1,0:T(8,128)(2,1)S(1)}, u32[]{:S(2)}, u32[]{:S(2)}) collective-permute-start(bf16[3,512,128]{2,1,0:T(8,128)(2,1)S(1)} %add_convert_fusion.5), channel_id=1, source_target_pairs={{0,8},{4,12},{8,16},{12,20},{16,24},{20,28},{1,9},{5,13},{9,17},{1... | collective-permute-start | bytes 1179656 | tf_op jit(solution)/shard_map/ppermute | solution.py:156
  86.7 1.3 %collective-permute-start.18 = (bf16[3,512,128]{2,1,0:T(8,128)(2,1)S(1)}, bf16[3,512,128]{2,1,0:T(8,128)(2,1)S(1)}, u32[]{:S(2)}, u32[]{:S(2)}) collective-permute-start(bf16[3,512,128]{2,1,0:T(8,128)(2,1)S(1)} %add_convert_fusion.4), channel_id=1, source_target_pairs={{24,16},{28,20},{16,8},{20,12},{8,0},{12,4},{25,17},{29,21},{17,9}... | collective-permute-start | bytes 1179656 | tf_op jit(solution)/shard_map/ppermute | solution.py:156
  88.0 2.5 %collective-permute-done.28 = bf16[3,512,128]{2,1,0:T(8,128)(2,1)S(1)} collective-permute-done((bf16[3,512,128]{2,1,0:T(8,128)(2,1)S(1)}, bf16[3,512,128]{2,1,0:T(8,128)(2,1)S(1)}, u32[]{:S(2)}, u32[]{:S(2)}) %collective-permute-start.28) | collective-permute-done | bytes 393248 | tf_op jit(solution)/shard_map/ppermute | solution.py:156
  90.6 4.4 %collective-permute-start.29 = (bf16[3,512,128]{2,1,0:T(8,128)(2,1)S(1)}, bf16[3,512,128]{2,1,0:T(8,128)(2,1)S(1)}, u32[]{:S(2)}, u32[]{:S(2)}) collective-permute-start(bf16[3,512,128]{2,1,0:T(8,128)(2,1)S(1)} %add_convert_fusion.2), channel_id=1, source_target_pairs={{0,8},{4,12},{8,16},{12,20},{16,24},{20,28},{1,9},{5,13},{9,17},{1... | collective-permute-start | bytes 1179656 | tf_op jit(solution)/shard_map/ppermute | solution.py:156
  95.0 0.1 add_convert_fusion.1
  95.1 1.3 %collective-permute-start.32 = (bf16[3,512,128]{2,1,0:T(8,128)(2,1)S(1)}, bf16[3,512,128]{2,1,0:T(8,128)(2,1)S(1)}, u32[]{:S(2)}, u32[]{:S(2)}) collective-permute-start(bf16[3,512,128]{2,1,0:T(8,128)(2,1)S(1)} %add_convert_fusion.1), channel_id=1, source_target_pairs={{24,16},{28,20},{16,8},{20,12},{8,0},{12,4},{25,17},{29,21},{17,9}... | collective-permute-start | bytes 1179656 | tf_op jit(solution)/shard_map/ppermute | solution.py:156
  96.5 2.4 %collective-permute-done.15 = bf16[3,512,128]{2,1,0:T(8,128)(2,1)S(1)} collective-permute-done((bf16[3,512,128]{2,1,0:T(8,128)(2,1)S(1)}, bf16[3,512,128]{2,1,0:T(8,128)(2,1)S(1)}, u32[]{:S(2)}, u32[]{:S(2)}) %collective-permute-start.15) | collective-permute-done | bytes 393248 | tf_op jit(solution)/shard_map/ppermute | solution.py:156
  98.9 0.2 add_convert_fusion.3.refs_1_
  99.0 7.5 %collective-permute-done.29 = bf16[3,512,128]{2,1,0:T(8,128)(2,1)S(1)} collective-permute-done((bf16[3,512,128]{2,1,0:T(8,128)(2,1)S(1)}, bf16[3,512,128]{2,1,0:T(8,128)(2,1)S(1)}, u32[]{:S(2)}, u32[]{:S(2)}) %collective-permute-start.29) | collective-permute-done | bytes 393248 | tf_op jit(solution)/shard_map/ppermute | solution.py:156
  106.5 0.2 add_convert_fusion.refs_2_
  106.7 2.8 %mix.1 = (bf16[2,128,128]{2,1,0:T(8,128)(2,1)S(1)}, bf16[2,128,128]{2,1,0:T(8,128)(2,1)S(1)}, bf16[2,128,128]{2,1,0:T(8,128)(2,1)S(1)}, bf16[2,128,128]{2,1,0:T(8,128)(2,1)S(1)}) custom-call(s32[3]{0:T(128)S(1)} %pad_add_fusion.refs_0_, bf16[3,512,128]{2,1,0:T(8,128)(2,1)S(1)} %add_convert_fusion.3.refs_1_, ...), custom_call_target="tpu_custom_call" | custom-call | tf_op jit(solution)/shard_map/mix/pallas_call | solution.py:256
  109.5 2.5 %collective-permute-start.33 = (bf16[2,128,128]{2,1,0:T(8,128)(2,1)S(1)}, bf16[2,128,128]{2,1,0:T(8,128)(2,1)S(1)}, u32[]{:S(2)}, u32[]{:S(2)}) collective-permute-start(bf16[2,128,128]{2,1,0:T(8,128)(2,1)S(1)} %get-tuple-element.50), channel_id=1, source_target_pairs={{0,8},{4,12},{8,0},{12,4},{16,24},{20,28},{24,16},{28,20},{1,9},{5... | collective-permute-start | bytes 196616 | tf_op jit(solution)/shard_map/ppermute | solution.py:27
  112.1 1.9 %collective-permute-start.34 = (bf16[2,128,128]{2,1,0:T(8,128)(2,1)S(1)}, bf16[2,128,128]{2,1,0:T(8,128)(2,1)S(1)}, u32[]{:S(2)}, u32[]{:S(2)}) collective-permute-start(bf16[2,128,128]{2,1,0:T(8,128)(2,1)S(1)} %get-tuple-element.51), channel_id=1, source_target_pairs={{0,16},{4,20},{8,24},{12,28},{16,0},{20,4},{24,8},{28,12},{1,17},{... | collective-permute-start | bytes 196616 | tf_op jit(solution)/shard_map/ppermute | solution.py:27
  113.9 1.4 %collective-permute-start.35 = (bf16[2,128,128]{2,1,0:T(8,128)(2,1)S(1)}, bf16[2,128,128]{2,1,0:T(8,128)(2,1)S(1)}, u32[]{:S(2)}, u32[]{:S(2)}) collective-permute-start(bf16[2,128,128]{2,1,0:T(8,128)(2,1)S(1)} %get-tuple-element.52), channel_id=1, source_target_pairs={{0,24},{4,28},{8,16},{12,20},{16,8},{20,12},{24,0},{28,4},{1,25},{... | collective-permute-start | bytes 196616 | tf_op jit(solution)/shard_map/ppermute | solution.py:27
  115.3 4.7 %collective-permute-done.34 = bf16[2,128,128]{2,1,0:T(8,128)(2,1)S(1)} collective-permute-done((bf16[2,128,128]{2,1,0:T(8,128)(2,1)S(1)}, bf16[2,128,128]{2,1,0:T(8,128)(2,1)S(1)}, u32[]{:S(2)}, u32[]{:S(2)}) %collective-permute-start.34) | collective-permute-done | bytes 65568 | tf_op jit(solution)/shard_map/ppermute | solution.py:27
  120.2 1.3 %collective-permute-done.36 = bf16[4,128,128]{2,1,0:T(8,128)(2,1)S(1)} collective-permute-done((bf16[4,128,128]{2,1,0:T(8,128)(2,1)S(1)}, bf16[4,128,128]{2,1,0:T(8,128)(2,1)S(1)}, u32[]{:S(2)}, u32[]{:S(2)}) %collective-permute-start.36) | collective-permute-done | bytes 131104 | tf_op jit(solution)/shard_map/ppermute | solution.py:22
  121.8 0.7 copy-done.2
  122.5 0.6 bitcast_dynamic-update-slice_fusion
  (60 shorter events, 1.6 us)
Async XLA Ops:
  0.0 18.5 %copy-start = (f32[3,3,1024]{2,1,0:T(4,128)S(1)}, f32[3,3,1024]{2,1,0:T(4,128)}, u32[]{:S(2)}) copy-start(f32[3,3,1024]{2,1,0:T(4,128)} %param.8) | copy-start | bytes 110596
  0.0 18.5 %collective-permute-start.6 = (bf16[3,1024,1024]{2,1,0:T(8,128)(2,1)}, bf16[3,1024,1024]{2,1,0:T(8,128)(2,1)}, u32[]{:S(2)}, u32[]{:S(2)}) collective-permute-start(bf16[3,1024,1024]{2,1,0:T(8,128)(2,1)} %bitcast.59), channel_id=1, source_target_pairs={{0,4},{4,0},{8,12},{12,8},{16,20},{20,16},{24,28},{28,24},{1,5},{5... | collective-permute-start | bytes 18874376 | tf_op jit(solution)/shard_map/ppermute | solution.py:22
  1.5 7.8 %collective-permute-start = (bf16[32,2048]{1,0:T(8,128)(2,1)S(1)}, bf16[32,2048]{1,0:T(8,128)(2,1)S(1)}, u32[]{:S(2)}, u32[]{:S(2)}) collective-permute-start(bf16[32,2048]{1,0:T(8,128)(2,1)S(1)} %get-tuple-element.63), channel_id=1, source_target_pairs={{0,3},{1,2},{2,1},{3,0},{4,7},{5,6},{6,5},{7,4},{8,11},{9,10},{10,... | collective-permute-start | bytes 393224 | tf_op jit(solution)/shard_map/ppermute | solution.py:31
  5.1 6.9 %collective-permute-start.1 = (bf16[32,2048]{1,0:T(8,128)(2,1)S(1)}, bf16[32,2048]{1,0:T(8,128)(2,1)S(1)}, u32[]{:S(2)}, u32[]{:S(2)}) collective-permute-start(bf16[32,2048]{1,0:T(8,128)(2,1)S(1)} %get-tuple-element.62), channel_id=1, source_target_pairs={{0,2},{1,3},{2,0},{3,1},{4,6},{5,7},{6,4},{7,5},{8,10},{9,11},{10,... | collective-permute-start | bytes 393224 | tf_op jit(solution)/shard_map/ppermute | solution.py:31
  5.6 6.7 %collective-permute-start.2 = (bf16[32,2048]{1,0:T(8,128)(2,1)S(1)}, bf16[32,2048]{1,0:T(8,128)(2,1)S(1)}, u32[]{:S(2)}, u32[]{:S(2)}) collective-permute-start(bf16[32,2048]{1,0:T(8,128)(2,1)S(1)} %get-tuple-element.61), channel_id=1, source_target_pairs={{0,1},{1,0},{2,3},{3,2},{4,5},{5,4},{6,7},{7,6},{8,9},{9,8},{10,11... | collective-permute-start | bytes 393224 | tf_op jit(solution)/shard_map/ppermute | solution.py:31
  13.3 11.4 %collective-permute-start.3 = (bf16[32,2048]{1,0:T(8,128)(2,1)S(1)}, bf16[32,2048]{1,0:T(8,128)(2,1)S(1)}, u32[]{:S(2)}, u32[]{:S(2)}) collective-permute-start(bf16[32,2048]{1,0:T(8,128)(2,1)S(1)} %get-tuple-element.55), channel_id=1, source_target_pairs={{0,8},{4,12},{8,0},{12,4},{16,24},{20,28},{24,16},{28,20},{1,9},{5... | collective-permute-start | bytes 393224 | tf_op jit(solution)/shard_map/ppermute | solution.py:27
  14.9 12.9 %collective-permute-start.4 = (bf16[32,2048]{1,0:T(8,128)(2,1)S(1)}, bf16[32,2048]{1,0:T(8,128)(2,1)S(1)}, u32[]{:S(2)}, u32[]{:S(2)}) collective-permute-start(bf16[32,2048]{1,0:T(8,128)(2,1)S(1)} %get-tuple-element.54), channel_id=1, source_target_pairs={{0,16},{4,20},{8,24},{12,28},{16,0},{20,4},{24,8},{28,12},{1,17},{... | collective-permute-start | bytes 393224 | tf_op jit(solution)/shard_map/ppermute | solution.py:27
  17.5 10.3 %collective-permute-start.5 = (bf16[32,2048]{1,0:T(8,128)(2,1)S(1)}, bf16[32,2048]{1,0:T(8,128)(2,1)S(1)}, u32[]{:S(2)}, u32[]{:S(2)}) collective-permute-start(bf16[32,2048]{1,0:T(8,128)(2,1)S(1)} %get-tuple-element.53), channel_id=1, source_target_pairs={{0,24},{4,28},{8,16},{12,20},{16,8},{20,12},{24,0},{28,4},{1,25},{... | collective-permute-start | bytes 393224 | tf_op jit(solution)/shard_map/ppermute | solution.py:27
  18.5 2.8 %copy-start.1 = (bf16[1024,3,1024]{2,0,1:T(8,128)(2,1)S(1)}, bf16[1024,3,1024]{2,0,1:T(8,128)(2,1)}, u32[]{:S(2)}) copy-start(bf16[1024,3,1024]{2,0,1:T(8,128)(2,1)} %param.7) | copy-start | bytes 18874372
  27.9 6.4 %collective-permute-start.11 = (bf16[64,2048]{1,0:T(8,128)(2,1)S(1)}, bf16[64,2048]{1,0:T(8,128)(2,1)S(1)}, u32[]{:S(2)}, u32[]{:S(2)}) collective-permute-start(bf16[64,2048]{1,0:T(8,128)(2,1)S(1)} %pad_maximum_fusion.1.refs_2_), channel_id=1, source_target_pairs={{0,2},{1,3},{2,0},{3,1},{4,6},{5,7},{6,4},{7,5},{8,10},{9,11},{10,... | collective-permute-start | bytes 786440 | tf_op jit(solution)/shard_map/ppermute | solution.py:31
  29.4 8.6 %collective-permute-start.9 = (bf16[64,2048]{1,0:T(8,128)(2,1)S(1)}, bf16[64,2048]{1,0:T(8,128)(2,1)S(1)}, u32[]{:S(2)}, u32[]{:S(2)}) collective-permute-start(bf16[64,2048]{1,0:T(8,128)(2,1)S(1)} %pad_maximum_fusion.refs_0_), channel_id=1, source_target_pairs={{0,1},{1,0},{2,3},{3,2},{4,5},{5,4},{6,7},{7,6},{8,9},{9,8},{10,11... | collective-permute-start | bytes 786440 | tf_op jit(solution)/shard_map/ppermute | solution.py:31
  30.0 10.9 %collective-permute-start.19 = (bf16[64,2048]{1,0:T(8,128)(2,1)S(1)}, bf16[64,2048]{1,0:T(8,128)(2,1)S(1)}, u32[]{:S(2)}, u32[]{:S(2)}) collective-permute-start(bf16[64,2048]{1,0:T(8,128)(2,1)S(1)} %pad_maximum_fusion.1.refs_2_), channel_id=1, source_target_pairs={{0,1},{1,0},{2,3},{3,2},{4,5},{5,4},{6,7},{7,6},{8,9},{9,8},{10,11... | collective-permute-start | bytes 786440 | tf_op jit(solution)/shard_map/ppermute | solution.py:31
  31.5 9.8 %collective-permute-start.8 = (bf16[64,2048]{1,0:T(8,128)(2,1)S(1)}, bf16[64,2048]{1,0:T(8,128)(2,1)S(1)}, u32[]{:S(2)}, u32[]{:S(2)}) collective-permute-start(bf16[64,2048]{1,0:T(8,128)(2,1)S(1)} %pad_maximum_fusion.1.refs_2_), channel_id=1, source_target_pairs={{0,4},{4,0},{8,12},{12,8},{16,20},{20,16},{24,28},{28,24},{1,5},{5... | collective-permute-start | bytes 786440 | tf_op jit(solution)/shard_map/ppermute | solution.py:22
  31.5 11.2 %collective-permute-start.7 = (bf16[64,2048]{1,0:T(8,128)(2,1)S(1)}, bf16[64,2048]{1,0:T(8,128)(2,1)S(1)}, u32[]{:S(2)}, u32[]{:S(2)}) collective-permute-start(bf16[64,2048]{1,0:T(8,128)(2,1)S(1)} %pad_maximum_fusion.refs_0_), channel_id=1, source_target_pairs={{0,4},{4,0},{8,12},{12,8},{16,20},{20,16},{24,28},{28,24},{1,5},{5... | collective-permute-start | bytes 786440 | tf_op jit(solution)/shard_map/ppermute | solution.py:22
  34.4 8.4 %collective-permute-start.12 = (bf16[64,2048]{1,0:T(8,128)(2,1)S(1)}, bf16[64,2048]{1,0:T(8,128)(2,1)S(1)}, u32[]{:S(2)}, u32[]{:S(2)}) collective-permute-start(bf16[64,2048]{1,0:T(8,128)(2,1)S(1)} %collective-permute-done.11.refs_6_), channel_id=1, source_target_pairs={{0,4},{4,0},{8,12},{12,8},{16,20},{20,16},{24,28},{28,24},{1,5},{5... | collective-permute-start | bytes 786440 | tf_op jit(solution)/shard_map/ppermute | solution.py:22
  38.1 5.2 %collective-permute-start.10 = (bf16[64,2048]{1,0:T(8,128)(2,1)S(1)}, bf16[64,2048]{1,0:T(8,128)(2,1)S(1)}, u32[]{:S(2)}, u32[]{:S(2)}) collective-permute-start(bf16[64,2048]{1,0:T(8,128)(2,1)S(1)} %collective-permute-done.9.refs_4_), channel_id=1, source_target_pairs={{0,4},{4,0},{8,12},{12,8},{16,20},{20,16},{24,28},{28,24},{1,5},{5... | collective-permute-start | bytes 786440 | tf_op jit(solution)/shard_map/ppermute | solution.py:22
  40.9 12.2 %collective-permute-start.21 = (bf16[64,2048]{1,0:T(8,128)(2,1)S(1)}, bf16[64,2048]{1,0:T(8,128)(2,1)S(1)}, u32[]{:S(2)}, u32[]{:S(2)}) collective-permute-start(bf16[64,2048]{1,0:T(8,128)(2,1)S(1)} %pad_maximum_fusion.refs_0_), channel_id=1, source_target_pairs={{0,2},{1,3},{2,0},{3,1},{4,6},{5,7},{6,4},{7,5},{8,10},{9,11},{10,... | collective-permute-start | bytes 786440 | tf_op jit(solution)/shard_map/ppermute | solution.py:31
  41.3 12.5 %collective-permute-start.25 = (bf16[64,2048]{1,0:T(8,128)(2,1)S(1)}, bf16[64,2048]{1,0:T(8,128)(2,1)S(1)}, u32[]{:S(2)}, u32[]{:S(2)}) collective-permute-start(bf16[64,2048]{1,0:T(8,128)(2,1)S(1)} %collective-permute-done.11.refs_6_), channel_id=1, source_target_pairs={{0,1},{1,0},{2,3},{3,2},{4,5},{5,4},{6,7},{7,6},{8,9},{9,8},{10,11... | collective-permute-start | bytes 786440 | tf_op jit(solution)/shard_map/ppermute | solution.py:31
  42.8 11.1 %collective-permute-start.20 = (bf16[64,2048]{1,0:T(8,128)(2,1)S(1)}, bf16[64,2048]{1,0:T(8,128)(2,1)S(1)}, u32[]{:S(2)}, u32[]{:S(2)}) collective-permute-start(bf16[64,2048]{1,0:T(8,128)(2,1)S(1)} %collective-permute-done.19.refs_0_), channel_id=1, source_target_pairs={{0,4},{4,0},{8,12},{12,8},{16,20},{20,16},{24,28},{28,24},{1,5},{5... | collective-permute-start | bytes 786440 | tf_op jit(solution)/shard_map/ppermute | solution.py:22
  42.8 11.5 %collective-permute-start.23 = (bf16[64,2048]{1,0:T(8,128)(2,1)S(1)}, bf16[64,2048]{1,0:T(8,128)(2,1)S(1)}, u32[]{:S(2)}, u32[]{:S(2)}) collective-permute-start(bf16[64,2048]{1,0:T(8,128)(2,1)S(1)} %collective-permute-done.9.refs_4_), channel_id=1, source_target_pairs={{0,2},{1,3},{2,0},{3,1},{4,6},{5,7},{6,4},{7,5},{8,10},{9,11},{10,... | collective-permute-start | bytes 786440 | tf_op jit(solution)/shard_map/ppermute | solution.py:31
  47.8 17.0 %collective-permute-start.13 = (bf16[3,512,128]{2,1,0:T(8,128)(2,1)S(1)}, bf16[3,512,128]{2,1,0:T(8,128)(2,1)S(1)}, u32[]{:S(2)}, u32[]{:S(2)}) collective-permute-start(bf16[3,512,128]{2,1,0:T(8,128)(2,1)S(1)} %get-tuple-element.39), channel_id=1, source_target_pairs={{0,8},{4,12},{1,9},{5,13},{2,10},{6,14},{3,11},{7,15}} | collective-permute-start | bytes 1179656 | tf_op jit(solution)/shard_map/ppermute | solution.py:156
  53.1 11.8 %collective-permute-start.16 = (bf16[3,512,128]{2,1,0:T(8,128)(2,1)S(1)}, bf16[3,512,128]{2,1,0:T(8,128)(2,1)S(1)}, u32[]{:S(2)}, u32[]{:S(2)}) collective-permute-start(bf16[3,512,128]{2,1,0:T(8,128)(2,1)S(1)} %get-tuple-element.37), channel_id=1, source_target_pairs={{24,16},{28,20},{25,17},{29,21},{26,18},{30,22},{27,19},{31,23}} | collective-permute-start | bytes 1179656 | tf_op jit(solution)/shard_map/ppermute | solution.py:156
  53.8 1.6 %collective-permute-start.22 = (bf16[64,2048]{1,0:T(8,128)(2,1)S(1)}, bf16[64,2048]{1,0:T(8,128)(2,1)S(1)}, u32[]{:S(2)}, u32[]{:S(2)}) collective-permute-start(bf16[64,2048]{1,0:T(8,128)(2,1)S(1)} %collective-permute-done.21.refs_2_), channel_id=1, source_target_pairs={{0,4},{4,0},{8,12},{12,8},{16,20},{20,16},{24,28},{28,24},{1,5},{5... | collective-permute-start | bytes 786440 | tf_op jit(solution)/shard_map/ppermute | solution.py:22
  53.8 1.9 %collective-permute-start.26 = (bf16[64,2048]{1,0:T(8,128)(2,1)S(1)}, bf16[64,2048]{1,0:T(8,128)(2,1)S(1)}, u32[]{:S(2)}, u32[]{:S(2)}) collective-permute-start(bf16[64,2048]{1,0:T(8,128)(2,1)S(1)} %collective-permute-done.25.refs_6_), channel_id=1, source_target_pairs={{0,4},{4,0},{8,12},{12,8},{16,20},{20,16},{24,28},{28,24},{1,5},{5... | collective-permute-start | bytes 786440 | tf_op jit(solution)/shard_map/ppermute | solution.py:22
  54.3 1.8 %collective-permute-start.24 = (bf16[64,2048]{1,0:T(8,128)(2,1)S(1)}, bf16[64,2048]{1,0:T(8,128)(2,1)S(1)}, u32[]{:S(2)}, u32[]{:S(2)}) collective-permute-start(bf16[64,2048]{1,0:T(8,128)(2,1)S(1)} %collective-permute-done.23.refs_4_), channel_id=1, source_target_pairs={{0,4},{4,0},{8,12},{12,8},{16,20},{20,16},{24,28},{28,24},{1,5},{5... | collective-permute-start | bytes 786440 | tf_op jit(solution)/shard_map/ppermute | solution.py:22
  60.7 12.9 %collective-permute-start.27 = (bf16[3,512,128]{2,1,0:T(8,128)(2,1)S(1)}, bf16[3,512,128]{2,1,0:T(8,128)(2,1)S(1)}, u32[]{:S(2)}, u32[]{:S(2)}) collective-permute-start(bf16[3,512,128]{2,1,0:T(8,128)(2,1)S(1)} %get-tuple-element.43), channel_id=1, source_target_pairs={{0,8},{4,12},{1,9},{5,13},{2,10},{6,14},{3,11},{7,15}} | collective-permute-start | bytes 1179656 | tf_op jit(solution)/shard_map/ppermute | solution.py:156
  64.2 9.4 %collective-permute-start.30 = (bf16[3,512,128]{2,1,0:T(8,128)(2,1)S(1)}, bf16[3,512,128]{2,1,0:T(8,128)(2,1)S(1)}, u32[]{:S(2)}, u32[]{:S(2)}) collective-permute-start(bf16[3,512,128]{2,1,0:T(8,128)(2,1)S(1)} %get-tuple-element.41), channel_id=1, source_target_pairs={{24,16},{28,20},{25,17},{29,21},{26,18},{30,22},{27,19},{31,23}} | collective-permute-start | bytes 1179656 | tf_op jit(solution)/shard_map/ppermute | solution.py:156
  65.1 17.0 %collective-permute-start.14 = (bf16[3,512,128]{2,1,0:T(8,128)(2,1)S(1)}, bf16[3,512,128]{2,1,0:T(8,128)(2,1)S(1)}, u32[]{:S(2)}, u32[]{:S(2)}) collective-permute-start(bf16[3,512,128]{2,1,0:T(8,128)(2,1)S(1)} %get-tuple-element.68), channel_id=1, source_target_pairs={{0,8},{4,12},{8,16},{12,20},{1,9},{5,13},{9,17},{13,21},{2,10},{6,... | collective-permute-start | bytes 1179656 | tf_op jit(solution)/shard_map/ppermute | solution.py:156
  66.4 20.2 %collective-permute-start.17 = (bf16[3,512,128]{2,1,0:T(8,128)(2,1)S(1)}, bf16[3,512,128]{2,1,0:T(8,128)(2,1)S(1)}, u32[]{:S(2)}, u32[]{:S(2)}) collective-permute-start(bf16[3,512,128]{2,1,0:T(8,128)(2,1)S(1)} %get-tuple-element.69), channel_id=1, source_target_pairs={{24,16},{28,20},{16,8},{20,12},{25,17},{29,21},{17,9},{21,13},{26,... | collective-permute-start | bytes 1179656 | tf_op jit(solution)/shard_map/ppermute | solution.py:156
  73.8 16.7 %collective-permute-start.28 = (bf16[3,512,128]{2,1,0:T(8,128)(2,1)S(1)}, bf16[3,512,128]{2,1,0:T(8,128)(2,1)S(1)}, u32[]{:S(2)}, u32[]{:S(2)}) collective-permute-start(bf16[3,512,128]{2,1,0:T(8,128)(2,1)S(1)} %get-tuple-element.66), channel_id=1, source_target_pairs={{0,8},{4,12},{8,16},{12,20},{1,9},{5,13},{9,17},{13,21},{2,10},{6,... | collective-permute-start | bytes 1179656 | tf_op jit(solution)/shard_map/ppermute | solution.py:156
  78.2 16.8 %collective-permute-start.31 = (bf16[3,512,128]{2,1,0:T(8,128)(2,1)S(1)}, bf16[3,512,128]{2,1,0:T(8,128)(2,1)S(1)}, u32[]{:S(2)}, u32[]{:S(2)}) collective-permute-start(bf16[3,512,128]{2,1,0:T(8,128)(2,1)S(1)} %get-tuple-element.67), channel_id=1, source_target_pairs={{24,16},{28,20},{16,8},{20,12},{25,17},{29,21},{17,9},{21,13},{26,... | collective-permute-start | bytes 1179656 | tf_op jit(solution)/shard_map/ppermute | solution.py:156
  82.1 16.7 %collective-permute-start.15 = (bf16[3,512,128]{2,1,0:T(8,128)(2,1)S(1)}, bf16[3,512,128]{2,1,0:T(8,128)(2,1)S(1)}, u32[]{:S(2)}, u32[]{:S(2)}) collective-permute-start(bf16[3,512,128]{2,1,0:T(8,128)(2,1)S(1)} %add_convert_fusion.5), channel_id=1, source_target_pairs={{0,8},{4,12},{8,16},{12,20},{16,24},{20,28},{1,9},{5,13},{9,17},{1... | collective-permute-start | bytes 1179656 | tf_op jit(solution)/shard_map/ppermute | solution.py:156
  86.7 12.2 %collective-permute-start.18 = (bf16[3,512,128]{2,1,0:T(8,128)(2,1)S(1)}, bf16[3,512,128]{2,1,0:T(8,128)(2,1)S(1)}, u32[]{:S(2)}, u32[]{:S(2)}) collective-permute-start(bf16[3,512,128]{2,1,0:T(8,128)(2,1)S(1)} %add_convert_fusion.4), channel_id=1, source_target_pairs={{24,16},{28,20},{16,8},{20,12},{8,0},{12,4},{25,17},{29,21},{17,9}... | collective-permute-start | bytes 1179656 | tf_op jit(solution)/shard_map/ppermute | solution.py:156
  90.6 15.9 %collective-permute-start.29 = (bf16[3,512,128]{2,1,0:T(8,128)(2,1)S(1)}, bf16[3,512,128]{2,1,0:T(8,128)(2,1)S(1)}, u32[]{:S(2)}, u32[]{:S(2)}) collective-permute-start(bf16[3,512,128]{2,1,0:T(8,128)(2,1)S(1)} %add_convert_fusion.2), channel_id=1, source_target_pairs={{0,8},{4,12},{8,16},{12,20},{16,24},{20,28},{1,9},{5,13},{9,17},{1... | collective-permute-start | bytes 1179656 | tf_op jit(solution)/shard_map/ppermute | solution.py:156
  95.1 11.4 %collective-permute-start.32 = (bf16[3,512,128]{2,1,0:T(8,128)(2,1)S(1)}, bf16[3,512,128]{2,1,0:T(8,128)(2,1)S(1)}, u32[]{:S(2)}, u32[]{:S(2)}) collective-permute-start(bf16[3,512,128]{2,1,0:T(8,128)(2,1)S(1)} %add_convert_fusion.1), channel_id=1, source_target_pairs={{24,16},{28,20},{16,8},{20,12},{8,0},{12,4},{25,17},{29,21},{17,9}... | collective-permute-start | bytes 1179656 | tf_op jit(solution)/shard_map/ppermute | solution.py:156
  109.5 5.8 %collective-permute-start.33 = (bf16[2,128,128]{2,1,0:T(8,128)(2,1)S(1)}, bf16[2,128,128]{2,1,0:T(8,128)(2,1)S(1)}, u32[]{:S(2)}, u32[]{:S(2)}) collective-permute-start(bf16[2,128,128]{2,1,0:T(8,128)(2,1)S(1)} %get-tuple-element.50), channel_id=1, source_target_pairs={{0,8},{4,12},{8,0},{12,4},{16,24},{20,28},{24,16},{28,20},{1,9},{5... | collective-permute-start | bytes 196616 | tf_op jit(solution)/shard_map/ppermute | solution.py:27
  112.1 8.0 %collective-permute-start.34 = (bf16[2,128,128]{2,1,0:T(8,128)(2,1)S(1)}, bf16[2,128,128]{2,1,0:T(8,128)(2,1)S(1)}, u32[]{:S(2)}, u32[]{:S(2)}) collective-permute-start(bf16[2,128,128]{2,1,0:T(8,128)(2,1)S(1)} %get-tuple-element.51), channel_id=1, source_target_pairs={{0,16},{4,20},{8,24},{12,28},{16,0},{20,4},{24,8},{28,12},{1,17},{... | collective-permute-start | bytes 196616 | tf_op jit(solution)/shard_map/ppermute | solution.py:27
  113.9 6.1 %collective-permute-start.35 = (bf16[2,128,128]{2,1,0:T(8,128)(2,1)S(1)}, bf16[2,128,128]{2,1,0:T(8,128)(2,1)S(1)}, u32[]{:S(2)}, u32[]{:S(2)}) collective-permute-start(bf16[2,128,128]{2,1,0:T(8,128)(2,1)S(1)} %get-tuple-element.52), channel_id=1, source_target_pairs={{0,24},{4,28},{8,16},{12,20},{16,8},{20,12},{24,0},{28,4},{1,25},{... | collective-permute-start | bytes 196616 | tf_op jit(solution)/shard_map/ppermute | solution.py:27
  120.1 1.4 %collective-permute-start.36 = (bf16[4,128,128]{2,1,0:T(8,128)(2,1)S(1)}, bf16[4,128,128]{2,1,0:T(8,128)(2,1)S(1)}, u32[]{:S(2)}, u32[]{:S(2)}) collective-permute-start(bf16[4,128,128]{2,1,0:T(8,128)(2,1)S(1)} %dynamic-slice_bitcast_fusion), channel_id=1, source_target_pairs={{0,4},{4,0},{8,12},{12,8},{16,20},{20,16},{24,28},{28,24},{1,5},{5... | collective-permute-start | bytes 393224 | tf_op jit(solution)/shard_map/ppermute | solution.py:22
  121.8 0.7 copy-start.2

commit v3 on v2

--- a/solution.py
+++ b/solution.py
@@ -47,6 +47,10 @@
         piece = pick(got, me ^ z ^ u)
         came.append(to_plane(piece, u, planes) if u else piece)
     return came
+
+
+def plane_of(z, r, planes):
+    return (z + (1 - 2 * (z % 2)) * r + planes) % planes
 
 
 def sending_order(planes):
@@ -62,7 +66,7 @@
         owner = core if side == 0 else 1 - core
         rows = pl.ds(pl.multiple_of(owner * depth, depth), depth)
         for i, r in enumerate(sending_order(planes)):
-            columns = pl.ds(pl.multiple_of(core * half + (z + r) % planes * lanes, lanes), lanes)
+            columns = pl.ds(pl.multiple_of(core * half + plane_of(z, r, planes) * lanes, lanes), lanes)
             copy = pltpu.make_async_copy(
                 w.at[:, :, columns], out_ref.at[:, rows, pl.ds(i * lanes, lanes)], sems.at[side, i]
             )
@@ -78,7 +82,7 @@
     if lanes % 128:
         w = jnp.concatenate([pick([w_own, w_sib], core), pick([w_own, w_sib], 1 - core)], axis=1)
         w = lax.dynamic_slice_in_dim(w, core * half, half, 2).reshape(3, 2 * depth, planes, lanes)
-        blocks = [lax.dynamic_index_in_dim(w, (z + r) % planes, 2, keepdims=False) for r in sending_order(planes)]
+        blocks = [lax.dynamic_index_in_dim(w, plane_of(z, r, planes), 2, keepdims=False) for r in sending_order(planes)]
         return jnp.concatenate(blocks, axis=2)
     hbm = pl.BlockSpec(memory_space=pltpu.HBM)
     return pl.pallas_call(
@@ -93,9 +97,11 @@
     )(jnp.stack([z, core]).astype(jnp.int32), w_own, w_sib)
 
 
-def project_kernel(planes, pieces, *refs):
+def project_kernel(planes, pieces, merged, *refs):
     x_refs, w_ref, outs, x_all = refs[:pieces], refs[pieces], refs[pieces + 1 : -1], refs[-1]
     lanes = w_ref.shape[2] // planes
+    if merged:
+        outs = [*outs[:-1], outs[-1].at[1], outs[-1].at[0]]
     at = 0
     for ref in x_refs:
         x_all[at : at + ref.shape[0]] = ref[...]
@@ -111,7 +117,7 @@
             outs[order[i + 1]][j] = sums[:, lanes:]
 
 
-def project(xs, w, planes):
+def project(xs, w, planes, merged):
     rows = sum(x.shape[0] for x in xs)
     wide, half = w.shape[1:]
     lanes = half // planes
@@ -119,13 +125,18 @@
         x = jnp.concatenate(xs, axis=0)
         sums = jnp.einsum("tk,jkc->jtc", x, w, preferred_element_type=F32).astype(BF16)
         order = sending_order(planes)
-        return [sums[:, :, order.index(r) * lanes : (order.index(r) + 1) * lanes] for r in range(planes)]
+        blocks = [sums[:, :, order.index(r) * lanes : (order.index(r) + 1) * lanes] for r in range(planes)]
+        return [*blocks[:-2], jnp.stack([blocks[-1], blocks[-2]])] if merged else blocks
     vmem = pl.BlockSpec(memory_space=pltpu.VMEM)
+    block = jax.ShapeDtypeStruct((3, rows, lanes), BF16)
+    out_shape = [block] * planes
+    if merged:
+        out_shape = [block] * (planes - 2) + [jax.ShapeDtypeStruct((2, 3, rows, lanes), BF16)]
     return pl.pallas_call(
-        lambda *refs: project_kernel(planes, len(xs), *refs),
+        lambda *refs: project_kernel(planes, len(xs), merged, *refs),
         in_specs=[vmem] * (len(xs) + 1),
-        out_specs=[vmem] * planes,
-        out_shape=[jax.ShapeDtypeStruct((3, rows, lanes), BF16)] * planes,
+        out_specs=[vmem] * len(out_shape),
+        out_shape=out_shape,
         scratch_shapes=[pltpu.VMEM((rows, wide), BF16)],
         compiler_params=pltpu.CompilerParams(vmem_limit_bytes=8 << 20),
         cost_estimate=pl.CostEstimate(flops=0, bytes_accessed=0, transcendentals=0),
@@ -141,26 +152,58 @@
 
 
 class LineSum:
-    def __init__(self, blocks):
-        self.blocks, self.last = blocks, len(blocks) - 1
-        self.step, self.came = 0, None
-
-    def send(self):
-        t, last = self.step, self.last
-        up, down = self.blocks[last - t], self.blocks[t + 1]
-        if t:
-            up, down = add(up, self.came[0]), add(down, self.came[1])
-        planes = range(min(t + 1, last))
-        up_route = [(2 * z + c, 2 * z + 2 + c) for z in planes for c in range(2)]
-        down_route = [(2 * (last - z) + c, 2 * (last - z) - 2 + c) for z in planes for c in range(2)]
-        self.came = [lax.ppermute(up, "ctx", up_route), lax.ppermute(down, "ctx", down_route)]
-        self.step += 1
-
-    def after(self, value):
-        *self.came, _ = lax.optimization_barrier((*self.came, value))
+    def __init__(self, planes):
+        self.planes, self.last = planes, planes - 1
+        self.blocks = [[] for _ in range(planes)]
+        self.even, self.odd = {-1: []}, {-1: []}
+
+    def take(self, blocks):
+        for mine, block in zip(self.blocks, blocks, strict=True):
+            mine.append(block)
+
+    def take_and_send(self, blocks):
+        *blocks, first = blocks
+        self.take([*blocks, first[1], first[0]])
+        came = self.exchange(0, first, 0)
+        for t in range(2):
+            self.even.setdefault(t, []).append(came[t])
+        self.odd[0] = []
+
+    def exchange(self, t, block, first):
+        route = []
+        for e in range(first, self.last, 2):
+            if e <= t:
+                route += [(2 * e + c, 2 * e + 2 + c) for c in range(2)]
+            if self.last - e - 1 <= t:
+                route += [(2 * e + 2 + c, 2 * e + c) for c in range(2)]
+        return lax.ppermute(block, "ctx", route) if route else None
+
+    def send(self, t, r, came, first):
+        sent = self.exchange(t, add_parts(self.blocks[r], came), first)
+        return [] if sent is None else [sent]
+
+    def send_even(self, t):
+        if t not in self.even:
+            self.even[t] = self.send(t, self.last - t, self.odd[t - 1], 0)
+
+    def send_odd(self, t):
+        if t not in self.odd:
+            self.odd[t] = self.send(t, t + 1, self.even[t - 1], 1)
 
     def total(self):
-        return add(self.blocks[0], *self.came)
+        return add_parts(self.blocks[0], self.even[self.last - 1], self.odd[self.last - 1])
+
+
+def add_parts(*values):
+    values = [value for value in values if value]
+    if len({len(value) for value in values}) > 1:
+        values = [[jnp.concatenate(value, axis=1)] if len(value) > 1 else value for value in values]
+    parts = [add(*blocks) if len(blocks) > 1 else blocks[0] for blocks in zip(*values, strict=True)]
+    return jnp.concatenate(parts, axis=1) if len(parts) > 1 else parts[0]
+
+
+def tie(first, then):
+    return lax.optimization_barrier((first, then))[1]
 
 
 def long_filters(decay, weight):
@@ -330,24 +373,33 @@
     middle = planes // 2
     x = [jnp.concatenate(by_plane[:middle], axis=0), jnp.concatenate(by_plane[middle:], axis=0)]
 
-    order = []
-
-    def project_pieces(pieces):
-        xs = [y for piece, _, _ in pieces for y in (piece, swap_cores(piece, n_ctx))]
-        order.append([(side, s, h * middle) for _, s, h in pieces for side in range(2)])
-        return LineSum(project(xs, w, planes))
-
-    near = [to_column(x[0], 1, n_ch), to_column(x[1], 2, n_ch), to_column(x[1], 1, n_ch), to_column(x[0], 2, n_ch)]
-    a = project_pieces([(x[0], 0, 0), (x[1], 0, 1), (near[0], 1, 0), (near[1], 2, 1)])
-    far = [to_column(near[0], 2, n_ch), to_column(near[1], 1, n_ch)]
-    rest = [(near[2], 1, 1), (near[3], 2, 0), (far[0], 3, 0), (far[1], 3, 1)]
-    rest += [(to_column(x[h], s, n_ch), s, h) for s in range(4, n_ch) for h in range(2)]
-    b = project_pieces(rest)
-    streams = [a, b]
-    for step in range(planes - 1):
-        for stream in streams:
-            stream.send()
-    data = [stream.total() for stream in streams]
+    order = [[], []]
+
+    def project_pieces(stream, xs, pieces, merged):
+        xs = xs + [swap_cores(y, n_ctx) for y in xs]
+        order[stream].extend([(side, s, h * middle) for side in range(2) for s, h in pieces])
+        return project(xs, w, planes, merged)
+
+    near = [to_column(x[0], 1, n_ch), to_column(x[1], 2, n_ch)]
+    rest = [
+        to_column(jnp.concatenate([x[1], near[1]], axis=0), 1, n_ch),
+        to_column(jnp.concatenate([x[0], near[0]], axis=0), 2, n_ch),
+    ]
+    rest += [to_column(x[h], s, n_ch) for s in range(4, n_ch) for h in range(2)]
+    a, b = LineSum(planes), LineSum(planes)
+    blocks = project_pieces(0, x, [(0, 0), (0, 1)], True)
+    a.take_and_send(blocks)
+    near = tie(blocks[0], near)
+    blocks = project_pieces(0, near, [(1, 0), (2, 1)], True)
+    a.take_and_send(blocks)
+    rest = tie(blocks[0], rest)
+    halves = [(1, 1), (3, 1), (2, 0), (3, 0)] + [(s, h) for s in range(4, n_ch) for h in range(2)]
+    b.take(project_pieces(1, rest, halves, False))
+    for t in range(planes - 1):
+        for stream in (a, b):
+            stream.send_even(t)
+            stream.send_odd(t)
+    data = [stream.total() for stream in (a, b)]
     outs = mix(
         data,
         order,

time: 124 us -> 117 us (0.944)
  waiting for transfers between devices: 44.7 us -> 28.2 us
  starting transfers between devices: 50.6 us -> 59.4 us
    ppermute x12 -> x10, waiting for transfers between devices: 22 us -> 9.37 us  [exchange(): return lax.ppermute(block, 'ctx', route) if route else None]
    ppermute x12 -> x10, starting transfers between devices: 28.6 us -> 40.5 us  [exchange(): return lax.ppermute(block, 'ctx', route) if route else None]
    ppermute x9 -> x7, waiting for transfers between devices: 11.8 us -> 9.51 us  [to_column(): return lax.ppermute(block, 'ch', [(j, j ^ distance) for j in range(n_ch)])]
    ppermute x9 -> x7, starting transfers between devices: 10.1 us -> 7.88 us  [to_column(): return lax.ppermute(block, 'ch', [(j, j ^ distance) for j in range(n_ch)])]
    ppermute x10 -> x8, waiting for transfers between devices: 3.02 us -> 1.34 us  [swap_cores(): return lax.ppermute(block, 'ctx', [(i, i ^ 1) for i in range(n_ctx)])]
    ppermute x6, starting transfers between devices: 10.2 us -> 8.9 us  [to_plane(): return lax.ppermute(block, 'ctx', route)]
    pallas_call x2 -> x3, Pallas kernels: 9.08 us -> 10.3 us  [project(): pl.pallas_call(lambda *refs: project_kernel(planes, len(xs), merged, *ref...]
  transfers between devices with their start and end apart: 37 -> 31, of which waited for: 16 -> 13; matrix products, arithmetic and copies ran while one was open for 6% -> 6% of each run, Pallas kernels for 10% -> 12%
where the time goes in v3:
time: 117 us
  starting transfers between devices  59.4 us (51%)
  waiting for transfers between devices  28.2 us (24%)
  Pallas kernels  16.5 us (14%)
  local copies, waits for them, and re-layouts  6.41 us (5%)
  other arithmetic  5.6 us (5%)
    ppermute x10, starting transfers between devices, exchange(): return lax.ppermute(block, 'ctx', route) if route else None  40.5 us
    pallas_call x3, Pallas kernels, project(): pl.pallas_call(lambda *refs: project_kernel(planes, len(xs), merged, *ref...  10.3 us
    ppermute x7, waiting for transfers between devices, to_column(): return lax.ppermute(block, 'ch', [(j, j ^ distance) for j in range(n_ch)])  9.51 us
    ppermute x10, waiting for transfers between devices, exchange(): return lax.ppermute(block, 'ctx', route) if route else None  9.37 us
    ppermute x6, starting transfers between devices, to_plane(): return lax.ppermute(block, 'ctx', route)  8.9 us
    ppermute x6, waiting for transfers between devices, to_plane(): return lax.ppermute(block, 'ctx', route)  7.95 us
    ppermute x7, starting transfers between devices, to_column(): return lax.ppermute(block, 'ch', [(j, j ^ distance) for j in range(n_ch)])  7.88 us
    unnamed x8, local copies, waits for them, and re-layouts  3.62 us
  transfers between devices with their start and end apart: 31, of which 13 were waited for; matrix products, arithmetic and copies ran while one was open for 6% of the time, Pallas kernels for 12%

profile of v3, /device:TPU:0, one launch (start us, length us, event | category | flops | bytes accessed | tf_op | source)
XLA Modules:
  0.0 116.6 jit_solution(10940304264410414998)
XLA Ops:
  0.0 0.5 collective-permute-start.6
  0.5 1.1 dynamic-slice_bitcast_fusion.1
  1.5 3.5 %collective-permute-start = (bf16[32,2048]{1,0:T(8,128)(2,1)S(1)}, bf16[32,2048]{1,0:T(8,128)(2,1)S(1)}, u32[]{:S(2)}, u32[]{:S(2)}) collective-permute-start(bf16[32,2048]{1,0:T(8,128)(2,1)S(1)} %get-tuple-element.79), channel_id=1, source_target_pairs={{0,3},{1,2},{2,1},{3,0},{4,7},{5,6},{6,5},{7,4},{8,11},{9,10},{10,... | collective-permute-start | bytes 393224 | tf_op jit(solution)/shard_map/ppermute | solution.py:31
  5.1 0.5 collective-permute-start.1
  5.6 0.1 collective-permute-start.2
  5.7 0.8 constant_dynamic-slice_fusion.1
  6.6 0.1 mul.90
  6.7 0.1 neg.20
  6.9 2.2 %multiply_reduce_fusion = f32[8,128,128]{2,1,0:T(8,128)S(1)} fusion(f32[128,128]{1,0:T(8,128)S(1)} %maximum_convert_fusion, f32[8,16]{1,0:T(8,128)S(1)} %get-tuple-element.83, f32[8,16]{1,0:T(8,128)S(1)} %get-tuple-element.82), kind=kLoop, calls=%fused_computation | loop fusion | flops 6160384 | bytes 590848 | tf_op jit(solution)/shard_map/reduce_sum | solution.py:213
  9.1 0.1 exponential_multiply_fusion
  9.2 0.1 pad_add_fusion.1.refs_0_
  9.3 2.7 %collective-permute-done.1 = bf16[32,2048]{1,0:T(8,128)(2,1)S(1)} collective-permute-done((bf16[32,2048]{1,0:T(8,128)(2,1)S(1)}, bf16[32,2048]{1,0:T(8,128)(2,1)S(1)}, u32[]{:S(2)}, u32[]{:S(2)}) %collective-permute-start.1) | collective-permute-done | bytes 131104 | tf_op jit(solution)/shard_map/ppermute | solution.py:31
  12.0 0.3 collective-permute-done.2
  12.3 1.0 fusion.11
  13.3 1.6 %collective-permute-start.3 = (bf16[32,2048]{1,0:T(8,128)(2,1)S(1)}, bf16[32,2048]{1,0:T(8,128)(2,1)S(1)}, u32[]{:S(2)}, u32[]{:S(2)}) collective-permute-start(bf16[32,2048]{1,0:T(8,128)(2,1)S(1)} %get-tuple-element.67), channel_id=1, source_target_pairs={{0,8},{4,12},{8,0},{12,4},{16,24},{20,28},{24,16},{28,20},{1,9},{5... | collective-permute-start | bytes 393224 | tf_op jit(solution)/shard_map/ppermute | solution.py:27
  14.9 2.6 %collective-permute-start.4 = (bf16[32,2048]{1,0:T(8,128)(2,1)S(1)}, bf16[32,2048]{1,0:T(8,128)(2,1)S(1)}, u32[]{:S(2)}, u32[]{:S(2)}) collective-permute-start(bf16[32,2048]{1,0:T(8,128)(2,1)S(1)} %get-tuple-element.66), channel_id=1, source_target_pairs={{0,16},{4,20},{8,24},{12,28},{16,0},{20,4},{24,8},{28,12},{1,17},{... | collective-permute-start | bytes 393224 | tf_op jit(solution)/shard_map/ppermute | solution.py:27
  17.5 0.2 collective-permute-start.5
  17.7 0.8 dynamic-slice_bitcast_fusion.4.refs_4_
  18.5 2.8 %copy-done.1 = bf16[1024,3,1024]{2,0,1:T(8,128)(2,1)S(1)} copy-done((bf16[1024,3,1024]{2,0,1:T(8,128)(2,1)S(1)}, bf16[1024,3,1024]{2,0,1:T(8,128)(2,1)}, u32[]{:S(2)}) %copy-start.1) | copy-done | bytes 6291480
  21.3 3.4 %stage.1.refs_4_ = bf16[3,2048,512]{2,1,0:T(8,128)(2,1)S(1)} custom-call(s32[2]{0:T(128)S(1)} %pad_add_fusion.1.refs_0_, bf16[3,1024,1024]{2,1,0:T(8,128)(2,1)S(1)} %bitcast.68, bf16[3,1024,1024]{2,1,0:T(8,128)(2,1)} %collective-permute-done.6.refs_2_), custom_call_target="tpu_custom_call" | custom-call | tf_op jit(solution)/shard_map/stage/pallas_call | solution.py:88
  24.7 3.1 %collective-permute-done.4 = bf16[32,2048]{1,0:T(8,128)(2,1)S(1)} collective-permute-done((bf16[32,2048]{1,0:T(8,128)(2,1)S(1)}, bf16[32,2048]{1,0:T(8,128)(2,1)S(1)}, u32[]{:S(2)}, u32[]{:S(2)}) %collective-permute-start.4) | collective-permute-done | bytes 131104 | tf_op jit(solution)/shard_map/ppermute | solution.py:27
  27.9 1.6 %collective-permute-start.9 = (bf16[64,2048]{1,0:T(8,128)(2,1)S(1)}, bf16[64,2048]{1,0:T(8,128)(2,1)S(1)}, u32[]{:S(2)}, u32[]{:S(2)}) collective-permute-start(bf16[64,2048]{1,0:T(8,128)(2,1)S(1)} %pad_maximum_fusion.4.refs_0_), channel_id=1, source_target_pairs={{0,1},{1,0},{2,3},{3,2},{4,5},{5,4},{6,7},{7,6},{8,9},{9,8},{10,11... | collective-permute-start | bytes 786440 | tf_op jit(solution)/shard_map/ppermute | solution.py:31
  29.5 0.4 collective-permute-start.10
  30.0 0.5 collective-permute-start.7
  30.5 3.9 %collective-permute-done.9.refs_0_ = bf16[64,2048]{1,0:T(8,128)(2,1)S(1)} collective-permute-done((bf16[64,2048]{1,0:T(8,128)(2,1)S(1)}, bf16[64,2048]{1,0:T(8,128)(2,1)S(1)}, u32[]{:S(2)}, u32[]{:S(2)}) %collective-permute-start.9) | collective-permute-done | bytes 262176 | tf_op jit(solution)/shard_map/ppermute | solution.py:31
  34.4 1.6 %collective-permute-start.19 = (bf16[128,2048]{1,0:T(8,128)(2,1)S(1)}, bf16[128,2048]{1,0:T(8,128)(2,1)S(1)}, u32[]{:S(2)}, u32[]{:S(2)}) collective-permute-start(bf16[128,2048]{1,0:T(8,128)(2,1)S(1)} %pad_maximum_fusion.1), channel_id=1, source_target_pairs={{0,2},{1,3},{2,0},{3,1},{4,6},{5,7},{6,4},{7,5},{8,10},{9,11},{10,... | collective-permute-start | bytes 1572872 | tf_op jit(solution)/shard_map/ppermute | solution.py:31
  36.1 2.4 %collective-permute-done.10.refs_1_ = bf16[64,2048]{1,0:T(8,128)(2,1)S(1)} collective-permute-done((bf16[64,2048]{1,0:T(8,128)(2,1)S(1)}, bf16[64,2048]{1,0:T(8,128)(2,1)S(1)}, u32[]{:S(2)}, u32[]{:S(2)}) %collective-permute-start.10) | collective-permute-done | bytes 262176 | tf_op jit(solution)/shard_map/ppermute | solution.py:31
  38.6 2.9 %project.3 = (bf16[3,256,128]{2,1,0:T(8,128)(2,1)S(1)}, bf16[3,256,128]{2,1,0:T(8,128)(2,1)S(1)}, bf16[2,3,256,128]{3,2,1,0:T(8,128)(2,1)S(1)}) custom-call(bf16[64,2048]{1,0:T(8,128)(2,1)S(1)} %pad_maximum_fusion.4.refs_0_, bf16[64,2048]{1,0:T(8,128)(2,1)S(1)} %pad_maximum_fusion.5.refs_1_, bf16[64,2048]{1,0:T(8,128)(2,1)S(1)} %collective-permute-done.7.refs_2_, ...), custom_call_target="tpu_custom_call" | custom-call | tf_op jit(solution)/shard_map/project/pallas_call | solution.py:135
  41.6 0.5 collective-permute-start.12
  42.0 2.6 %collective-permute-start.13 = (bf16[2,3,256,128]{3,2,1,0:T(8,128)(2,1)S(1)}, bf16[2,3,256,128]{3,2,1,0:T(8,128)(2,1)S(1)}, u32[]{:S(2)}, u32[]{:S(2)}) collective-permute-start(bf16[2,3,256,128]{3,2,1,0:T(8,128)(2,1)S(1)} %get-tuple-element.48), channel_id=1, source_target_pairs={{0,8},{4,12},{24,16},{28,20},{1,9},{5,13},{25,17},{29,21},{2,10},{... | collective-permute-start | bytes 1179656 | tf_op jit(solution)/shard_map/ppermute | solution.py:179
  44.7 2.9 %project.4 = (bf16[3,256,128]{2,1,0:T(8,128)(2,1)S(1)}, bf16[3,256,128]{2,1,0:T(8,128)(2,1)S(1)}, bf16[2,3,256,128]{3,2,1,0:T(8,128)(2,1)S(1)}) custom-call(bf16[64,2048]{1,0:T(8,128)(2,1)S(1)} %collective-permute-done.9.refs_0_, bf16[64,2048]{1,0:T(8,128)(2,1)S(1)} %collective-permute-done.10.refs_1_, bf16[64,2048]{1,0:T(8,128)(2,1)S(1)} %collective-permute-done.11.refs_2_, ...), custom_call_target="tpu_custom_call" | custom-call | tf_op jit(solution)/shard_map/project/pallas_call | solution.py:135
  47.5 0.2 collective-permute-done.18.refs_0_
  47.8 0.5 collective-permute-start.21
  48.3 4.7 %collective-permute-start.14 = (bf16[2,3,256,128]{3,2,1,0:T(8,128)(2,1)S(1)}, bf16[2,3,256,128]{3,2,1,0:T(8,128)(2,1)S(1)}, u32[]{:S(2)}, u32[]{:S(2)}) collective-permute-start(bf16[2,3,256,128]{3,2,1,0:T(8,128)(2,1)S(1)} %get-tuple-element.49), channel_id=1, source_target_pairs={{0,8},{4,12},{24,16},{28,20},{1,9},{5,13},{25,17},{29,21},{2,10},{... | collective-permute-start | bytes 1179656 | tf_op jit(solution)/shard_map/ppermute | solution.py:179
  53.0 0.4 collective-permute-done.13
  53.3 0.1 fusion
  53.5 4.5 %project.5 = (bf16[3,512,128]{2,1,0:T(8,128)(2,1)S(1)}, bf16[3,512,128]{2,1,0:T(8,128)(2,1)S(1)}, bf16[3,512,128]{2,1,0:T(8,128)(2,1)S(1)}, bf16[3,512,128]{2,1,0:T(8,128)(2,1)S(1)}) custom-call(bf16[128,2048]{1,0:T(8,128)(2,1)S(1)} %collective-permute-done.18.refs_0_, bf16[128,2048]{1,0:T(8,128)(2,1)S(1)} %collective-permute-done.19.refs_1_, ...), custom_call_target="tpu_custom_call" | custom-call | tf_op jit(solution)/shard_map/project/pallas_call | solution.py:135
  58.0 4.4 %collective-permute-start.22 = (bf16[3,512,128]{2,1,0:T(8,128)(2,1)S(1)}, bf16[3,512,128]{2,1,0:T(8,128)(2,1)S(1)}, u32[]{:S(2)}, u32[]{:S(2)}) collective-permute-start(bf16[3,512,128]{2,1,0:T(8,128)(2,1)S(1)} %get-tuple-element.55), channel_id=1, source_target_pairs={{0,8},{4,12},{24,16},{28,20},{1,9},{5,13},{25,17},{29,21},{2,10},{... | collective-permute-start | bytes 1179656 | tf_op jit(solution)/shard_map/ppermute | solution.py:179
  62.4 0.1 fusion.1
  62.6 0.7 collective-permute-start.15
  63.3 0.7 collective-permute-start.17
  64.0 8.1 %collective-permute-start.25 = (bf16[3,512,128]{2,1,0:T(8,128)(2,1)S(1)}, bf16[3,512,128]{2,1,0:T(8,128)(2,1)S(1)}, u32[]{:S(2)}, u32[]{:S(2)}) collective-permute-start(bf16[3,512,128]{2,1,0:T(8,128)(2,1)S(1)} %get-tuple-element.54), channel_id=1, source_target_pairs={{0,8},{4,12},{24,16},{28,20},{1,9},{5,13},{25,17},{29,21},{2,10},{... | collective-permute-start | bytes 1179656 | tf_op jit(solution)/shard_map/ppermute | solution.py:179
  72.1 0.1 add_convert_fusion.3
  72.2 0.7 collective-permute-start.23
  72.9 0.1 add_convert_fusion.5
  73.0 5.3 %collective-permute-start.16 = (bf16[3,512,128]{2,1,0:T(8,128)(2,1)S(1)}, bf16[3,512,128]{2,1,0:T(8,128)(2,1)S(1)}, u32[]{:S(2)}, u32[]{:S(2)}) collective-permute-start(bf16[3,512,128]{2,1,0:T(8,128)(2,1)S(1)} %add_convert_fusion.5), channel_id=1, source_target_pairs={{0,8},{4,12},{8,0},{12,4},{16,24},{20,28},{24,16},{28,20},{1,9},{5... | collective-permute-start | bytes 1179656 | tf_op jit(solution)/shard_map/ppermute | solution.py:179
  78.4 3.2 %collective-permute-done.25 = bf16[3,512,128]{2,1,0:T(8,128)(2,1)S(1)} collective-permute-done((bf16[3,512,128]{2,1,0:T(8,128)(2,1)S(1)}, bf16[3,512,128]{2,1,0:T(8,128)(2,1)S(1)}, u32[]{:S(2)}, u32[]{:S(2)}) %collective-permute-start.25) | collective-permute-done | bytes 393248 | tf_op jit(solution)/shard_map/ppermute | solution.py:179
  81.6 0.1 add_convert_fusion.1
  81.7 0.7 collective-permute-start.26
  82.4 0.1 add_convert_fusion.2
  82.5 12.7 %collective-permute-start.24 = (bf16[3,512,128]{2,1,0:T(8,128)(2,1)S(1)}, bf16[3,512,128]{2,1,0:T(8,128)(2,1)S(1)}, u32[]{:S(2)}, u32[]{:S(2)}) collective-permute-start(bf16[3,512,128]{2,1,0:T(8,128)(2,1)S(1)} %add_convert_fusion.2), channel_id=1, source_target_pairs={{0,8},{4,12},{8,0},{12,4},{16,24},{20,28},{24,16},{28,20},{1,9},{5... | collective-permute-start | bytes 1179656 | tf_op jit(solution)/shard_map/ppermute | solution.py:179
  95.3 0.2 add_convert_fusion.4.refs_1_
  95.5 5.7 %collective-permute-done.24 = bf16[3,512,128]{2,1,0:T(8,128)(2,1)S(1)} collective-permute-done((bf16[3,512,128]{2,1,0:T(8,128)(2,1)S(1)}, bf16[3,512,128]{2,1,0:T(8,128)(2,1)S(1)}, u32[]{:S(2)}, u32[]{:S(2)}) %collective-permute-start.24) | collective-permute-done | bytes 393248 | tf_op jit(solution)/shard_map/ppermute | solution.py:179
  101.2 0.2 add_convert_fusion.refs_2_
  101.4 2.8 %mix.1 = (bf16[2,128,128]{2,1,0:T(8,128)(2,1)S(1)}, bf16[2,128,128]{2,1,0:T(8,128)(2,1)S(1)}, bf16[2,128,128]{2,1,0:T(8,128)(2,1)S(1)}, bf16[2,128,128]{2,1,0:T(8,128)(2,1)S(1)}) custom-call(s32[3]{0:T(128)S(1)} %pad_add_fusion.refs_0_, bf16[3,512,128]{2,1,0:T(8,128)(2,1)S(1)} %add_convert_fusion.4.refs_1_, ...), custom_call_target="tpu_custom_call" | custom-call | tf_op jit(solution)/shard_map/mix/pallas_call | solution.py:299
  104.2 1.8 %collective-permute-start.27 = (bf16[2,128,128]{2,1,0:T(8,128)(2,1)S(1)}, bf16[2,128,128]{2,1,0:T(8,128)(2,1)S(1)}, u32[]{:S(2)}, u32[]{:S(2)}) collective-permute-start(bf16[2,128,128]{2,1,0:T(8,128)(2,1)S(1)} %get-tuple-element.62), channel_id=1, source_target_pairs={{0,8},{4,12},{8,0},{12,4},{16,24},{20,28},{24,16},{28,20},{1,9},{5... | collective-permute-start | bytes 196616 | tf_op jit(solution)/shard_map/ppermute | solution.py:27
  106.1 1.2 %collective-permute-start.28 = (bf16[2,128,128]{2,1,0:T(8,128)(2,1)S(1)}, bf16[2,128,128]{2,1,0:T(8,128)(2,1)S(1)}, u32[]{:S(2)}, u32[]{:S(2)}) collective-permute-start(bf16[2,128,128]{2,1,0:T(8,128)(2,1)S(1)} %get-tuple-element.63), channel_id=1, source_target_pairs={{0,16},{4,20},{8,24},{12,28},{16,0},{20,4},{24,8},{28,12},{1,17},{... | collective-permute-start | bytes 196616 | tf_op jit(solution)/shard_map/ppermute | solution.py:27
  107.3 1.4 %collective-permute-start.29 = (bf16[2,128,128]{2,1,0:T(8,128)(2,1)S(1)}, bf16[2,128,128]{2,1,0:T(8,128)(2,1)S(1)}, u32[]{:S(2)}, u32[]{:S(2)}) collective-permute-start(bf16[2,128,128]{2,1,0:T(8,128)(2,1)S(1)} %get-tuple-element.64), channel_id=1, source_target_pairs={{0,24},{4,28},{8,16},{12,20},{16,8},{20,12},{24,0},{28,4},{1,25},{... | collective-permute-start | bytes 196616 | tf_op jit(solution)/shard_map/ppermute | solution.py:27
  108.7 0.2 collective-permute-done.27
  108.9 3.0 %collective-permute-done.28 = bf16[2,128,128]{2,1,0:T(8,128)(2,1)S(1)} collective-permute-done((bf16[2,128,128]{2,1,0:T(8,128)(2,1)S(1)}, bf16[2,128,128]{2,1,0:T(8,128)(2,1)S(1)}, u32[]{:S(2)}, u32[]{:S(2)}) %collective-permute-start.28) | collective-permute-done | bytes 65568 | tf_op jit(solution)/shard_map/ppermute | solution.py:27
  111.9 1.5 %collective-permute-done.29 = bf16[2,128,128]{2,1,0:T(8,128)(2,1)S(1)} collective-permute-done((bf16[2,128,128]{2,1,0:T(8,128)(2,1)S(1)}, bf16[2,128,128]{2,1,0:T(8,128)(2,1)S(1)}, u32[]{:S(2)}, u32[]{:S(2)}) %collective-permute-start.29) | collective-permute-done | bytes 65568 | tf_op jit(solution)/shard_map/ppermute | solution.py:27
  113.6 1.3 %collective-permute-done.30 = bf16[4,128,128]{2,1,0:T(8,128)(2,1)S(1)} collective-permute-done((bf16[4,128,128]{2,1,0:T(8,128)(2,1)S(1)}, bf16[4,128,128]{2,1,0:T(8,128)(2,1)S(1)}, u32[]{:S(2)}, u32[]{:S(2)}) %collective-permute-start.30) | collective-permute-done | bytes 131104 | tf_op jit(solution)/shard_map/ppermute | solution.py:22
  115.3 0.7 copy-done.2
  115.9 0.6 bitcast_dynamic-update-slice_fusion
  (53 shorter events, 1.1 us)
Async XLA Ops:
  0.0 18.5 %copy-start = (f32[3,3,1024]{2,1,0:T(4,128)S(1)}, f32[3,3,1024]{2,1,0:T(4,128)}, u32[]{:S(2)}) copy-start(f32[3,3,1024]{2,1,0:T(4,128)} %param.8) | copy-start | bytes 110596
  0.0 18.5 %collective-permute-start.6 = (bf16[3,1024,1024]{2,1,0:T(8,128)(2,1)}, bf16[3,1024,1024]{2,1,0:T(8,128)(2,1)}, u32[]{:S(2)}, u32[]{:S(2)}) collective-permute-start(bf16[3,1024,1024]{2,1,0:T(8,128)(2,1)} %bitcast.67), channel_id=1, source_target_pairs={{0,4},{4,0},{8,12},{12,8},{16,20},{20,16},{24,28},{28,24},{1,5},{5... | collective-permute-start | bytes 18874376 | tf_op jit(solution)/shard_map/ppermute | solution.py:22
  1.5 7.8 %collective-permute-start = (bf16[32,2048]{1,0:T(8,128)(2,1)S(1)}, bf16[32,2048]{1,0:T(8,128)(2,1)S(1)}, u32[]{:S(2)}, u32[]{:S(2)}) collective-permute-start(bf16[32,2048]{1,0:T(8,128)(2,1)S(1)} %get-tuple-element.79), channel_id=1, source_target_pairs={{0,3},{1,2},{2,1},{3,0},{4,7},{5,6},{6,5},{7,4},{8,11},{9,10},{10,... | collective-permute-start | bytes 393224 | tf_op jit(solution)/shard_map/ppermute | solution.py:31
  5.1 6.9 %collective-permute-start.1 = (bf16[32,2048]{1,0:T(8,128)(2,1)S(1)}, bf16[32,2048]{1,0:T(8,128)(2,1)S(1)}, u32[]{:S(2)}, u32[]{:S(2)}) collective-permute-start(bf16[32,2048]{1,0:T(8,128)(2,1)S(1)} %get-tuple-element.78), channel_id=1, source_target_pairs={{0,2},{1,3},{2,0},{3,1},{4,6},{5,7},{6,4},{7,5},{8,10},{9,11},{10,... | collective-permute-start | bytes 393224 | tf_op jit(solution)/shard_map/ppermute | solution.py:31
  5.6 6.7 %collective-permute-start.2 = (bf16[32,2048]{1,0:T(8,128)(2,1)S(1)}, bf16[32,2048]{1,0:T(8,128)(2,1)S(1)}, u32[]{:S(2)}, u32[]{:S(2)}) collective-permute-start(bf16[32,2048]{1,0:T(8,128)(2,1)S(1)} %get-tuple-element.77), channel_id=1, source_target_pairs={{0,1},{1,0},{2,3},{3,2},{4,5},{5,4},{6,7},{7,6},{8,9},{9,8},{10,11... | collective-permute-start | bytes 393224 | tf_op jit(solution)/shard_map/ppermute | solution.py:31
  13.3 11.4 %collective-permute-start.3 = (bf16[32,2048]{1,0:T(8,128)(2,1)S(1)}, bf16[32,2048]{1,0:T(8,128)(2,1)S(1)}, u32[]{:S(2)}, u32[]{:S(2)}) collective-permute-start(bf16[32,2048]{1,0:T(8,128)(2,1)S(1)} %get-tuple-element.67), channel_id=1, source_target_pairs={{0,8},{4,12},{8,0},{12,4},{16,24},{20,28},{24,16},{28,20},{1,9},{5... | collective-permute-start | bytes 393224 | tf_op jit(solution)/shard_map/ppermute | solution.py:27
  14.9 12.9 %collective-permute-start.4 = (bf16[32,2048]{1,0:T(8,128)(2,1)S(1)}, bf16[32,2048]{1,0:T(8,128)(2,1)S(1)}, u32[]{:S(2)}, u32[]{:S(2)}) collective-permute-start(bf16[32,2048]{1,0:T(8,128)(2,1)S(1)} %get-tuple-element.66), channel_id=1, source_target_pairs={{0,16},{4,20},{8,24},{12,28},{16,0},{20,4},{24,8},{28,12},{1,17},{... | collective-permute-start | bytes 393224 | tf_op jit(solution)/shard_map/ppermute | solution.py:27
  17.5 10.3 %collective-permute-start.5 = (bf16[32,2048]{1,0:T(8,128)(2,1)S(1)}, bf16[32,2048]{1,0:T(8,128)(2,1)S(1)}, u32[]{:S(2)}, u32[]{:S(2)}) collective-permute-start(bf16[32,2048]{1,0:T(8,128)(2,1)S(1)} %get-tuple-element.65), channel_id=1, source_target_pairs={{0,24},{4,28},{8,16},{12,20},{16,8},{20,12},{24,0},{28,4},{1,25},{... | collective-permute-start | bytes 393224 | tf_op jit(solution)/shard_map/ppermute | solution.py:27
  18.5 2.8 %copy-start.1 = (bf16[1024,3,1024]{2,0,1:T(8,128)(2,1)S(1)}, bf16[1024,3,1024]{2,0,1:T(8,128)(2,1)}, u32[]{:S(2)}) copy-start(bf16[1024,3,1024]{2,0,1:T(8,128)(2,1)} %param.7) | copy-start | bytes 18874372
  27.9 6.4 %collective-permute-start.9 = (bf16[64,2048]{1,0:T(8,128)(2,1)S(1)}, bf16[64,2048]{1,0:T(8,128)(2,1)S(1)}, u32[]{:S(2)}, u32[]{:S(2)}) collective-permute-start(bf16[64,2048]{1,0:T(8,128)(2,1)S(1)} %pad_maximum_fusion.4.refs_0_), channel_id=1, source_target_pairs={{0,1},{1,0},{2,3},{3,2},{4,5},{5,4},{6,7},{7,6},{8,9},{9,8},{10,11... | collective-permute-start | bytes 786440 | tf_op jit(solution)/shard_map/ppermute | solution.py:31
  29.5 8.9 %collective-permute-start.10 = (bf16[64,2048]{1,0:T(8,128)(2,1)S(1)}, bf16[64,2048]{1,0:T(8,128)(2,1)S(1)}, u32[]{:S(2)}, u32[]{:S(2)}) collective-permute-start(bf16[64,2048]{1,0:T(8,128)(2,1)S(1)} %pad_maximum_fusion.5.refs_1_), channel_id=1, source_target_pairs={{0,2},{1,3},{2,0},{3,1},{4,6},{5,7},{6,4},{7,5},{8,10},{9,11},{10,... | collective-permute-start | bytes 786440 | tf_op jit(solution)/shard_map/ppermute | solution.py:31
  30.0 8.6 %collective-permute-start.8 = (bf16[64,2048]{1,0:T(8,128)(2,1)S(1)}, bf16[64,2048]{1,0:T(8,128)(2,1)S(1)}, u32[]{:S(2)}, u32[]{:S(2)}) collective-permute-start(bf16[64,2048]{1,0:T(8,128)(2,1)S(1)} %pad_maximum_fusion.5.refs_1_), channel_id=1, source_target_pairs={{0,4},{4,0},{8,12},{12,8},{16,20},{20,16},{24,28},{28,24},{1,5},{5... | collective-permute-start | bytes 786440 | tf_op jit(solution)/shard_map/ppermute | solution.py:22
  30.0 8.6 %collective-permute-start.7 = (bf16[64,2048]{1,0:T(8,128)(2,1)S(1)}, bf16[64,2048]{1,0:T(8,128)(2,1)S(1)}, u32[]{:S(2)}, u32[]{:S(2)}) collective-permute-start(bf16[64,2048]{1,0:T(8,128)(2,1)S(1)} %pad_maximum_fusion.4.refs_0_), channel_id=1, source_target_pairs={{0,4},{4,0},{8,12},{12,8},{16,20},{20,16},{24,28},{28,24},{1,5},{5... | collective-permute-start | bytes 786440 | tf_op jit(solution)/shard_map/ppermute | solution.py:22
  34.4 13.1 %collective-permute-start.19 = (bf16[128,2048]{1,0:T(8,128)(2,1)S(1)}, bf16[128,2048]{1,0:T(8,128)(2,1)S(1)}, u32[]{:S(2)}, u32[]{:S(2)}) collective-permute-start(bf16[128,2048]{1,0:T(8,128)(2,1)S(1)} %pad_maximum_fusion.1), channel_id=1, source_target_pairs={{0,2},{1,3},{2,0},{3,1},{4,6},{5,7},{6,4},{7,5},{8,10},{9,11},{10,... | collective-permute-start | bytes 1572872 | tf_op jit(solution)/shard_map/ppermute | solution.py:31
  38.5 9.2 %collective-permute-start.18 = (bf16[128,2048]{1,0:T(8,128)(2,1)S(1)}, bf16[128,2048]{1,0:T(8,128)(2,1)S(1)}, u32[]{:S(2)}, u32[]{:S(2)}) collective-permute-start(bf16[128,2048]{1,0:T(8,128)(2,1)S(1)} %pad_maximum_fusion), channel_id=1, source_target_pairs={{0,1},{1,0},{2,3},{3,2},{4,5},{5,4},{6,7},{7,6},{8,9},{9,8},{10,11... | collective-permute-start | bytes 1572872 | tf_op jit(solution)/shard_map/ppermute | solution.py:31
  41.5 3.2 %collective-permute-start.11 = (bf16[64,2048]{1,0:T(8,128)(2,1)S(1)}, bf16[64,2048]{1,0:T(8,128)(2,1)S(1)}, u32[]{:S(2)}, u32[]{:S(2)}) collective-permute-start(bf16[64,2048]{1,0:T(8,128)(2,1)S(1)} %collective-permute-done.9.refs_0_), channel_id=1, source_target_pairs={{0,4},{4,0},{8,12},{12,8},{16,20},{20,16},{24,28},{28,24},{1,5},{5... | collective-permute-start | bytes 786440 | tf_op jit(solution)/shard_map/ppermute | solution.py:22
  41.6 3.1 %collective-permute-start.12 = (bf16[64,2048]{1,0:T(8,128)(2,1)S(1)}, bf16[64,2048]{1,0:T(8,128)(2,1)S(1)}, u32[]{:S(2)}, u32[]{:S(2)}) collective-permute-start(bf16[64,2048]{1,0:T(8,128)(2,1)S(1)} %collective-permute-done.10.refs_1_), channel_id=1, source_target_pairs={{0,4},{4,0},{8,12},{12,8},{16,20},{20,16},{24,28},{28,24},{1,5},{5... | collective-permute-start | bytes 786440 | tf_op jit(solution)/shard_map/ppermute | solution.py:22
  42.0 11.3 %collective-permute-start.13 = (bf16[2,3,256,128]{3,2,1,0:T(8,128)(2,1)S(1)}, bf16[2,3,256,128]{3,2,1,0:T(8,128)(2,1)S(1)}, u32[]{:S(2)}, u32[]{:S(2)}) collective-permute-start(bf16[2,3,256,128]{3,2,1,0:T(8,128)(2,1)S(1)} %get-tuple-element.48), channel_id=1, source_target_pairs={{0,8},{4,12},{24,16},{28,20},{1,9},{5,13},{25,17},{29,21},{2,10},{... | collective-permute-start | bytes 1179656 | tf_op jit(solution)/shard_map/ppermute | solution.py:179
  47.7 5.7 %collective-permute-start.20 = (bf16[128,2048]{1,0:T(8,128)(2,1)S(1)}, bf16[128,2048]{1,0:T(8,128)(2,1)S(1)}, u32[]{:S(2)}, u32[]{:S(2)}) collective-permute-start(bf16[128,2048]{1,0:T(8,128)(2,1)S(1)} %collective-permute-done.18.refs_0_), channel_id=1, source_target_pairs={{0,4},{4,0},{8,12},{12,8},{16,20},{20,16},{24,28},{28,24},{1,5},{5... | collective-permute-start | bytes 1572872 | tf_op jit(solution)/shard_map/ppermute | solution.py:22
  47.8 5.7 %collective-permute-start.21 = (bf16[128,2048]{1,0:T(8,128)(2,1)S(1)}, bf16[128,2048]{1,0:T(8,128)(2,1)S(1)}, u32[]{:S(2)}, u32[]{:S(2)}) collective-permute-start(bf16[128,2048]{1,0:T(8,128)(2,1)S(1)} %collective-permute-done.19.refs_1_), channel_id=1, source_target_pairs={{0,4},{4,0},{8,12},{12,8},{16,20},{20,16},{24,28},{28,24},{1,5},{5... | collective-permute-start | bytes 1572872 | tf_op jit(solution)/shard_map/ppermute | solution.py:22
  48.3 14.2 %collective-permute-start.14 = (bf16[2,3,256,128]{3,2,1,0:T(8,128)(2,1)S(1)}, bf16[2,3,256,128]{3,2,1,0:T(8,128)(2,1)S(1)}, u32[]{:S(2)}, u32[]{:S(2)}) collective-permute-start(bf16[2,3,256,128]{3,2,1,0:T(8,128)(2,1)S(1)} %get-tuple-element.49), channel_id=1, source_target_pairs={{0,8},{4,12},{24,16},{28,20},{1,9},{5,13},{25,17},{29,21},{2,10},{... | collective-permute-start | bytes 1179656 | tf_op jit(solution)/shard_map/ppermute | solution.py:179
  58.0 14.1 %collective-permute-start.22 = (bf16[3,512,128]{2,1,0:T(8,128)(2,1)S(1)}, bf16[3,512,128]{2,1,0:T(8,128)(2,1)S(1)}, u32[]{:S(2)}, u32[]{:S(2)}) collective-permute-start(bf16[3,512,128]{2,1,0:T(8,128)(2,1)S(1)} %get-tuple-element.55), channel_id=1, source_target_pairs={{0,8},{4,12},{24,16},{28,20},{1,9},{5,13},{25,17},{29,21},{2,10},{... | collective-permute-start | bytes 1179656 | tf_op jit(solution)/shard_map/ppermute | solution.py:179
  62.6 10.3 %collective-permute-start.15 = (bf16[3,512,128]{2,1,0:T(8,128)(2,1)S(1)}, bf16[3,512,128]{2,1,0:T(8,128)(2,1)S(1)}, u32[]{:S(2)}, u32[]{:S(2)}) collective-permute-start(bf16[3,512,128]{2,1,0:T(8,128)(2,1)S(1)} %pad_maximum_fusion.2), channel_id=1, source_target_pairs={{8,16},{12,20},{16,8},{20,12},{9,17},{13,21},{17,9},{21,13},{10,18... | collective-permute-start | bytes 1179656 | tf_op jit(solution)/shard_map/ppermute | solution.py:179
  63.3 32.0 %collective-permute-start.17 = (bf16[3,512,128]{2,1,0:T(8,128)(2,1)S(1)}, bf16[3,512,128]{2,1,0:T(8,128)(2,1)S(1)}, u32[]{:S(2)}, u32[]{:S(2)}) collective-permute-start(bf16[3,512,128]{2,1,0:T(8,128)(2,1)S(1)} %pad_maximum_fusion.3), channel_id=1, source_target_pairs={{8,16},{12,20},{16,8},{20,12},{9,17},{13,21},{17,9},{21,13},{10,18... | collective-permute-start | bytes 1179656 | tf_op jit(solution)/shard_map/ppermute | solution.py:179
  64.0 17.6 %collective-permute-start.25 = (bf16[3,512,128]{2,1,0:T(8,128)(2,1)S(1)}, bf16[3,512,128]{2,1,0:T(8,128)(2,1)S(1)}, u32[]{:S(2)}, u32[]{:S(2)}) collective-permute-start(bf16[3,512,128]{2,1,0:T(8,128)(2,1)S(1)} %get-tuple-element.54), channel_id=1, source_target_pairs={{0,8},{4,12},{24,16},{28,20},{1,9},{5,13},{25,17},{29,21},{2,10},{... | collective-permute-start | bytes 1179656 | tf_op jit(solution)/shard_map/ppermute | solution.py:179
  72.2 10.2 %collective-permute-start.23 = (bf16[3,512,128]{2,1,0:T(8,128)(2,1)S(1)}, bf16[3,512,128]{2,1,0:T(8,128)(2,1)S(1)}, u32[]{:S(2)}, u32[]{:S(2)}) collective-permute-start(bf16[3,512,128]{2,1,0:T(8,128)(2,1)S(1)} %add_convert_fusion.3), channel_id=1, source_target_pairs={{8,16},{12,20},{16,8},{20,12},{9,17},{13,21},{17,9},{21,13},{10,18... | collective-permute-start | bytes 1179656 | tf_op jit(solution)/shard_map/ppermute | solution.py:179
  73.0 22.3 %collective-permute-start.16 = (bf16[3,512,128]{2,1,0:T(8,128)(2,1)S(1)}, bf16[3,512,128]{2,1,0:T(8,128)(2,1)S(1)}, u32[]{:S(2)}, u32[]{:S(2)}) collective-permute-start(bf16[3,512,128]{2,1,0:T(8,128)(2,1)S(1)} %add_convert_fusion.5), channel_id=1, source_target_pairs={{0,8},{4,12},{8,0},{12,4},{16,24},{20,28},{24,16},{28,20},{1,9},{5... | collective-permute-start | bytes 1179656 | tf_op jit(solution)/shard_map/ppermute | solution.py:179
  81.7 13.8 %collective-permute-start.26 = (bf16[3,512,128]{2,1,0:T(8,128)(2,1)S(1)}, bf16[3,512,128]{2,1,0:T(8,128)(2,1)S(1)}, u32[]{:S(2)}, u32[]{:S(2)}) collective-permute-start(bf16[3,512,128]{2,1,0:T(8,128)(2,1)S(1)} %add_convert_fusion.1), channel_id=1, source_target_pairs={{8,16},{12,20},{16,8},{20,12},{9,17},{13,21},{17,9},{21,13},{10,18... | collective-permute-start | bytes 1179656 | tf_op jit(solution)/shard_map/ppermute | solution.py:179
  82.5 18.7 %collective-permute-start.24 = (bf16[3,512,128]{2,1,0:T(8,128)(2,1)S(1)}, bf16[3,512,128]{2,1,0:T(8,128)(2,1)S(1)}, u32[]{:S(2)}, u32[]{:S(2)}) collective-permute-start(bf16[3,512,128]{2,1,0:T(8,128)(2,1)S(1)} %add_convert_fusion.2), channel_id=1, source_target_pairs={{0,8},{4,12},{8,0},{12,4},{16,24},{20,28},{24,16},{28,20},{1,9},{5... | collective-permute-start | bytes 1179656 | tf_op jit(solution)/shard_map/ppermute | solution.py:179
  104.2 4.7 %collective-permute-start.27 = (bf16[2,128,128]{2,1,0:T(8,128)(2,1)S(1)}, bf16[2,128,128]{2,1,0:T(8,128)(2,1)S(1)}, u32[]{:S(2)}, u32[]{:S(2)}) collective-permute-start(bf16[2,128,128]{2,1,0:T(8,128)(2,1)S(1)} %get-tuple-element.62), channel_id=1, source_target_pairs={{0,8},{4,12},{8,0},{12,4},{16,24},{20,28},{24,16},{28,20},{1,9},{5... | collective-permute-start | bytes 196616 | tf_op jit(solution)/shard_map/ppermute | solution.py:27
  106.1 5.9 %collective-permute-start.28 = (bf16[2,128,128]{2,1,0:T(8,128)(2,1)S(1)}, bf16[2,128,128]{2,1,0:T(8,128)(2,1)S(1)}, u32[]{:S(2)}, u32[]{:S(2)}) collective-permute-start(bf16[2,128,128]{2,1,0:T(8,128)(2,1)S(1)} %get-tuple-element.63), channel_id=1, source_target_pairs={{0,16},{4,20},{8,24},{12,28},{16,0},{20,4},{24,8},{28,12},{1,17},{... | collective-permute-start | bytes 196616 | tf_op jit(solution)/shard_map/ppermute | solution.py:27
  107.3 6.2 %collective-permute-start.29 = (bf16[2,128,128]{2,1,0:T(8,128)(2,1)S(1)}, bf16[2,128,128]{2,1,0:T(8,128)(2,1)S(1)}, u32[]{:S(2)}, u32[]{:S(2)}) collective-permute-start(bf16[2,128,128]{2,1,0:T(8,128)(2,1)S(1)} %get-tuple-element.64), channel_id=1, source_target_pairs={{0,24},{4,28},{8,16},{12,20},{16,8},{20,12},{24,0},{28,4},{1,25},{... | collective-permute-start | bytes 196616 | tf_op jit(solution)/shard_map/ppermute | solution.py:27
  113.6 1.4 %collective-permute-start.30 = (bf16[4,128,128]{2,1,0:T(8,128)(2,1)S(1)}, bf16[4,128,128]{2,1,0:T(8,128)(2,1)S(1)}, u32[]{:S(2)}, u32[]{:S(2)}) collective-permute-start(bf16[4,128,128]{2,1,0:T(8,128)(2,1)S(1)} %dynamic-slice_bitcast_fusion), channel_id=1, source_target_pairs={{0,4},{4,0},{8,12},{12,8},{16,20},{20,16},{24,28},{28,24},{1,5},{5... | collective-permute-start | bytes 393224 | tf_op jit(solution)/shard_map/ppermute | solution.py:22
  115.2 0.7 copy-start.2

commit v4 on v3

--- a/solution.py
+++ b/solution.py
@@ -190,8 +190,24 @@
         if t not in self.odd:
             self.odd[t] = self.send(t, t + 1, self.even[t - 1], 1)
 
-    def total(self):
-        return add_parts(self.blocks[0], self.even[self.last - 1], self.odd[self.last - 1])
+
+def finish(streams, cuts):
+    last = streams[0].last
+    t = last - 1
+    for stream in streams:
+        stream.send_even(t)
+    odd = [add_parts(stream.blocks[t + 1], stream.even[t - 1]) for stream in streams]
+    whole = lambda value: jnp.concatenate(value, axis=1) if len(value) > 1 else value[0]
+    near = [(whole(stream.blocks[0]), whole(stream.even[t])) for stream in streams]
+    terms = []
+    for cut in cuts:
+        came = streams[0].exchange(t, jnp.concatenate([block[cut] for block in odd], axis=1), 1)
+        row, of_cut = 0, []
+        for block, even in near:
+            of_cut.append([(block, cut.start, 0), (even, cut.start, 0), (came, 0, row)])
+            row += block.shape[1]
+        terms.append(of_cut)
+    return terms
 
 
 def add_parts(*values):
@@ -226,23 +242,45 @@
     return high, (value - high.astype(F32)).astype(BF16)
 
 
-def mix_kernel(order, parts, planes, n_ch, where_ref, *refs):
-    data, (taps, skip, near, collect, emit), refs = refs[:parts], refs[parts : parts + 5], refs[parts + 5 :]
-    outs, (proj, long_in, done) = refs[:planes], refs[planes:]
-    core, me, z = where_ref[0], where_ref[1], where_ref[2]
+def unpack(data):
+    arrays, places = [], []
+    for terms in data:
+        places.append([])
+        for array, plane, row in terms:
+            at = next((i for i, known in enumerate(arrays) if known is array), len(arrays))
+            arrays += [array] if at == len(arrays) else []
+            places[-1].append((at, plane, row))
+    return arrays, places
+
+
+def place(order, data, refs, count, proj, where_ref, planes, n_ch):
+    core, me = where_ref[0], where_ref[1]
+    proj[:, 0:8] = jnp.zeros((count, 8, proj.shape[2]), F32)
+    rows = CHUNK // n_ch
+    for pieces, terms in zip(order, data, strict=True):
+        start = 0
+        for side, s, k0 in pieces:
+            owner = core if side == 0 else 1 - core
+            for k in range(k0, k0 + planes // 2):
+                at = pl.multiple_of((2 * k + owner) * CHUNK + (me ^ s) * rows + 8, 8)
+                for j in range(count):
+                    total = add(*(refs[i][plane + j, row + start : row + start + rows] for i, plane, row in terms))
+                    proj[j, pl.ds(at, rows)] = total.astype(F32)
+                start += rows
+
+
+def short_mix(taps, j, proj, at, n):
+    total = 0.0
+    for lag in range(3):
+        total += taps[lag, j : j + 1] * proj[at, 8 - lag + n * CHUNK : 8 - lag + (n + 1) * CHUNK]
+    return total
+
+
+def convolve_kernel(order, data, count, planes, n_ch, where_ref, *refs):
+    taps, skip, near, collect, emit, done, proj, long_in = refs[count:]
     lanes = skip.shape[1]
     groups = near.shape[0]
-    proj[:, 0:8] = jnp.zeros((3, 8, lanes), F32)
-    rows = CHUNK // n_ch
-    for pieces, ref in zip(order, data, strict=True):
-        start = 0
-        for side, s, first in pieces:
-            owner = core if side == 0 else 1 - core
-            for k in range(first, first + planes // 2):
-                at = (2 * k + owner) * CHUNK + (me ^ s) * rows + 8
-                for j in range(3):
-                    proj[j, pl.ds(pl.multiple_of(at, 8), rows)] = ref[j, start : start + rows].astype(F32)
-                start += rows
+    place(order, data, refs, 2, proj, where_ref, planes, n_ch)
 
     lane_group = lax.broadcasted_iota(jnp.int32, (1, lanes), 1) // GROUP
     pole_group = lax.broadcasted_iota(jnp.int32, (collect.shape[0], lanes), 0) // (collect.shape[0] // groups)
@@ -254,13 +292,7 @@
     state = jnp.zeros(same.shape, F32)
     chunks = 2 * planes
     for n in range(chunks):
-        mixed = []
-        for j in range(3):
-            total = 0.0
-            for lag in range(3):
-                total += taps[lag, j : j + 1] * proj[j, 8 - lag + n * CHUNK : 8 - lag + (n + 1) * CHUNK]
-            mixed.append(total)
-        gated = (mixed[1] * mixed[2]).astype(BF16)
+        gated = (short_mix(taps, 1, proj, 0, n) * short_mix(taps, 2, proj, 1, n)).astype(BF16)
         gated2 = jnp.concatenate([gated, gated], axis=0)
         long_out = skip[...] * gated.astype(F32)
         if n:
@@ -273,7 +305,6 @@
             state = keep * state + jnp.where(same, fresh, 0.0)
         long_in[n // 2, n % 2] = gated2
         done[n * CHUNK : (n + 1) * CHUNK] = long_out
-        proj[0, 8 + n * CHUNK - 8 : n * CHUNK + CHUNK] = mixed[0]
     for g in range(groups):
         near2 = jnp.concatenate(halves_of(near[g]), axis=1)
         mine = lane_group == g
@@ -283,55 +314,93 @@
             for c in range(2):
                 at = slice((2 * k + c) * CHUNK, (2 * k + c + 1) * CHUNK)
                 done[at] += jnp.where(mine, both[:, c * lanes : (c + 1) * lanes], 0.0)
-    for u in range(planes):
-        at = pl.multiple_of((z ^ u) * 2 * CHUNK, CHUNK)
-        both = proj[0, pl.ds(at, 2 * CHUNK)] * done[pl.ds(at, 2 * CHUNK)]
-        outs[u][...] = both.astype(BF16).reshape(2, CHUNK, lanes)
-
-
-def mix(data, order, taps, skip, filters, core, me, z, planes, n_ch):
+
+
+def convolve(data, order, taps, skip, filters, where, planes, n_ch):
     lanes = skip.shape[1]
+    length = 2 * planes * CHUNK
     if lanes % 128:
-        return mix_plainly(data, order, taps, skip, filters, core, me, z, planes, n_ch)
-    poles = filters[1].shape[0]
-    length = 2 * planes * CHUNK
+        mixed = mix_plainly(data, order, 2, taps[:, 1:], where, planes, n_ch)
+        return convolve_plainly(mixed, skip, filters)
     vmem = pl.BlockSpec(memory_space=pltpu.VMEM)
+    arrays, data = unpack(data)
     return pl.pallas_call(
-        lambda *refs: mix_kernel(order, len(data), planes, n_ch, *refs),
-        in_specs=[pl.BlockSpec(memory_space=pltpu.SMEM)] + [vmem] * (len(data) + 5),
-        out_specs=[vmem] * planes,
-        out_shape=[jax.ShapeDtypeStruct((2, CHUNK, lanes), BF16)] * planes,
+        lambda *refs: convolve_kernel(order, data, len(arrays), planes, n_ch, *refs),
+        in_specs=[pl.BlockSpec(memory_space=pltpu.SMEM)] + [vmem] * (len(arrays) + 5),
+        out_specs=vmem,
+        out_shape=jax.ShapeDtypeStruct((length, lanes), F32),
         scratch_shapes=[
-            pltpu.VMEM((3, length + 8, lanes), F32),
+            pltpu.VMEM((2, length + 8, lanes), F32),
             pltpu.VMEM((planes, 2, 2 * CHUNK, lanes), BF16),
-            pltpu.VMEM((length, lanes), F32),
         ],
         compiler_params=pltpu.CompilerParams(vmem_limit_bytes=8 << 20),
         cost_estimate=pl.CostEstimate(flops=0, bytes_accessed=0, transcendentals=0),
-        name="mix",
-    )(
-        jnp.stack([core, me, z]).astype(jnp.int32), *data, taps, skip, *filters
-    )
-
-
-def mix_plainly(data, order, taps, skip, filters, core, me, z, planes, n_ch):
-    lanes = skip.shape[1]
-    near, collect, emit = filters
-    keep = collect[:, 0] * collect[:, CHUNK - 2]
-    groups, rows = near.shape[0], CHUNK // n_ch
+        name="convolve",
+    )(where, *arrays, taps, skip, *filters)
+
+
+def gate_kernel(order, data, count, planes, n_ch, where_ref, *refs):
+    taps, long_out = refs[count : count + 2]
+    outs, (proj, done) = refs[count + 2 : -2], refs[-2:]
+    z = where_ref[2]
+    place(order, data, refs, 1, proj, where_ref, planes, n_ch)
+    for n in range(2 * planes):
+        at = slice(n * CHUNK, (n + 1) * CHUNK)
+        done[at] = (short_mix(taps, 0, proj, 0, n) * long_out[at]).astype(BF16)
+    for u in range(planes):
+        at = pl.multiple_of((z ^ u) * 2 * CHUNK, CHUNK)
+        outs[u][...] = done[pl.ds(at, 2 * CHUNK)].reshape(outs[u].shape)
+
+
+def gate(data, order, taps, long_out, where, planes, n_ch):
+    length, lanes = long_out.shape
+    if lanes % 128:
+        mixed = mix_plainly(data, order, 1, taps[:, :1], where, planes, n_ch)
+        out = (mixed[0] * long_out).astype(BF16).reshape(planes, 2, CHUNK, lanes)
+        return [lax.dynamic_index_in_dim(out, where[2] ^ u, 0, keepdims=False) for u in range(planes)]
+    vmem = pl.BlockSpec(memory_space=pltpu.VMEM)
+    arrays, data = unpack(data)
+    return pl.pallas_call(
+        lambda *refs: gate_kernel(order, data, len(arrays), planes, n_ch, *refs),
+        in_specs=[pl.BlockSpec(memory_space=pltpu.SMEM)] + [vmem] * (len(arrays) + 2),
+        out_specs=[vmem] * planes,
+        out_shape=[jax.ShapeDtypeStruct((2, CHUNK, lanes), BF16)] * planes,
+        scratch_shapes=[pltpu.VMEM((1, length + 8, lanes), F32), pltpu.VMEM((length, lanes), BF16)],
+        compiler_params=pltpu.CompilerParams(vmem_limit_bytes=8 << 20),
+        cost_estimate=pl.CostEstimate(flops=0, bytes_accessed=0, transcendentals=0),
+        name="gate",
+    )(where, *arrays, taps, long_out)
+
+
+def mix_plainly(data, order, count, taps, where, planes, n_ch):
+    core, me = where[0], where[1]
+    lanes = taps.shape[2]
+    length = [terms[0][0].shape[1] for terms in data]
+    data = [
+        add(*(array[plane : plane + count, row : row + rows] for array, plane, row in terms))
+        for terms, rows in zip(data, length, strict=True)
+    ]
+    rows = CHUNK // n_ch
     sides = [[[None, None] for _ in range(n_ch)] for _ in range(2)]
     for pieces, block in zip(order, data, strict=True):
-        cut = block.reshape(3, len(pieces), planes // 2, rows, lanes)
+        cut = block.reshape(count, len(pieces), planes // 2, rows, lanes)
         for i, (side, s, first) in enumerate(pieces):
             sides[side][s][first > 0] = cut[:, i]
     sides = [[jnp.concatenate(halves, axis=1) for halves in side] for side in sides]
     sides = [jnp.stack([pick(side, me ^ p) for p in range(n_ch)], axis=2) for side in sides]
     both = jnp.stack([pick(sides, core), pick(sides, 1 - core)], axis=2)
-    proj = both.reshape(3, -1, lanes).astype(F32)
+    proj = both.reshape(count, -1, lanes).astype(F32)
     length = proj.shape[1]
     padded = jnp.pad(proj, ((0, 0), (2, 0), (0, 0)))
-    mixed = sum(taps[lag][:, None] * padded[:, 2 - lag : 2 - lag + length] for lag in range(3))
-    gated = lax.optimization_barrier((mixed[1] * mixed[2]).astype(BF16)).astype(F32)
+    return sum(taps[lag][:, None] * padded[:, 2 - lag : 2 - lag + length] for lag in range(3))
+
+
+def convolve_plainly(mixed, skip, filters):
+    near, collect, emit = filters
+    keep = collect[:, 0] * collect[:, CHUNK - 2]
+    groups = near.shape[0]
+    length, lanes = mixed.shape[1:]
+    gated = lax.optimization_barrier((mixed[0] * mixed[1]).astype(BF16)).astype(F32)
     chunks = length // CHUNK
     columns = gated.reshape(chunks, CHUNK, groups, GROUP)
     high = lax.Precision.HIGHEST
@@ -342,9 +411,35 @@
         states.append(state)
         state = keep.reshape(groups, -1, 1) * state + fresh[n]
     out += jnp.einsum("igr,ngrc->nigc", emit.reshape(CHUNK, groups, -1), jnp.stack(states), precision=high)
-    out = (mixed[0] * (out.reshape(length, lanes) + skip * gated)).astype(BF16)
-    out = out.reshape(planes, 2, CHUNK, lanes)
-    return [lax.dynamic_index_in_dim(out, z ^ u, 0, keepdims=False) for u in range(planes)]
+    return out.reshape(length, lanes) + skip * gated
+
+
+def collect_kernel(planes, where_ref, *refs):
+    blocks, (given, out_ref) = refs[:planes], refs[planes:]
+    core, z = where_ref[0], where_ref[1]
+    lanes = given.shape[2]
+    for u in range(planes):
+        for owner, block in ((core, blocks[u][core]), (1 - core, given[u])):
+            at = pl.multiple_of((owner * planes + (z ^ u)) * lanes, lanes)
+            out_ref[:, pl.ds(at, lanes)] = block
+
+
+def collect_columns(blocks, given, core, z, planes):
+    tokens, lanes = given.shape[1:]
+    if lanes % 128:
+        keep = [lax.dynamic_index_in_dim(block, core, 0, keepdims=False) for block in blocks]
+        pairs = [[jnp.where(core == c, keep[u], given[u]) for u in range(planes)] for c in range(2)]
+        return jnp.concatenate([pick(pairs[c], z ^ k) for c in range(2) for k in range(planes)], axis=1)
+    vmem = pl.BlockSpec(memory_space=pltpu.VMEM)
+    return pl.pallas_call(
+        lambda *refs: collect_kernel(planes, *refs),
+        in_specs=[pl.BlockSpec(memory_space=pltpu.SMEM)] + [vmem] * (planes + 1),
+        out_specs=vmem,
+        out_shape=jax.ShapeDtypeStruct((tokens, 2 * planes * lanes), BF16),
+        compiler_params=pltpu.CompilerParams(vmem_limit_bytes=8 << 20),
+        cost_estimate=pl.CostEstimate(flops=0, bytes_accessed=0, transcendentals=0),
+        name="collect_columns",
+    )(jnp.stack([core, z]).astype(jnp.int32), *blocks, given)
 
 
 def local(tokens, w_in, short_filter, decay_rate, residue, skip):
@@ -395,30 +490,17 @@
     rest = tie(blocks[0], rest)
     halves = [(1, 1), (3, 1), (2, 0), (3, 0)] + [(s, h) for s in range(4, n_ch) for h in range(2)]
     b.take(project_pieces(1, rest, halves, False))
-    for t in range(planes - 1):
+    for t in range(planes - 2):
         for stream in (a, b):
             stream.send_even(t)
             stream.send_odd(t)
-    data = [stream.total() for stream in (a, b)]
-    outs = mix(
-        data,
-        order,
-        taps,
-        direct,
-        filters,
-        core,
-        me,
-        z,
-        planes,
-        n_ch,
-    )
+    pair, query = finish([a, b], [slice(1, 3), slice(0, 1)])
+    where = jnp.stack([core, me, z]).astype(jnp.int32)
+    long_out = convolve(pair, order, taps, direct, filters, where, planes, n_ch)
+    outs = gate(query, order, taps, long_out, where, planes, n_ch)
     came = [to_plane(block, u, planes) if u else block for u, block in enumerate(outs)]
-    came = jnp.stack(came)
-    keep = lax.dynamic_index_in_dim(came, core, 1, keepdims=False)
-    given = swap_cores(lax.dynamic_index_in_dim(came, 1 - core, 1, keepdims=False), n_ctx)
-    sides = [jnp.where(core == 0, keep, given), jnp.where(core == 0, given, keep)]
-    columns = [pick([sides[c][u] for u in range(planes)], z ^ k) for c in range(2) for k in range(planes)]
-    return jnp.concatenate(columns, axis=1)
+    given = jnp.stack([lax.dynamic_index_in_dim(block, 1 - core, 0, keepdims=False) for block in came])
+    return collect_columns(came, swap_cores(given, n_ctx), core, z, planes)
 
 
 def solution(mesh):

time: 117 us -> 114 us (0.974)
  starting transfers between devices: 59.4 us -> 54.1 us
  Pallas kernels: 16.5 us -> 18.6 us
    ppermute x10, starting transfers between devices: 40.5 us -> 32.8 us  [exchange(): return lax.ppermute(block, 'ctx', route) if route else None]
    ppermute x6, starting transfers between devices: 8.9 us -> 11.4 us  [to_plane(): return lax.ppermute(block, 'ctx', route)]
    pallas_call x1 -> x3, Pallas kernels: 2.83 us -> 4.93 us  [the longest x1 2.83 us: convolve(): pl.pallas_call(lambda *refs: convolve_kernel(order, data, len(arrays), pl...]
    unnamed x8 -> x7, local copies, waits for them, and re-layouts: 3.62 us -> 2.94 us
  transfers between devices with their start and end apart: 31 -> 31, of which waited for: 13 -> 13; matrix products, arithmetic and copies ran while one was open for 6% -> 9% of each run, Pallas kernels for 12% -> 15%
where the time goes in v4:
time: 114 us; the launch traced here: 113 us
  starting transfers between devices  54.1 us (47%)
  waiting for transfers between devices  27.4 us (24%)
  Pallas kernels  18.6 us (16%)
  other arithmetic  6.72 us (6%)
  local copies, waits for them, and re-layouts  5.78 us (5%)
    ppermute x10, starting transfers between devices, exchange(): return lax.ppermute(block, 'ctx', route) if route else None  32.8 us
    ppermute x6, starting transfers between devices, to_plane(): return lax.ppermute(block, 'ctx', route)  11.4 us
    pallas_call x3, Pallas kernels, project(): pl.pallas_call(lambda *refs: project_kernel(planes, len(xs), merged, *ref...  10.3 us
    ppermute x7, waiting for transfers between devices, to_column(): return lax.ppermute(block, 'ch', [(j, j ^ distance) for j in range(n_ch)])  9.52 us
    ppermute x10, waiting for transfers between devices, exchange(): return lax.ppermute(block, 'ctx', route) if route else None  9.13 us
    ppermute x7, starting transfers between devices, to_column(): return lax.ppermute(block, 'ch', [(j, j ^ distance) for j in range(n_ch)])  7.88 us
    ppermute x6, waiting for transfers between devices, to_plane(): return lax.ppermute(block, 'ctx', route)  7.46 us
    pallas_call x1, Pallas kernels, stage(): pl.pallas_call(lambda *refs: stage_kernel(planes, *refs), in_specs=[pl.Bl...  3.39 us
  transfers between devices with their start and end apart: 31, of which 13 were waited for; matrix products, arithmetic and copies ran while one was open for 9% of the time, Pallas kernels for 15%

profile of v4, /device:TPU:0, one launch (start us, length us, event | category | flops | bytes accessed | tf_op | source)
XLA Modules:
  0.0 113.1 jit_solution(13463717034335572765)
XLA Ops:
  0.0 0.5 collective-permute-start.6
  0.5 1.1 dynamic-slice_bitcast_fusion
  1.5 3.5 %collective-permute-start = (bf16[32,2048]{1,0:T(8,128)(2,1)S(1)}, bf16[32,2048]{1,0:T(8,128)(2,1)S(1)}, u32[]{:S(2)}, u32[]{:S(2)}) collective-permute-start(bf16[32,2048]{1,0:T(8,128)(2,1)S(1)} %get-tuple-element.79), channel_id=1, source_target_pairs={{0,3},{1,2},{2,1},{3,0},{4,7},{5,6},{6,5},{7,4},{8,11},{9,10},{10,... | collective-permute-start | bytes 393224 | tf_op jit(solution)/shard_map/ppermute | solution.py:31
  5.1 0.5 collective-permute-start.1
  5.6 0.1 collective-permute-start.2
  5.7 0.8 constant_dynamic-slice_fusion.5
  6.6 0.1 mul.90
  6.7 0.1 neg.20
  6.9 2.2 %multiply_reduce_fusion = f32[8,128,128]{2,1,0:T(8,128)S(1)} fusion(f32[128,128]{1,0:T(8,128)S(1)} %maximum_convert_fusion, f32[8,16]{1,0:T(8,128)S(1)} %get-tuple-element.81, f32[8,16]{1,0:T(8,128)S(1)} %get-tuple-element.80), kind=kLoop, calls=%fused_computation | loop fusion | flops 6160384 | bytes 590848 | tf_op jit(solution)/shard_map/reduce_sum | solution.py:229
  9.1 0.1 exponential_multiply_fusion
  9.3 2.7 %collective-permute-done.1 = bf16[32,2048]{1,0:T(8,128)(2,1)S(1)} collective-permute-done((bf16[32,2048]{1,0:T(8,128)(2,1)S(1)}, bf16[32,2048]{1,0:T(8,128)(2,1)S(1)}, u32[]{:S(2)}, u32[]{:S(2)}) %collective-permute-start.1) | collective-permute-done | bytes 131104 | tf_op jit(solution)/shard_map/ppermute | solution.py:31
  12.0 0.3 collective-permute-done.2
  12.3 1.0 fusion.13
  13.3 1.6 %collective-permute-start.3 = (bf16[32,2048]{1,0:T(8,128)(2,1)S(1)}, bf16[32,2048]{1,0:T(8,128)(2,1)S(1)}, u32[]{:S(2)}, u32[]{:S(2)}) collective-permute-start(bf16[32,2048]{1,0:T(8,128)(2,1)S(1)} %get-tuple-element.67), channel_id=1, source_target_pairs={{0,8},{4,12},{8,0},{12,4},{16,24},{20,28},{24,16},{28,20},{1,9},{5... | collective-permute-start | bytes 393224 | tf_op jit(solution)/shard_map/ppermute | solution.py:27
  14.9 2.6 %collective-permute-start.4 = (bf16[32,2048]{1,0:T(8,128)(2,1)S(1)}, bf16[32,2048]{1,0:T(8,128)(2,1)S(1)}, u32[]{:S(2)}, u32[]{:S(2)}) collective-permute-start(bf16[32,2048]{1,0:T(8,128)(2,1)S(1)} %get-tuple-element.66), channel_id=1, source_target_pairs={{0,16},{4,20},{8,24},{12,28},{16,0},{20,4},{24,8},{28,12},{1,17},{... | collective-permute-start | bytes 393224 | tf_op jit(solution)/shard_map/ppermute | solution.py:27
  17.5 0.2 collective-permute-start.5
  17.7 0.8 dynamic-slice_bitcast_fusion.3.refs_7_
  18.5 2.8 %copy-done.1 = bf16[1024,3,1024]{2,0,1:T(8,128)(2,1)S(1)} copy-done((bf16[1024,3,1024]{2,0,1:T(8,128)(2,1)S(1)}, bf16[1024,3,1024]{2,0,1:T(8,128)(2,1)}, u32[]{:S(2)}) %copy-start.1) | copy-done | bytes 6291480
  21.3 3.4 %stage.1.refs_4_ = bf16[3,2048,512]{2,1,0:T(8,128)(2,1)S(1)} custom-call(s32[2]{0:T(128)S(1)} %pad_add_fusion.2.refs_0_, bf16[3,1024,1024]{2,1,0:T(8,128)(2,1)S(1)} %bitcast.43, bf16[3,1024,1024]{2,1,0:T(8,128)(2,1)} %collective-permute-done.6.refs_2_), custom_call_target="tpu_custom_call" | custom-call | tf_op jit(solution)/shard_map/stage/pallas_call | solution.py:88
  24.7 3.1 %collective-permute-done.4 = bf16[32,2048]{1,0:T(8,128)(2,1)S(1)} collective-permute-done((bf16[32,2048]{1,0:T(8,128)(2,1)S(1)}, bf16[32,2048]{1,0:T(8,128)(2,1)S(1)}, u32[]{:S(2)}, u32[]{:S(2)}) %collective-permute-start.4) | collective-permute-done | bytes 131104 | tf_op jit(solution)/shard_map/ppermute | solution.py:27
  27.9 1.6 %collective-permute-start.9 = (bf16[64,2048]{1,0:T(8,128)(2,1)S(1)}, bf16[64,2048]{1,0:T(8,128)(2,1)S(1)}, u32[]{:S(2)}, u32[]{:S(2)}) collective-permute-start(bf16[64,2048]{1,0:T(8,128)(2,1)S(1)} %pad_maximum_fusion.5.refs_0_), channel_id=1, source_target_pairs={{0,1},{1,0},{2,3},{3,2},{4,5},{5,4},{6,7},{7,6},{8,9},{9,8},{10,11... | collective-permute-start | bytes 786440 | tf_op jit(solution)/shard_map/ppermute | solution.py:31
  29.5 0.4 collective-permute-start.10
  30.0 0.5 collective-permute-start.7
  30.5 3.9 %collective-permute-done.9.refs_0_ = bf16[64,2048]{1,0:T(8,128)(2,1)S(1)} collective-permute-done((bf16[64,2048]{1,0:T(8,128)(2,1)S(1)}, bf16[64,2048]{1,0:T(8,128)(2,1)S(1)}, u32[]{:S(2)}, u32[]{:S(2)}) %collective-permute-start.9) | collective-permute-done | bytes 262176 | tf_op jit(solution)/shard_map/ppermute | solution.py:31
  34.4 1.6 %collective-permute-start.18 = (bf16[128,2048]{1,0:T(8,128)(2,1)S(1)}, bf16[128,2048]{1,0:T(8,128)(2,1)S(1)}, u32[]{:S(2)}, u32[]{:S(2)}) collective-permute-start(bf16[128,2048]{1,0:T(8,128)(2,1)S(1)} %pad_maximum_fusion.2), channel_id=1, source_target_pairs={{0,2},{1,3},{2,0},{3,1},{4,6},{5,7},{6,4},{7,5},{8,10},{9,11},{10,... | collective-permute-start | bytes 1572872 | tf_op jit(solution)/shard_map/ppermute | solution.py:31
  36.1 2.4 %collective-permute-done.10.refs_1_ = bf16[64,2048]{1,0:T(8,128)(2,1)S(1)} collective-permute-done((bf16[64,2048]{1,0:T(8,128)(2,1)S(1)}, bf16[64,2048]{1,0:T(8,128)(2,1)S(1)}, u32[]{:S(2)}, u32[]{:S(2)}) %collective-permute-start.10) | collective-permute-done | bytes 262176 | tf_op jit(solution)/shard_map/ppermute | solution.py:31
  38.6 2.9 %project.3 = (bf16[3,256,128]{2,1,0:T(8,128)(2,1)S(1)}, bf16[3,256,128]{2,1,0:T(8,128)(2,1)S(1)}, bf16[2,3,256,128]{3,2,1,0:T(8,128)(2,1)S(1)}) custom-call(bf16[64,2048]{1,0:T(8,128)(2,1)S(1)} %pad_maximum_fusion.5.refs_0_, bf16[64,2048]{1,0:T(8,128)(2,1)S(1)} %pad_maximum_fusion.6.refs_1_, bf16[64,2048]{1,0:T(8,128)(2,1)S(1)} %collective-permute-done.7.refs_2_, ...), custom_call_target="tpu_custom_call" | custom-call | tf_op jit(solution)/shard_map/project/pallas_call | solution.py:135
  41.6 0.5 collective-permute-start.12
  42.1 2.6 %collective-permute-start.13 = (bf16[2,3,256,128]{3,2,1,0:T(8,128)(2,1)S(1)}, bf16[2,3,256,128]{3,2,1,0:T(8,128)(2,1)S(1)}, u32[]{:S(2)}, u32[]{:S(2)}) collective-permute-start(bf16[2,3,256,128]{3,2,1,0:T(8,128)(2,1)S(1)} %get-tuple-element.48), channel_id=1, source_target_pairs={{0,8},{4,12},{24,16},{28,20},{1,9},{5,13},{25,17},{29,21},{2,10},{... | collective-permute-start | bytes 1179656 | tf_op jit(solution)/shard_map/ppermute | solution.py:179
  44.6 2.9 %project.4 = (bf16[3,256,128]{2,1,0:T(8,128)(2,1)S(1)}, bf16[3,256,128]{2,1,0:T(8,128)(2,1)S(1)}, bf16[2,3,256,128]{3,2,1,0:T(8,128)(2,1)S(1)}) custom-call(bf16[64,2048]{1,0:T(8,128)(2,1)S(1)} %collective-permute-done.9.refs_0_, bf16[64,2048]{1,0:T(8,128)(2,1)S(1)} %collective-permute-done.10.refs_1_, bf16[64,2048]{1,0:T(8,128)(2,1)S(1)} %collective-permute-done.11.refs_2_, ...), custom_call_target="tpu_custom_call" | custom-call | tf_op jit(solution)/shard_map/project/pallas_call | solution.py:135
  47.5 0.2 collective-permute-done.17.refs_0_
  47.7 0.5 collective-permute-start.20
  48.3 4.7 %collective-permute-start.14 = (bf16[2,3,256,128]{3,2,1,0:T(8,128)(2,1)S(1)}, bf16[2,3,256,128]{3,2,1,0:T(8,128)(2,1)S(1)}, u32[]{:S(2)}, u32[]{:S(2)}) collective-permute-start(bf16[2,3,256,128]{3,2,1,0:T(8,128)(2,1)S(1)} %get-tuple-element.49), channel_id=1, source_target_pairs={{0,8},{4,12},{24,16},{28,20},{1,9},{5,13},{25,17},{29,21},{2,10},{... | collective-permute-start | bytes 1179656 | tf_op jit(solution)/shard_map/ppermute | solution.py:179
  52.9 0.4 collective-permute-done.13
  53.3 0.1 fusion.4
  53.4 4.5 %project.5 = (bf16[3,512,128]{2,1,0:T(8,128)(2,1)S(1)}, bf16[3,512,128]{2,1,0:T(8,128)(2,1)S(1)}, bf16[3,512,128]{2,1,0:T(8,128)(2,1)S(1)}, bf16[3,512,128]{2,1,0:T(8,128)(2,1)S(1)}) custom-call(bf16[128,2048]{1,0:T(8,128)(2,1)S(1)} %collective-permute-done.17.refs_0_, bf16[128,2048]{1,0:T(8,128)(2,1)S(1)} %collective-permute-done.18.refs_1_, ...), custom_call_target="tpu_custom_call" | custom-call | tf_op jit(solution)/shard_map/project/pallas_call | solution.py:135
  58.0 4.4 %collective-permute-start.23 = (bf16[3,512,128]{2,1,0:T(8,128)(2,1)S(1)}, bf16[3,512,128]{2,1,0:T(8,128)(2,1)S(1)}, u32[]{:S(2)}, u32[]{:S(2)}) collective-permute-start(bf16[3,512,128]{2,1,0:T(8,128)(2,1)S(1)} %get-tuple-element.52), channel_id=1, source_target_pairs={{0,8},{4,12},{24,16},{28,20},{1,9},{5,13},{25,17},{29,21},{2,10},{... | collective-permute-start | bytes 1179656 | tf_op jit(solution)/shard_map/ppermute | solution.py:179
  62.4 0.1 fusion.5
  62.6 0.7 collective-permute-start.15
  63.3 6.5 %collective-permute-start.21 = (bf16[3,512,128]{2,1,0:T(8,128)(2,1)S(1)}, bf16[3,512,128]{2,1,0:T(8,128)(2,1)S(1)}, u32[]{:S(2)}, u32[]{:S(2)}) collective-permute-start(bf16[3,512,128]{2,1,0:T(8,128)(2,1)S(1)} %get-tuple-element.53), channel_id=1, source_target_pairs={{0,8},{4,12},{24,16},{28,20},{1,9},{5,13},{25,17},{29,21},{2,10},{... | collective-permute-start | bytes 1179656 | tf_op jit(solution)/shard_map/ppermute | solution.py:179
  69.7 1.5 %collective-permute-done.23 = bf16[3,512,128]{2,1,0:T(8,128)(2,1)S(1)} collective-permute-done((bf16[3,512,128]{2,1,0:T(8,128)(2,1)S(1)}, bf16[3,512,128]{2,1,0:T(8,128)(2,1)S(1)}, u32[]{:S(2)}, u32[]{:S(2)}) %collective-permute-start.23) | collective-permute-done | bytes 393248 | tf_op jit(solution)/shard_map/ppermute | solution.py:179
  71.3 0.1 add_convert_fusion.1
  71.4 0.7 collective-permute-start.24
  72.1 0.1 add_convert_fusion.3
  72.2 6.0 %collective-permute-start.16 = (bf16[3,512,128]{2,1,0:T(8,128)(2,1)S(1)}, bf16[3,512,128]{2,1,0:T(8,128)(2,1)S(1)}, u32[]{:S(2)}, u32[]{:S(2)}) collective-permute-start(bf16[3,512,128]{2,1,0:T(8,128)(2,1)S(1)} %add_convert_fusion.3), channel_id=1, source_target_pairs={{0,8},{4,12},{8,0},{12,4},{16,24},{20,28},{24,16},{28,20},{1,9},{5... | collective-permute-start | bytes 1179656 | tf_op jit(solution)/shard_map/ppermute | solution.py:179
  78.2 1.5 %collective-permute-done.21 = bf16[3,512,128]{2,1,0:T(8,128)(2,1)S(1)} collective-permute-done((bf16[3,512,128]{2,1,0:T(8,128)(2,1)S(1)}, bf16[3,512,128]{2,1,0:T(8,128)(2,1)S(1)}, u32[]{:S(2)}, u32[]{:S(2)}) %collective-permute-start.21) | collective-permute-done | bytes 393248 | tf_op jit(solution)/shard_map/ppermute | solution.py:179
  79.7 0.1 add_convert_fusion.2
  79.8 0.8 fusion
  80.7 0.7 collective-permute-start.26
  81.4 0.9 add_convert_fusion
  82.2 5.9 %collective-permute-start.25 = (bf16[3,512,128]{2,1,0:T(8,128)(2,1)}, bf16[3,512,128]{2,1,0:T(8,128)(2,1)S(1)}, u32[]{:S(2)}, u32[]{:S(2)}) collective-permute-start(bf16[3,512,128]{2,1,0:T(8,128)(2,1)} %add_convert_fusion), channel_id=1, source_target_pairs={{0,8},{4,12},{8,0},{12,4},{16,24},{20,28},{24,16},{28,20},{1,9},{5... | collective-permute-start | bytes 1179656 | tf_op jit(solution)/shard_map/ppermute | solution.py:179
  88.2 0.7 fusion.1
  88.9 0.7 collective-permute-start.22
  89.5 0.1 pad_add_fusion.1.refs_0_
  89.7 5.7 %collective-permute-done.25.refs_5_ = bf16[3,512,128]{2,1,0:T(8,128)(2,1)S(1)} collective-permute-done((bf16[3,512,128]{2,1,0:T(8,128)(2,1)}, bf16[3,512,128]{2,1,0:T(8,128)(2,1)S(1)}, u32[]{:S(2)}, u32[]{:S(2)}) %collective-permute-start.25) | collective-permute-done | bytes 393248 | tf_op jit(solution)/shard_map/ppermute | solution.py:179
  95.4 2.8 %convolve.1.refs_7_ = f32[1024,128]{1,0:T(8,128)S(1)} custom-call(s32[3]{0:T(128)S(1)} %pad_add_fusion.1.refs_0_, bf16[3,512,128]{2,1,0:T(8,128)(2,1)S(1)} %constant_dynamic-update-slice_fusion.refs_1_, bf16[3,512,128]{2,1,0:T(8,128)(2,1)S(1)} %collective-permute-done.16.refs_2_, bf16[2,1024,128]{2,1,0:T(8,128)(2,1)S(1)} %collective-permute-done.26.refs_3_, ...), custom_call_target="tpu_custom_call" | custom-call | tf_op jit(solution)/shard_map/convolve/pallas_call | solution.py:327
  98.3 0.8 gate.1
  99.1 2.6 %collective-permute-start.29 = (bf16[2,128,128]{2,1,0:T(8,128)(2,1)S(1)}, bf16[2,128,128]{2,1,0:T(8,128)(2,1)S(1)}, u32[]{:S(2)}, u32[]{:S(2)}) collective-permute-start(bf16[2,128,128]{2,1,0:T(8,128)(2,1)S(1)} %get-tuple-element.64), channel_id=1, source_target_pairs={{0,24},{4,28},{8,16},{12,20},{16,8},{20,12},{24,0},{28,4},{1,25},{... | collective-permute-start | bytes 196616 | tf_op jit(solution)/shard_map/ppermute | solution.py:27
  101.7 4.3 %collective-permute-start.28 = (bf16[2,128,128]{2,1,0:T(8,128)(2,1)S(1)}, bf16[2,128,128]{2,1,0:T(8,128)(2,1)S(1)}, u32[]{:S(2)}, u32[]{:S(2)}) collective-permute-start(bf16[2,128,128]{2,1,0:T(8,128)(2,1)S(1)} %get-tuple-element.63), channel_id=1, source_target_pairs={{0,16},{4,20},{8,24},{12,28},{16,0},{20,4},{24,8},{28,12},{1,17},{... | collective-permute-start | bytes 196616 | tf_op jit(solution)/shard_map/ppermute | solution.py:27
  106.0 3.6 %collective-permute-done.28.refs_3_ = bf16[2,128,128]{2,1,0:T(8,128)(2,1)S(1)} collective-permute-done((bf16[2,128,128]{2,1,0:T(8,128)(2,1)S(1)}, bf16[2,128,128]{2,1,0:T(8,128)(2,1)S(1)}, u32[]{:S(2)}, u32[]{:S(2)}) %collective-permute-start.28) | collective-permute-done | bytes 65568 | tf_op jit(solution)/shard_map/ppermute | solution.py:27
  109.7 0.7 collective-permute-done.27.refs_2_
  110.5 0.1 pad_add_fusion.refs_0_
  110.5 1.3 %collective-permute-done.30.refs_5_ = bf16[4,128,128]{2,1,0:T(8,128)(2,1)S(1)} collective-permute-done((bf16[4,128,128]{2,1,0:T(8,128)(2,1)S(1)}, bf16[4,128,128]{2,1,0:T(8,128)(2,1)S(1)}, u32[]{:S(2)}, u32[]{:S(2)}) %collective-permute-start.30) | collective-permute-done | bytes 131104 | tf_op jit(solution)/shard_map/ppermute | solution.py:22
  111.8 1.3 %collect_columns.1 = bf16[128,1024]{1,0:T(8,128)(2,1)} custom-call(s32[2]{0:T(128)S(1)} %pad_add_fusion.refs_0_, bf16[2,128,128]{2,1,0:T(8,128)(2,1)S(1)} %get-tuple-element.61.refs_1_, bf16[2,128,128]{2,1,0:T(8,128)(2,1)S(1)} %collective-permute-done.27.refs_2_, bf16[2,128,128]{2,1,0:T(8,128)(2,1)S(1)} %collective-permute-done.28.refs_3_, ...), custom_call_target="tpu_custom_call" | custom-call | tf_op jit(solution)/shard_map/collect_columns/pallas_call | solution.py:434
  (51 shorter events, 0.9 us)
Async XLA Ops:
  0.0 18.5 %copy-start = (f32[3,3,1024]{2,1,0:T(4,128)S(1)}, f32[3,3,1024]{2,1,0:T(4,128)}, u32[]{:S(2)}) copy-start(f32[3,3,1024]{2,1,0:T(4,128)} %param.8) | copy-start | bytes 110596
  0.0 18.5 %collective-permute-start.6 = (bf16[3,1024,1024]{2,1,0:T(8,128)(2,1)}, bf16[3,1024,1024]{2,1,0:T(8,128)(2,1)}, u32[]{:S(2)}, u32[]{:S(2)}) collective-permute-start(bf16[3,1024,1024]{2,1,0:T(8,128)(2,1)} %bitcast.42), channel_id=1, source_target_pairs={{0,4},{4,0},{8,12},{12,8},{16,20},{20,16},{24,28},{28,24},{1,5},{5... | collective-permute-start | bytes 18874376 | tf_op jit(solution)/shard_map/ppermute | solution.py:22
  1.5 7.8 %collective-permute-start = (bf16[32,2048]{1,0:T(8,128)(2,1)S(1)}, bf16[32,2048]{1,0:T(8,128)(2,1)S(1)}, u32[]{:S(2)}, u32[]{:S(2)}) collective-permute-start(bf16[32,2048]{1,0:T(8,128)(2,1)S(1)} %get-tuple-element.79), channel_id=1, source_target_pairs={{0,3},{1,2},{2,1},{3,0},{4,7},{5,6},{6,5},{7,4},{8,11},{9,10},{10,... | collective-permute-start | bytes 393224 | tf_op jit(solution)/shard_map/ppermute | solution.py:31
  5.1 6.9 %collective-permute-start.1 = (bf16[32,2048]{1,0:T(8,128)(2,1)S(1)}, bf16[32,2048]{1,0:T(8,128)(2,1)S(1)}, u32[]{:S(2)}, u32[]{:S(2)}) collective-permute-start(bf16[32,2048]{1,0:T(8,128)(2,1)S(1)} %get-tuple-element.78), channel_id=1, source_target_pairs={{0,2},{1,3},{2,0},{3,1},{4,6},{5,7},{6,4},{7,5},{8,10},{9,11},{10,... | collective-permute-start | bytes 393224 | tf_op jit(solution)/shard_map/ppermute | solution.py:31
  5.6 6.7 %collective-permute-start.2 = (bf16[32,2048]{1,0:T(8,128)(2,1)S(1)}, bf16[32,2048]{1,0:T(8,128)(2,1)S(1)}, u32[]{:S(2)}, u32[]{:S(2)}) collective-permute-start(bf16[32,2048]{1,0:T(8,128)(2,1)S(1)} %get-tuple-element.77), channel_id=1, source_target_pairs={{0,1},{1,0},{2,3},{3,2},{4,5},{5,4},{6,7},{7,6},{8,9},{9,8},{10,11... | collective-permute-start | bytes 393224 | tf_op jit(solution)/shard_map/ppermute | solution.py:31
  13.3 11.4 %collective-permute-start.3 = (bf16[32,2048]{1,0:T(8,128)(2,1)S(1)}, bf16[32,2048]{1,0:T(8,128)(2,1)S(1)}, u32[]{:S(2)}, u32[]{:S(2)}) collective-permute-start(bf16[32,2048]{1,0:T(8,128)(2,1)S(1)} %get-tuple-element.67), channel_id=1, source_target_pairs={{0,8},{4,12},{8,0},{12,4},{16,24},{20,28},{24,16},{28,20},{1,9},{5... | collective-permute-start | bytes 393224 | tf_op jit(solution)/shard_map/ppermute | solution.py:27
  14.9 12.9 %collective-permute-start.4 = (bf16[32,2048]{1,0:T(8,128)(2,1)S(1)}, bf16[32,2048]{1,0:T(8,128)(2,1)S(1)}, u32[]{:S(2)}, u32[]{:S(2)}) collective-permute-start(bf16[32,2048]{1,0:T(8,128)(2,1)S(1)} %get-tuple-element.66), channel_id=1, source_target_pairs={{0,16},{4,20},{8,24},{12,28},{16,0},{20,4},{24,8},{28,12},{1,17},{... | collective-permute-start | bytes 393224 | tf_op jit(solution)/shard_map/ppermute | solution.py:27
  17.5 10.3 %collective-permute-start.5 = (bf16[32,2048]{1,0:T(8,128)(2,1)S(1)}, bf16[32,2048]{1,0:T(8,128)(2,1)S(1)}, u32[]{:S(2)}, u32[]{:S(2)}) collective-permute-start(bf16[32,2048]{1,0:T(8,128)(2,1)S(1)} %get-tuple-element.65), channel_id=1, source_target_pairs={{0,24},{4,28},{8,16},{12,20},{16,8},{20,12},{24,0},{28,4},{1,25},{... | collective-permute-start | bytes 393224 | tf_op jit(solution)/shard_map/ppermute | solution.py:27
  18.5 2.8 %copy-start.1 = (bf16[1024,3,1024]{2,0,1:T(8,128)(2,1)S(1)}, bf16[1024,3,1024]{2,0,1:T(8,128)(2,1)}, u32[]{:S(2)}) copy-start(bf16[1024,3,1024]{2,0,1:T(8,128)(2,1)} %param.7) | copy-start | bytes 18874372
  27.9 6.4 %collective-permute-start.9 = (bf16[64,2048]{1,0:T(8,128)(2,1)S(1)}, bf16[64,2048]{1,0:T(8,128)(2,1)S(1)}, u32[]{:S(2)}, u32[]{:S(2)}) collective-permute-start(bf16[64,2048]{1,0:T(8,128)(2,1)S(1)} %pad_maximum_fusion.5.refs_0_), channel_id=1, source_target_pairs={{0,1},{1,0},{2,3},{3,2},{4,5},{5,4},{6,7},{7,6},{8,9},{9,8},{10,11... | collective-permute-start | bytes 786440 | tf_op jit(solution)/shard_map/ppermute | solution.py:31
  29.5 8.9 %collective-permute-start.10 = (bf16[64,2048]{1,0:T(8,128)(2,1)S(1)}, bf16[64,2048]{1,0:T(8,128)(2,1)S(1)}, u32[]{:S(2)}, u32[]{:S(2)}) collective-permute-start(bf16[64,2048]{1,0:T(8,128)(2,1)S(1)} %pad_maximum_fusion.6.refs_1_), channel_id=1, source_target_pairs={{0,2},{1,3},{2,0},{3,1},{4,6},{5,7},{6,4},{7,5},{8,10},{9,11},{10,... | collective-permute-start | bytes 786440 | tf_op jit(solution)/shard_map/ppermute | solution.py:31
  29.9 8.6 %collective-permute-start.8 = (bf16[64,2048]{1,0:T(8,128)(2,1)S(1)}, bf16[64,2048]{1,0:T(8,128)(2,1)S(1)}, u32[]{:S(2)}, u32[]{:S(2)}) collective-permute-start(bf16[64,2048]{1,0:T(8,128)(2,1)S(1)} %pad_maximum_fusion.6.refs_1_), channel_id=1, source_target_pairs={{0,4},{4,0},{8,12},{12,8},{16,20},{20,16},{24,28},{28,24},{1,5},{5... | collective-permute-start | bytes 786440 | tf_op jit(solution)/shard_map/ppermute | solution.py:22
  30.0 8.6 %collective-permute-start.7 = (bf16[64,2048]{1,0:T(8,128)(2,1)S(1)}, bf16[64,2048]{1,0:T(8,128)(2,1)S(1)}, u32[]{:S(2)}, u32[]{:S(2)}) collective-permute-start(bf16[64,2048]{1,0:T(8,128)(2,1)S(1)} %pad_maximum_fusion.5.refs_0_), channel_id=1, source_target_pairs={{0,4},{4,0},{8,12},{12,8},{16,20},{20,16},{24,28},{28,24},{1,5},{5... | collective-permute-start | bytes 786440 | tf_op jit(solution)/shard_map/ppermute | solution.py:22
  34.4 13.1 %collective-permute-start.18 = (bf16[128,2048]{1,0:T(8,128)(2,1)S(1)}, bf16[128,2048]{1,0:T(8,128)(2,1)S(1)}, u32[]{:S(2)}, u32[]{:S(2)}) collective-permute-start(bf16[128,2048]{1,0:T(8,128)(2,1)S(1)} %pad_maximum_fusion.2), channel_id=1, source_target_pairs={{0,2},{1,3},{2,0},{3,1},{4,6},{5,7},{6,4},{7,5},{8,10},{9,11},{10,... | collective-permute-start | bytes 1572872 | tf_op jit(solution)/shard_map/ppermute | solution.py:31
  38.5 9.2 %collective-permute-start.17 = (bf16[128,2048]{1,0:T(8,128)(2,1)S(1)}, bf16[128,2048]{1,0:T(8,128)(2,1)S(1)}, u32[]{:S(2)}, u32[]{:S(2)}) collective-permute-start(bf16[128,2048]{1,0:T(8,128)(2,1)S(1)} %pad_maximum_fusion.1), channel_id=1, source_target_pairs={{0,1},{1,0},{2,3},{3,2},{4,5},{5,4},{6,7},{7,6},{8,9},{9,8},{10,11... | collective-permute-start | bytes 1572872 | tf_op jit(solution)/shard_map/ppermute | solution.py:31
  41.5 3.1 %collective-permute-start.11 = (bf16[64,2048]{1,0:T(8,128)(2,1)S(1)}, bf16[64,2048]{1,0:T(8,128)(2,1)S(1)}, u32[]{:S(2)}, u32[]{:S(2)}) collective-permute-start(bf16[64,2048]{1,0:T(8,128)(2,1)S(1)} %collective-permute-done.9.refs_0_), channel_id=1, source_target_pairs={{0,4},{4,0},{8,12},{12,8},{16,20},{20,16},{24,28},{28,24},{1,5},{5... | collective-permute-start | bytes 786440 | tf_op jit(solution)/shard_map/ppermute | solution.py:22
  41.6 3.1 %collective-permute-start.12 = (bf16[64,2048]{1,0:T(8,128)(2,1)S(1)}, bf16[64,2048]{1,0:T(8,128)(2,1)S(1)}, u32[]{:S(2)}, u32[]{:S(2)}) collective-permute-start(bf16[64,2048]{1,0:T(8,128)(2,1)S(1)} %collective-permute-done.10.refs_1_), channel_id=1, source_target_pairs={{0,4},{4,0},{8,12},{12,8},{16,20},{20,16},{24,28},{28,24},{1,5},{5... | collective-permute-start | bytes 786440 | tf_op jit(solution)/shard_map/ppermute | solution.py:22
  42.1 11.3 %collective-permute-start.13 = (bf16[2,3,256,128]{3,2,1,0:T(8,128)(2,1)S(1)}, bf16[2,3,256,128]{3,2,1,0:T(8,128)(2,1)S(1)}, u32[]{:S(2)}, u32[]{:S(2)}) collective-permute-start(bf16[2,3,256,128]{3,2,1,0:T(8,128)(2,1)S(1)} %get-tuple-element.48), channel_id=1, source_target_pairs={{0,8},{4,12},{24,16},{28,20},{1,9},{5,13},{25,17},{29,21},{2,10},{... | collective-permute-start | bytes 1179656 | tf_op jit(solution)/shard_map/ppermute | solution.py:179
  47.7 5.7 %collective-permute-start.19 = (bf16[128,2048]{1,0:T(8,128)(2,1)S(1)}, bf16[128,2048]{1,0:T(8,128)(2,1)S(1)}, u32[]{:S(2)}, u32[]{:S(2)}) collective-permute-start(bf16[128,2048]{1,0:T(8,128)(2,1)S(1)} %collective-permute-done.17.refs_0_), channel_id=1, source_target_pairs={{0,4},{4,0},{8,12},{12,8},{16,20},{20,16},{24,28},{28,24},{1,5},{5... | collective-permute-start | bytes 1572872 | tf_op jit(solution)/shard_map/ppermute | solution.py:22
  47.7 5.7 %collective-permute-start.20 = (bf16[128,2048]{1,0:T(8,128)(2,1)S(1)}, bf16[128,2048]{1,0:T(8,128)(2,1)S(1)}, u32[]{:S(2)}, u32[]{:S(2)}) collective-permute-start(bf16[128,2048]{1,0:T(8,128)(2,1)S(1)} %collective-permute-done.18.refs_1_), channel_id=1, source_target_pairs={{0,4},{4,0},{8,12},{12,8},{16,20},{20,16},{24,28},{28,24},{1,5},{5... | collective-permute-start | bytes 1572872 | tf_op jit(solution)/shard_map/ppermute | solution.py:22
  48.3 14.2 %collective-permute-start.14 = (bf16[2,3,256,128]{3,2,1,0:T(8,128)(2,1)S(1)}, bf16[2,3,256,128]{3,2,1,0:T(8,128)(2,1)S(1)}, u32[]{:S(2)}, u32[]{:S(2)}) collective-permute-start(bf16[2,3,256,128]{3,2,1,0:T(8,128)(2,1)S(1)} %get-tuple-element.49), channel_id=1, source_target_pairs={{0,8},{4,12},{24,16},{28,20},{1,9},{5,13},{25,17},{29,21},{2,10},{... | collective-permute-start | bytes 1179656 | tf_op jit(solution)/shard_map/ppermute | solution.py:179
  58.0 13.3 %collective-permute-start.23 = (bf16[3,512,128]{2,1,0:T(8,128)(2,1)S(1)}, bf16[3,512,128]{2,1,0:T(8,128)(2,1)S(1)}, u32[]{:S(2)}, u32[]{:S(2)}) collective-permute-start(bf16[3,512,128]{2,1,0:T(8,128)(2,1)S(1)} %get-tuple-element.52), channel_id=1, source_target_pairs={{0,8},{4,12},{24,16},{28,20},{1,9},{5,13},{25,17},{29,21},{2,10},{... | collective-permute-start | bytes 1179656 | tf_op jit(solution)/shard_map/ppermute | solution.py:179
  62.6 9.5 %collective-permute-start.15 = (bf16[3,512,128]{2,1,0:T(8,128)(2,1)S(1)}, bf16[3,512,128]{2,1,0:T(8,128)(2,1)S(1)}, u32[]{:S(2)}, u32[]{:S(2)}) collective-permute-start(bf16[3,512,128]{2,1,0:T(8,128)(2,1)S(1)} %pad_maximum_fusion.3), channel_id=1, source_target_pairs={{8,16},{12,20},{16,8},{20,12},{9,17},{13,21},{17,9},{21,13},{10,18... | collective-permute-start | bytes 1179656 | tf_op jit(solution)/shard_map/ppermute | solution.py:179
  63.3 16.4 %collective-permute-start.21 = (bf16[3,512,128]{2,1,0:T(8,128)(2,1)S(1)}, bf16[3,512,128]{2,1,0:T(8,128)(2,1)S(1)}, u32[]{:S(2)}, u32[]{:S(2)}) collective-permute-start(bf16[3,512,128]{2,1,0:T(8,128)(2,1)S(1)} %get-tuple-element.53), channel_id=1, source_target_pairs={{0,8},{4,12},{24,16},{28,20},{1,9},{5,13},{25,17},{29,21},{2,10},{... | collective-permute-start | bytes 1179656 | tf_op jit(solution)/shard_map/ppermute | solution.py:179
  71.4 10.0 %collective-permute-start.24 = (bf16[3,512,128]{2,1,0:T(8,128)(2,1)S(1)}, bf16[3,512,128]{2,1,0:T(8,128)(2,1)S(1)}, u32[]{:S(2)}, u32[]{:S(2)}) collective-permute-start(bf16[3,512,128]{2,1,0:T(8,128)(2,1)S(1)} %add_convert_fusion.1), channel_id=1, source_target_pairs={{8,16},{12,20},{16,8},{20,12},{9,17},{13,21},{17,9},{21,13},{10,18... | collective-permute-start | bytes 1179656 | tf_op jit(solution)/shard_map/ppermute | solution.py:179
  72.2 17.5 %collective-permute-start.16 = (bf16[3,512,128]{2,1,0:T(8,128)(2,1)S(1)}, bf16[3,512,128]{2,1,0:T(8,128)(2,1)S(1)}, u32[]{:S(2)}, u32[]{:S(2)}) collective-permute-start(bf16[3,512,128]{2,1,0:T(8,128)(2,1)S(1)} %add_convert_fusion.3), channel_id=1, source_target_pairs={{0,8},{4,12},{8,0},{12,4},{16,24},{20,28},{24,16},{28,20},{1,9},{5... | collective-permute-start | bytes 1179656 | tf_op jit(solution)/shard_map/ppermute | solution.py:179
  80.7 9.0 %collective-permute-start.26 = (bf16[2,1024,128]{2,1,0:T(8,128)(2,1)}, bf16[2,1024,128]{2,1,0:T(8,128)(2,1)S(1)}, u32[]{:S(2)}, u32[]{:S(2)}) collective-permute-start(bf16[2,1024,128]{2,1,0:T(8,128)(2,1)} %fusion), channel_id=1, source_target_pairs={{8,16},{12,20},{16,8},{20,12},{9,17},{13,21},{17,9},{21,13},{10,18... | collective-permute-start | bytes 1572872 | tf_op jit(solution)/shard_map/ppermute | solution.py:179
  82.2 13.2 %collective-permute-start.25 = (bf16[3,512,128]{2,1,0:T(8,128)(2,1)}, bf16[3,512,128]{2,1,0:T(8,128)(2,1)S(1)}, u32[]{:S(2)}, u32[]{:S(2)}) collective-permute-start(bf16[3,512,128]{2,1,0:T(8,128)(2,1)} %add_convert_fusion), channel_id=1, source_target_pairs={{0,8},{4,12},{8,0},{12,4},{16,24},{20,28},{24,16},{28,20},{1,9},{5... | collective-permute-start | bytes 1179656 | tf_op jit(solution)/shard_map/ppermute | solution.py:179
  88.9 9.4 %collective-permute-start.22 = (bf16[1,1024,128]{2,1,0:T(8,128)(2,1)}, bf16[1,1024,128]{2,1,0:T(8,128)(2,1)S(1)}, u32[]{:S(2)}, u32[]{:S(2)}) collective-permute-start(bf16[1,1024,128]{2,1,0:T(8,128)(2,1)} %fusion.1), channel_id=1, source_target_pairs={{8,16},{12,20},{16,8},{20,12},{9,17},{13,21},{17,9},{21,13},{10,18... | collective-permute-start | bytes 786440 | tf_op jit(solution)/shard_map/ppermute | solution.py:179
  99.1 6.9 %collective-permute-start.29 = (bf16[2,128,128]{2,1,0:T(8,128)(2,1)S(1)}, bf16[2,128,128]{2,1,0:T(8,128)(2,1)S(1)}, u32[]{:S(2)}, u32[]{:S(2)}) collective-permute-start(bf16[2,128,128]{2,1,0:T(8,128)(2,1)S(1)} %get-tuple-element.64), channel_id=1, source_target_pairs={{0,24},{4,28},{8,16},{12,20},{16,8},{20,12},{24,0},{28,4},{1,25},{... | collective-permute-start | bytes 196616 | tf_op jit(solution)/shard_map/ppermute | solution.py:27
  101.7 8.0 %collective-permute-start.28 = (bf16[2,128,128]{2,1,0:T(8,128)(2,1)S(1)}, bf16[2,128,128]{2,1,0:T(8,128)(2,1)S(1)}, u32[]{:S(2)}, u32[]{:S(2)}) collective-permute-start(bf16[2,128,128]{2,1,0:T(8,128)(2,1)S(1)} %get-tuple-element.63), channel_id=1, source_target_pairs={{0,16},{4,20},{8,24},{12,28},{16,0},{20,4},{24,8},{28,12},{1,17},{... | collective-permute-start | bytes 196616 | tf_op jit(solution)/shard_map/ppermute | solution.py:27
  106.0 4.3 %collective-permute-start.27 = (bf16[2,128,128]{2,1,0:T(8,128)(2,1)S(1)}, bf16[2,128,128]{2,1,0:T(8,128)(2,1)S(1)}, u32[]{:S(2)}, u32[]{:S(2)}) collective-permute-start(bf16[2,128,128]{2,1,0:T(8,128)(2,1)S(1)} %get-tuple-element.62), channel_id=1, source_target_pairs={{0,8},{4,12},{8,0},{12,4},{16,24},{20,28},{24,16},{28,20},{1,9},{5... | collective-permute-start | bytes 196616 | tf_op jit(solution)/shard_map/ppermute | solution.py:27
  110.4 1.4 %collective-permute-start.30 = (bf16[4,128,128]{2,1,0:T(8,128)(2,1)S(1)}, bf16[4,128,128]{2,1,0:T(8,128)(2,1)S(1)}, u32[]{:S(2)}, u32[]{:S(2)}) collective-permute-start(bf16[4,128,128]{2,1,0:T(8,128)(2,1)S(1)} %pad_maximum_fusion.7), channel_id=1, source_target_pairs={{0,4},{4,0},{8,12},{12,8},{16,20},{20,16},{24,28},{28,24},{1,5},{5... | collective-permute-start | bytes 393224 | tf_op jit(solution)/shard_map/ppermute | solution.py:22

commit v5 on v4

--- a/solution.py
+++ b/solution.py
@@ -54,7 +54,7 @@
 
 
 def sending_order(planes):
-    return [planes - 1, *range(1, planes - 1), 0]
+    return [*reversed(range(planes))]
 
 
 def stage_kernel(planes, where_ref, w_own, w_sib, out_ref, sems):
@@ -97,24 +97,25 @@
     )(jnp.stack([z, core]).astype(jnp.int32), w_own, w_sib)
 
 
-def project_kernel(planes, pieces, merged, *refs):
+def project_kernel(planes, pieces, merged, pairs, *refs):
     x_refs, w_ref, outs, x_all = refs[:pieces], refs[pieces], refs[pieces + 1 : -1], refs[-1]
     lanes = w_ref.shape[2] // planes
     if merged:
-        outs = [*outs[:-1], outs[-1].at[1], outs[-1].at[0]]
+        outs = [outs[0].at[1], outs[0].at[0]]
     at = 0
     for ref in x_refs:
         x_all[at : at + ref.shape[0]] = ref[...]
         at += ref.shape[0]
     order = sending_order(planes)
-    for i in range(0, planes, 2):
+    first = order[pairs[-1] + 1]
+    for i in pairs:
 
         @pl.loop(0, 3)
         def _(j):
             w = w_ref[j, :, i * lanes : (i + 2) * lanes]
             sums = jnp.dot(x_all[...], w, preferred_element_type=F32).astype(BF16)
-            outs[order[i]][j] = sums[:, :lanes]
-            outs[order[i + 1]][j] = sums[:, lanes:]
+            outs[order[i] - first][j] = sums[:, :lanes]
+            outs[order[i + 1] - first][j] = sums[:, lanes:]
 
 
 def project(xs, w, planes, merged):
@@ -129,19 +130,24 @@
         return [*blocks[:-2], jnp.stack([blocks[-1], blocks[-2]])] if merged else blocks
     vmem = pl.BlockSpec(memory_space=pltpu.VMEM)
     block = jax.ShapeDtypeStruct((3, rows, lanes), BF16)
-    out_shape = [block] * planes
-    if merged:
-        out_shape = [block] * (planes - 2) + [jax.ShapeDtypeStruct((2, 3, rows, lanes), BF16)]
-    return pl.pallas_call(
-        lambda *refs: project_kernel(planes, len(xs), merged, *refs),
-        in_specs=[vmem] * (len(xs) + 1),
-        out_specs=[vmem] * len(out_shape),
-        out_shape=out_shape,
-        scratch_shapes=[pltpu.VMEM((rows, wide), BF16)],
-        compiler_params=pltpu.CompilerParams(vmem_limit_bytes=8 << 20),
-        cost_estimate=pl.CostEstimate(flops=0, bytes_accessed=0, transcendentals=0),
-        name="project",
-    )(*xs, pltpu.with_memory_space_constraint(w, pltpu.VMEM))
+
+    def call(merged, pairs):
+        out_shape = [block] * (2 * len(pairs))
+        if merged:
+            out_shape = [jax.ShapeDtypeStruct((2, 3, rows, lanes), BF16)]
+        return pl.pallas_call(
+            lambda *refs: project_kernel(planes, len(xs), merged, pairs, *refs),
+            in_specs=[vmem] * (len(xs) + 1),
+            out_specs=[vmem] * len(out_shape),
+            out_shape=out_shape,
+            scratch_shapes=[pltpu.VMEM((rows, wide), BF16)],
+            compiler_params=pltpu.CompilerParams(vmem_limit_bytes=8 << 20),
+            cost_estimate=pl.CostEstimate(flops=0, bytes_accessed=0, transcendentals=0),
+            name="project",
+        )(*xs, pltpu.with_memory_space_constraint(w, pltpu.VMEM))
+
+    pairs = [*range(0, planes, 2)]
+    return [*call(False, pairs[1:]), *call(True, pairs[:1])] if merged else call(False, pairs)
 
 
 def add(*blocks):
@@ -484,10 +490,10 @@
     a, b = LineSum(planes), LineSum(planes)
     blocks = project_pieces(0, x, [(0, 0), (0, 1)], True)
     a.take_and_send(blocks)
-    near = tie(blocks[0], near)
+    near = tie(blocks[-1], near)
     blocks = project_pieces(0, near, [(1, 0), (2, 1)], True)
     a.take_and_send(blocks)
-    rest = tie(blocks[0], rest)
+    rest = tie(blocks[-1], rest)
     halves = [(1, 1), (3, 1), (2, 0), (3, 0)] + [(s, h) for s in range(4, n_ch) for h in range(2)]
     b.take(project_pieces(1, rest, halves, False))
     for t in range(planes - 2):

time: 114 us -> 113 us (level)
  starting transfers between devices: 54.1 us -> 45.7 us
  waiting for transfers between devices: 27.4 us -> 34.7 us
    ppermute x10, starting transfers between devices: 32.8 us -> 26.3 us  [exchange(): return lax.ppermute(block, 'ctx', route) if route else None]
    ppermute x10, waiting for transfers between devices: 9.13 us -> 14.1 us  [exchange(): return lax.ppermute(block, 'ctx', route) if route else None]
    ppermute x7, waiting for transfers between devices: 9.52 us -> 12.4 us  [to_column(): return lax.ppermute(block, 'ch', [(j, j ^ distance) for j in range(n_ch)])]
    ppermute x6, starting transfers between devices: 11.4 us -> 9.41 us  [to_plane(): return lax.ppermute(block, 'ctx', route)]
    pallas_call x3 -> x5, Pallas kernels: 10.3 us -> 10.4 us  [call(): pl.pallas_call(lambda *refs: project_kernel(planes, len(xs), merged, pair...]
  transfers between devices with their start and end apart: 31 -> 31, of which waited for: 13 -> 15; matrix products, arithmetic and copies ran while one was open for 9% -> 9% of each run, Pallas kernels for 15% -> 15%
where the time goes in v5:
time: 113 us; the launch traced here: 112 us
  starting transfers between devices  45.7 us (40%)
  waiting for transfers between devices  34.7 us (31%)
  Pallas kernels  18.7 us (17%)
  other arithmetic  6.73 us (6%)
  local copies, waits for them, and re-layouts  5.78 us (5%)
    ppermute x10, starting transfers between devices, exchange(): return lax.ppermute(block, 'ctx', route) if route else None  26.3 us
    ppermute x10, waiting for transfers between devices, exchange(): return lax.ppermute(block, 'ctx', route) if route else None  14.1 us
    ppermute x7, waiting for transfers between devices, to_column(): return lax.ppermute(block, 'ch', [(j, j ^ distance) for j in range(n_ch)])  12.4 us
    pallas_call x5, Pallas kernels, call(): pl.pallas_call(lambda *refs: project_kernel(planes, len(xs), merged, pair...  10.4 us
    ppermute x6, starting transfers between devices, to_plane(): return lax.ppermute(block, 'ctx', route)  9.41 us
    ppermute x7, starting transfers between devices, to_column(): return lax.ppermute(block, 'ch', [(j, j ^ distance) for j in range(n_ch)])  7.88 us
    ppermute x6, waiting for transfers between devices, to_plane(): return lax.ppermute(block, 'ctx', route)  6.91 us
    pallas_call x1, Pallas kernels, stage(): pl.pallas_call(lambda *refs: stage_kernel(planes, *refs), in_specs=[pl.Bl...  3.39 us
  transfers between devices with their start and end apart: 31, of which 15 were waited for; matrix products, arithmetic and copies ran while one was open for 9% of the time, Pallas kernels for 15%

profile of v5, /device:TPU:0, one launch (start us, length us, event | category | flops | bytes accessed | tf_op | source)
XLA Modules:
  0.0 112.1 jit_solution(17070683434340779265)
XLA Ops:
  0.0 0.5 collective-permute-start.6
  0.5 1.1 dynamic-slice_bitcast_fusion
  1.5 3.5 %collective-permute-start = (bf16[32,2048]{1,0:T(8,128)(2,1)S(1)}, bf16[32,2048]{1,0:T(8,128)(2,1)S(1)}, u32[]{:S(2)}, u32[]{:S(2)}) collective-permute-start(bf16[32,2048]{1,0:T(8,128)(2,1)S(1)} %get-tuple-element.75), channel_id=1, source_target_pairs={{0,3},{1,2},{2,1},{3,0},{4,7},{5,6},{6,5},{7,4},{8,11},{9,10},{10,... | collective-permute-start | bytes 393224 | tf_op jit(solution)/shard_map/ppermute | solution.py:31
  5.1 0.5 collective-permute-start.1
  5.6 0.1 collective-permute-start.2
  5.7 0.8 constant_dynamic-slice_fusion.5
  6.9 2.2 %multiply_reduce_fusion = f32[8,128,128]{2,1,0:T(8,128)S(1)} fusion(f32[128,128]{1,0:T(8,128)S(1)} %maximum_convert_fusion, f32[8,16]{1,0:T(8,128)S(1)} %get-tuple-element.77, f32[8,16]{1,0:T(8,128)S(1)} %get-tuple-element.76), kind=kLoop, calls=%fused_computation | loop fusion | flops 6160384 | bytes 590848 | tf_op jit(solution)/shard_map/reduce_sum | solution.py:235
  9.1 0.1 exponential_multiply_fusion
  9.3 2.7 %collective-permute-done.1 = bf16[32,2048]{1,0:T(8,128)(2,1)S(1)} collective-permute-done((bf16[32,2048]{1,0:T(8,128)(2,1)S(1)}, bf16[32,2048]{1,0:T(8,128)(2,1)S(1)}, u32[]{:S(2)}, u32[]{:S(2)}) %collective-permute-start.1) | collective-permute-done | bytes 131104 | tf_op jit(solution)/shard_map/ppermute | solution.py:31
  12.0 0.3 collective-permute-done.2
  12.3 1.0 fusion.13
  13.3 1.6 %collective-permute-start.3 = (bf16[32,2048]{1,0:T(8,128)(2,1)S(1)}, bf16[32,2048]{1,0:T(8,128)(2,1)S(1)}, u32[]{:S(2)}, u32[]{:S(2)}) collective-permute-start(bf16[32,2048]{1,0:T(8,128)(2,1)S(1)} %get-tuple-element.63), channel_id=1, source_target_pairs={{0,8},{4,12},{8,0},{12,4},{16,24},{20,28},{24,16},{28,20},{1,9},{5... | collective-permute-start | bytes 393224 | tf_op jit(solution)/shard_map/ppermute | solution.py:27
  14.9 2.6 %collective-permute-start.4 = (bf16[32,2048]{1,0:T(8,128)(2,1)S(1)}, bf16[32,2048]{1,0:T(8,128)(2,1)S(1)}, u32[]{:S(2)}, u32[]{:S(2)}) collective-permute-start(bf16[32,2048]{1,0:T(8,128)(2,1)S(1)} %get-tuple-element.62), channel_id=1, source_target_pairs={{0,16},{4,20},{8,24},{12,28},{16,0},{20,4},{24,8},{28,12},{1,17},{... | collective-permute-start | bytes 393224 | tf_op jit(solution)/shard_map/ppermute | solution.py:27
  17.5 0.2 collective-permute-start.5
  17.7 0.8 dynamic-slice_bitcast_fusion.3.refs_7_
  18.5 2.8 %copy-done.1 = bf16[1024,3,1024]{2,0,1:T(8,128)(2,1)S(1)} copy-done((bf16[1024,3,1024]{2,0,1:T(8,128)(2,1)S(1)}, bf16[1024,3,1024]{2,0,1:T(8,128)(2,1)}, u32[]{:S(2)}) %copy-start.1) | copy-done | bytes 6291480
  21.3 3.4 %stage.1.refs_4_ = bf16[3,2048,512]{2,1,0:T(8,128)(2,1)S(1)} custom-call(s32[2]{0:T(128)S(1)} %pad_add_fusion.2.refs_0_, bf16[3,1024,1024]{2,1,0:T(8,128)(2,1)S(1)} %bitcast.43, bf16[3,1024,1024]{2,1,0:T(8,128)(2,1)} %collective-permute-done.6.refs_2_), custom_call_target="tpu_custom_call" | custom-call | tf_op jit(solution)/shard_map/stage/pallas_call | solution.py:88
  24.7 3.1 %collective-permute-done.4 = bf16[32,2048]{1,0:T(8,128)(2,1)S(1)} collective-permute-done((bf16[32,2048]{1,0:T(8,128)(2,1)S(1)}, bf16[32,2048]{1,0:T(8,128)(2,1)S(1)}, u32[]{:S(2)}, u32[]{:S(2)}) %collective-permute-start.4) | collective-permute-done | bytes 131104 | tf_op jit(solution)/shard_map/ppermute | solution.py:27
  27.9 1.6 %collective-permute-start.9 = (bf16[64,2048]{1,0:T(8,128)(2,1)S(1)}, bf16[64,2048]{1,0:T(8,128)(2,1)S(1)}, u32[]{:S(2)}, u32[]{:S(2)}) collective-permute-start(bf16[64,2048]{1,0:T(8,128)(2,1)S(1)} %pad_maximum_fusion.5.refs_0_), channel_id=1, source_target_pairs={{0,1},{1,0},{2,3},{3,2},{4,5},{5,4},{6,7},{7,6},{8,9},{9,8},{10,11... | collective-permute-start | bytes 786440 | tf_op jit(solution)/shard_map/ppermute | solution.py:31
  29.5 0.4 collective-permute-start.10
  30.0 0.5 collective-permute-start.7
  30.5 3.9 %collective-permute-done.9.refs_0_ = bf16[64,2048]{1,0:T(8,128)(2,1)S(1)} collective-permute-done((bf16[64,2048]{1,0:T(8,128)(2,1)S(1)}, bf16[64,2048]{1,0:T(8,128)(2,1)S(1)}, u32[]{:S(2)}, u32[]{:S(2)}) %collective-permute-start.9) | collective-permute-done | bytes 262176 | tf_op jit(solution)/shard_map/ppermute | solution.py:31
  34.4 1.6 %collective-permute-start.18 = (bf16[128,2048]{1,0:T(8,128)(2,1)S(1)}, bf16[128,2048]{1,0:T(8,128)(2,1)S(1)}, u32[]{:S(2)}, u32[]{:S(2)}) collective-permute-start(bf16[128,2048]{1,0:T(8,128)(2,1)S(1)} %pad_maximum_fusion.2), channel_id=1, source_target_pairs={{0,2},{1,3},{2,0},{3,1},{4,6},{5,7},{6,4},{7,5},{8,10},{9,11},{10,... | collective-permute-start | bytes 1572872 | tf_op jit(solution)/shard_map/ppermute | solution.py:31
  36.1 2.4 %collective-permute-done.10.refs_1_ = bf16[64,2048]{1,0:T(8,128)(2,1)S(1)} collective-permute-done((bf16[64,2048]{1,0:T(8,128)(2,1)S(1)}, bf16[64,2048]{1,0:T(8,128)(2,1)S(1)}, u32[]{:S(2)}, u32[]{:S(2)}) %collective-permute-start.10) | collective-permute-done | bytes 262176 | tf_op jit(solution)/shard_map/ppermute | solution.py:31
  38.6 1.4 %project.6 = bf16[2,3,256,128]{3,2,1,0:T(8,128)(2,1)S(1)} custom-call(bf16[64,2048]{1,0:T(8,128)(2,1)S(1)} %pad_maximum_fusion.5.refs_0_, bf16[64,2048]{1,0:T(8,128)(2,1)S(1)} %pad_maximum_fusion.6.refs_1_, bf16[64,2048]{1,0:T(8,128)(2,1)S(1)} %collective-permute-done.7.refs_2_, bf16[64,2048]{1,0:T(8,128)(2,1)S(1)} %collective-permute-done.8.refs_3_, ...), custom_call_target="tpu_custom_call" | custom-call | tf_op jit(solution)/shard_map/project/pallas_call | solution.py:138
  40.1 0.5 collective-permute-start.12
  40.6 2.6 %collective-permute-start.13 = (bf16[2,3,256,128]{3,2,1,0:T(8,128)(2,1)S(1)}, bf16[2,3,256,128]{3,2,1,0:T(8,128)(2,1)S(1)}, u32[]{:S(2)}, u32[]{:S(2)}) collective-permute-start(bf16[2,3,256,128]{3,2,1,0:T(8,128)(2,1)S(1)} %project.6), channel_id=1, source_target_pairs={{0,8},{4,12},{24,16},{28,20},{1,9},{5,13},{25,17},{29,21},{2,10},{... | collective-permute-start | bytes 1179656 | tf_op jit(solution)/shard_map/ppermute | solution.py:185
  43.2 1.4 %project.8 = bf16[2,3,256,128]{3,2,1,0:T(8,128)(2,1)S(1)} custom-call(bf16[64,2048]{1,0:T(8,128)(2,1)S(1)} %collective-permute-done.9.refs_0_, bf16[64,2048]{1,0:T(8,128)(2,1)S(1)} %collective-permute-done.10.refs_1_, bf16[64,2048]{1,0:T(8,128)(2,1)S(1)} %collective-permute-done.11.refs_2_, bf16[64,2048]{1,0:T(8,128)(2,1)S(1)} %collective-permute-done.12.refs_3_, ...), custom_call_target="tpu_custom_call" | custom-call | tf_op jit(solution)/shard_map/project/pallas_call | solution.py:138
  44.7 2.5 %collective-permute-done.18.refs_1_ = bf16[128,2048]{1,0:T(8,128)(2,1)S(1)} collective-permute-done((bf16[128,2048]{1,0:T(8,128)(2,1)S(1)}, bf16[128,2048]{1,0:T(8,128)(2,1)S(1)}, u32[]{:S(2)}, u32[]{:S(2)}) %collective-permute-start.18) | collective-permute-done | bytes 524320 | tf_op jit(solution)/shard_map/ppermute | solution.py:31
  47.2 0.6 collective-permute-done.17.refs_0_
  47.8 0.5 collective-permute-start.20
  48.3 4.7 %collective-permute-start.14 = (bf16[2,3,256,128]{3,2,1,0:T(8,128)(2,1)S(1)}, bf16[2,3,256,128]{3,2,1,0:T(8,128)(2,1)S(1)}, u32[]{:S(2)}, u32[]{:S(2)}) collective-permute-start(bf16[2,3,256,128]{3,2,1,0:T(8,128)(2,1)S(1)} %project.8), channel_id=1, source_target_pairs={{0,8},{4,12},{24,16},{28,20},{1,9},{5,13},{25,17},{29,21},{2,10},{... | collective-permute-start | bytes 1179656 | tf_op jit(solution)/shard_map/ppermute | solution.py:185
  53.0 0.1 fusion.4
  53.1 4.5 %project.9 = (bf16[3,512,128]{2,1,0:T(8,128)(2,1)S(1)}, bf16[3,512,128]{2,1,0:T(8,128)(2,1)S(1)}, bf16[3,512,128]{2,1,0:T(8,128)(2,1)S(1)}, bf16[3,512,128]{2,1,0:T(8,128)(2,1)S(1)}) custom-call(bf16[128,2048]{1,0:T(8,128)(2,1)S(1)} %collective-permute-done.17.refs_0_, bf16[128,2048]{1,0:T(8,128)(2,1)S(1)} %collective-permute-done.18.refs_1_, ...), custom_call_target="tpu_custom_call" | custom-call | tf_op jit(solution)/shard_map/project/pallas_call | solution.py:138
  57.6 3.2 %collective-permute-start.23 = (bf16[3,512,128]{2,1,0:T(8,128)(2,1)S(1)}, bf16[3,512,128]{2,1,0:T(8,128)(2,1)S(1)}, u32[]{:S(2)}, u32[]{:S(2)}) collective-permute-start(bf16[3,512,128]{2,1,0:T(8,128)(2,1)S(1)} %get-tuple-element.48), channel_id=1, source_target_pairs={{0,8},{4,12},{24,16},{28,20},{1,9},{5,13},{25,17},{29,21},{2,10},{... | collective-permute-start | bytes 1179656 | tf_op jit(solution)/shard_map/ppermute | solution.py:185
  60.9 1.5 %collective-permute-done.14 = bf16[2,3,256,128]{3,2,1,0:T(8,128)(2,1)S(1)} collective-permute-done((bf16[2,3,256,128]{3,2,1,0:T(8,128)(2,1)S(1)}, bf16[2,3,256,128]{3,2,1,0:T(8,128)(2,1)S(1)}, u32[]{:S(2)}, u32[]{:S(2)}) %collective-permute-start.14) | collective-permute-done | bytes 393248 | tf_op jit(solution)/shard_map/ppermute | solution.py:185
  62.4 0.1 fusion.5
  62.6 0.7 collective-permute-start.15
  63.2 1.5 %project.5 = (bf16[3,256,128]{2,1,0:T(8,128)(2,1)S(1)}, bf16[3,256,128]{2,1,0:T(8,128)(2,1)S(1)}) custom-call(bf16[64,2048]{1,0:T(8,128)(2,1)S(1)} %pad_maximum_fusion.5.refs_0_, bf16[64,2048]{1,0:T(8,128)(2,1)S(1)} %pad_maximum_fusion.6.refs_1_, bf16[64,2048]{1,0:T(8,128)(2,1)S(1)} %collective-permute-done.7.refs_2_, ...), custom_call_target="tpu_custom_call" | custom-call | tf_op jit(solution)/shard_map/project/pallas_call | solution.py:138
  64.7 1.5 %project.7 = (bf16[3,256,128]{2,1,0:T(8,128)(2,1)S(1)}, bf16[3,256,128]{2,1,0:T(8,128)(2,1)S(1)}) custom-call(bf16[64,2048]{1,0:T(8,128)(2,1)S(1)} %collective-permute-done.9.refs_0_, bf16[64,2048]{1,0:T(8,128)(2,1)S(1)} %collective-permute-done.10.refs_1_, bf16[64,2048]{1,0:T(8,128)(2,1)S(1)} %collective-permute-done.11.refs_2_, ...), custom_call_target="tpu_custom_call" | custom-call | tf_op jit(solution)/shard_map/project/pallas_call | solution.py:138
  66.2 7.4 %collective-permute-start.21 = (bf16[3,512,128]{2,1,0:T(8,128)(2,1)S(1)}, bf16[3,512,128]{2,1,0:T(8,128)(2,1)S(1)}, u32[]{:S(2)}, u32[]{:S(2)}) collective-permute-start(bf16[3,512,128]{2,1,0:T(8,128)(2,1)S(1)} %get-tuple-element.49), channel_id=1, source_target_pairs={{0,8},{4,12},{24,16},{28,20},{1,9},{5,13},{25,17},{29,21},{2,10},{... | collective-permute-start | bytes 1179656 | tf_op jit(solution)/shard_map/ppermute | solution.py:185
  73.6 0.1 add_convert_fusion.1
  73.7 0.7 collective-permute-start.24
  74.4 0.1 add_convert_fusion.3
  74.6 1.8 %collective-permute-start.16 = (bf16[3,512,128]{2,1,0:T(8,128)(2,1)S(1)}, bf16[3,512,128]{2,1,0:T(8,128)(2,1)S(1)}, u32[]{:S(2)}, u32[]{:S(2)}) collective-permute-start(bf16[3,512,128]{2,1,0:T(8,128)(2,1)S(1)} %add_convert_fusion.3), channel_id=1, source_target_pairs={{0,8},{4,12},{8,0},{12,4},{16,24},{20,28},{24,16},{28,20},{1,9},{5... | collective-permute-start | bytes 1179656 | tf_op jit(solution)/shard_map/ppermute | solution.py:185
  76.3 6.8 %collective-permute-done.21 = bf16[3,512,128]{2,1,0:T(8,128)(2,1)S(1)} collective-permute-done((bf16[3,512,128]{2,1,0:T(8,128)(2,1)S(1)}, bf16[3,512,128]{2,1,0:T(8,128)(2,1)S(1)}, u32[]{:S(2)}, u32[]{:S(2)}) %collective-permute-start.21) | collective-permute-done | bytes 393248 | tf_op jit(solution)/shard_map/ppermute | solution.py:185
  83.3 0.8 fusion
  84.1 0.7 collective-permute-start.26
  84.8 0.9 add_convert_fusion
  85.7 4.0 %collective-permute-start.25 = (bf16[3,512,128]{2,1,0:T(8,128)(2,1)}, bf16[3,512,128]{2,1,0:T(8,128)(2,1)S(1)}, u32[]{:S(2)}, u32[]{:S(2)}) collective-permute-start(bf16[3,512,128]{2,1,0:T(8,128)(2,1)} %add_convert_fusion), channel_id=1, source_target_pairs={{0,8},{4,12},{8,0},{12,4},{16,24},{20,28},{24,16},{28,20},{1,9},{5... | collective-permute-start | bytes 1179656 | tf_op jit(solution)/shard_map/ppermute | solution.py:185
  89.7 0.7 fusion.1
  90.4 0.7 collective-permute-start.22
  91.2 0.3 collective-permute-done.16.refs_2_
  91.6 5.4 %collective-permute-done.25.refs_5_ = bf16[3,512,128]{2,1,0:T(8,128)(2,1)S(1)} collective-permute-done((bf16[3,512,128]{2,1,0:T(8,128)(2,1)}, bf16[3,512,128]{2,1,0:T(8,128)(2,1)S(1)}, u32[]{:S(2)}, u32[]{:S(2)}) %collective-permute-start.25) | collective-permute-done | bytes 393248 | tf_op jit(solution)/shard_map/ppermute | solution.py:185
  97.0 2.8 %convolve.1.refs_7_ = f32[1024,128]{1,0:T(8,128)S(1)} custom-call(s32[3]{0:T(128)S(1)} %pad_add_fusion.1.refs_0_, bf16[3,512,128]{2,1,0:T(8,128)(2,1)S(1)} %constant_dynamic-update-slice_fusion.refs_1_, bf16[3,512,128]{2,1,0:T(8,128)(2,1)S(1)} %collective-permute-done.16.refs_2_, bf16[2,1024,128]{2,1,0:T(8,128)(2,1)S(1)} %collective-permute-done.26.refs_3_, ...), custom_call_target="tpu_custom_call" | custom-call | tf_op jit(solution)/shard_map/convolve/pallas_call | solution.py:333
  99.8 0.8 gate.1
  100.6 1.4 %collective-permute-start.29 = (bf16[2,128,128]{2,1,0:T(8,128)(2,1)S(1)}, bf16[2,128,128]{2,1,0:T(8,128)(2,1)S(1)}, u32[]{:S(2)}, u32[]{:S(2)}) collective-permute-start(bf16[2,128,128]{2,1,0:T(8,128)(2,1)S(1)} %get-tuple-element.60), channel_id=1, source_target_pairs={{0,24},{4,28},{8,16},{12,20},{16,8},{20,12},{24,0},{28,4},{1,25},{... | collective-permute-start | bytes 196616 | tf_op jit(solution)/shard_map/ppermute | solution.py:27
  102.0 3.1 %collective-permute-start.28 = (bf16[2,128,128]{2,1,0:T(8,128)(2,1)S(1)}, bf16[2,128,128]{2,1,0:T(8,128)(2,1)S(1)}, u32[]{:S(2)}, u32[]{:S(2)}) collective-permute-start(bf16[2,128,128]{2,1,0:T(8,128)(2,1)S(1)} %get-tuple-element.59), channel_id=1, source_target_pairs={{0,16},{4,20},{8,24},{12,28},{16,0},{20,4},{24,8},{28,12},{1,17},{... | collective-permute-start | bytes 196616 | tf_op jit(solution)/shard_map/ppermute | solution.py:27
  105.1 0.5 collective-permute-start.27
  105.6 1.2 %collective-permute-done.29.refs_4_ = bf16[2,128,128]{2,1,0:T(8,128)(2,1)S(1)} collective-permute-done((bf16[2,128,128]{2,1,0:T(8,128)(2,1)S(1)}, bf16[2,128,128]{2,1,0:T(8,128)(2,1)S(1)}, u32[]{:S(2)}, u32[]{:S(2)}) %collective-permute-start.29) | collective-permute-done | bytes 65568 | tf_op jit(solution)/shard_map/ppermute | solution.py:27
  106.8 1.4 %collective-permute-done.28.refs_3_ = bf16[2,128,128]{2,1,0:T(8,128)(2,1)S(1)} collective-permute-done((bf16[2,128,128]{2,1,0:T(8,128)(2,1)S(1)}, bf16[2,128,128]{2,1,0:T(8,128)(2,1)S(1)}, u32[]{:S(2)}, u32[]{:S(2)}) %collective-permute-start.28) | collective-permute-done | bytes 65568 | tf_op jit(solution)/shard_map/ppermute | solution.py:27
  108.2 1.2 %collective-permute-done.27.refs_2_ = bf16[2,128,128]{2,1,0:T(8,128)(2,1)S(1)} collective-permute-done((bf16[2,128,128]{2,1,0:T(8,128)(2,1)S(1)}, bf16[2,128,128]{2,1,0:T(8,128)(2,1)S(1)}, u32[]{:S(2)}, u32[]{:S(2)}) %collective-permute-start.27) | collective-permute-done | bytes 65568 | tf_op jit(solution)/shard_map/ppermute | solution.py:27
  109.5 1.3 %collective-permute-done.30.refs_5_ = bf16[4,128,128]{2,1,0:T(8,128)(2,1)S(1)} collective-permute-done((bf16[4,128,128]{2,1,0:T(8,128)(2,1)S(1)}, bf16[4,128,128]{2,1,0:T(8,128)(2,1)S(1)}, u32[]{:S(2)}, u32[]{:S(2)}) %collective-permute-start.30) | collective-permute-done | bytes 131104 | tf_op jit(solution)/shard_map/ppermute | solution.py:22
  110.8 1.3 %collect_columns.1 = bf16[128,1024]{1,0:T(8,128)(2,1)} custom-call(s32[2]{0:T(128)S(1)} %pad_add_fusion.refs_0_, bf16[2,128,128]{2,1,0:T(8,128)(2,1)S(1)} %get-tuple-element.57.refs_1_, bf16[2,128,128]{2,1,0:T(8,128)(2,1)S(1)} %collective-permute-done.27.refs_2_, bf16[2,128,128]{2,1,0:T(8,128)(2,1)S(1)} %collective-permute-done.28.refs_3_, ...), custom_call_target="tpu_custom_call" | custom-call | tf_op jit(solution)/shard_map/collect_columns/pallas_call | solution.py:440
  (53 shorter events, 1.3 us)
Async XLA Ops:
  0.0 18.5 %copy-start = (f32[3,3,1024]{2,1,0:T(4,128)S(1)}, f32[3,3,1024]{2,1,0:T(4,128)}, u32[]{:S(2)}) copy-start(f32[3,3,1024]{2,1,0:T(4,128)} %param.8) | copy-start | bytes 110596
  0.0 18.5 %collective-permute-start.6 = (bf16[3,1024,1024]{2,1,0:T(8,128)(2,1)}, bf16[3,1024,1024]{2,1,0:T(8,128)(2,1)}, u32[]{:S(2)}, u32[]{:S(2)}) collective-permute-start(bf16[3,1024,1024]{2,1,0:T(8,128)(2,1)} %bitcast.42), channel_id=1, source_target_pairs={{0,4},{4,0},{8,12},{12,8},{16,20},{20,16},{24,28},{28,24},{1,5},{5... | collective-permute-start | bytes 18874376 | tf_op jit(solution)/shard_map/ppermute | solution.py:22
  1.5 7.8 %collective-permute-start = (bf16[32,2048]{1,0:T(8,128)(2,1)S(1)}, bf16[32,2048]{1,0:T(8,128)(2,1)S(1)}, u32[]{:S(2)}, u32[]{:S(2)}) collective-permute-start(bf16[32,2048]{1,0:T(8,128)(2,1)S(1)} %get-tuple-element.75), channel_id=1, source_target_pairs={{0,3},{1,2},{2,1},{3,0},{4,7},{5,6},{6,5},{7,4},{8,11},{9,10},{10,... | collective-permute-start | bytes 393224 | tf_op jit(solution)/shard_map/ppermute | solution.py:31
  5.1 6.9 %collective-permute-start.1 = (bf16[32,2048]{1,0:T(8,128)(2,1)S(1)}, bf16[32,2048]{1,0:T(8,128)(2,1)S(1)}, u32[]{:S(2)}, u32[]{:S(2)}) collective-permute-start(bf16[32,2048]{1,0:T(8,128)(2,1)S(1)} %get-tuple-element.74), channel_id=1, source_target_pairs={{0,2},{1,3},{2,0},{3,1},{4,6},{5,7},{6,4},{7,5},{8,10},{9,11},{10,... | collective-permute-start | bytes 393224 | tf_op jit(solution)/shard_map/ppermute | solution.py:31
  5.6 6.7 %collective-permute-start.2 = (bf16[32,2048]{1,0:T(8,128)(2,1)S(1)}, bf16[32,2048]{1,0:T(8,128)(2,1)S(1)}, u32[]{:S(2)}, u32[]{:S(2)}) collective-permute-start(bf16[32,2048]{1,0:T(8,128)(2,1)S(1)} %get-tuple-element.73), channel_id=1, source_target_pairs={{0,1},{1,0},{2,3},{3,2},{4,5},{5,4},{6,7},{7,6},{8,9},{9,8},{10,11... | collective-permute-start | bytes 393224 | tf_op jit(solution)/shard_map/ppermute | solution.py:31
  13.3 11.4 %collective-permute-start.3 = (bf16[32,2048]{1,0:T(8,128)(2,1)S(1)}, bf16[32,2048]{1,0:T(8,128)(2,1)S(1)}, u32[]{:S(2)}, u32[]{:S(2)}) collective-permute-start(bf16[32,2048]{1,0:T(8,128)(2,1)S(1)} %get-tuple-element.63), channel_id=1, source_target_pairs={{0,8},{4,12},{8,0},{12,4},{16,24},{20,28},{24,16},{28,20},{1,9},{5... | collective-permute-start | bytes 393224 | tf_op jit(solution)/shard_map/ppermute | solution.py:27
  14.9 12.9 %collective-permute-start.4 = (bf16[32,2048]{1,0:T(8,128)(2,1)S(1)}, bf16[32,2048]{1,0:T(8,128)(2,1)S(1)}, u32[]{:S(2)}, u32[]{:S(2)}) collective-permute-start(bf16[32,2048]{1,0:T(8,128)(2,1)S(1)} %get-tuple-element.62), channel_id=1, source_target_pairs={{0,16},{4,20},{8,24},{12,28},{16,0},{20,4},{24,8},{28,12},{1,17},{... | collective-permute-start | bytes 393224 | tf_op jit(solution)/shard_map/ppermute | solution.py:27
  17.5 10.3 %collective-permute-start.5 = (bf16[32,2048]{1,0:T(8,128)(2,1)S(1)}, bf16[32,2048]{1,0:T(8,128)(2,1)S(1)}, u32[]{:S(2)}, u32[]{:S(2)}) collective-permute-start(bf16[32,2048]{1,0:T(8,128)(2,1)S(1)} %get-tuple-element.61), channel_id=1, source_target_pairs={{0,24},{4,28},{8,16},{12,20},{16,8},{20,12},{24,0},{28,4},{1,25},{... | collective-permute-start | bytes 393224 | tf_op jit(solution)/shard_map/ppermute | solution.py:27
  18.5 2.8 %copy-start.1 = (bf16[1024,3,1024]{2,0,1:T(8,128)(2,1)S(1)}, bf16[1024,3,1024]{2,0,1:T(8,128)(2,1)}, u32[]{:S(2)}) copy-start(bf16[1024,3,1024]{2,0,1:T(8,128)(2,1)} %param.7) | copy-start | bytes 18874372
  27.9 6.4 %collective-permute-start.9 = (bf16[64,2048]{1,0:T(8,128)(2,1)S(1)}, bf16[64,2048]{1,0:T(8,128)(2,1)S(1)}, u32[]{:S(2)}, u32[]{:S(2)}) collective-permute-start(bf16[64,2048]{1,0:T(8,128)(2,1)S(1)} %pad_maximum_fusion.5.refs_0_), channel_id=1, source_target_pairs={{0,1},{1,0},{2,3},{3,2},{4,5},{5,4},{6,7},{7,6},{8,9},{9,8},{10,11... | collective-permute-start | bytes 786440 | tf_op jit(solution)/shard_map/ppermute | solution.py:31
  29.5 8.9 %collective-permute-start.10 = (bf16[64,2048]{1,0:T(8,128)(2,1)S(1)}, bf16[64,2048]{1,0:T(8,128)(2,1)S(1)}, u32[]{:S(2)}, u32[]{:S(2)}) collective-permute-start(bf16[64,2048]{1,0:T(8,128)(2,1)S(1)} %pad_maximum_fusion.6.refs_1_), channel_id=1, source_target_pairs={{0,2},{1,3},{2,0},{3,1},{4,6},{5,7},{6,4},{7,5},{8,10},{9,11},{10,... | collective-permute-start | bytes 786440 | tf_op jit(solution)/shard_map/ppermute | solution.py:31
  30.0 8.6 %collective-permute-start.8 = (bf16[64,2048]{1,0:T(8,128)(2,1)S(1)}, bf16[64,2048]{1,0:T(8,128)(2,1)S(1)}, u32[]{:S(2)}, u32[]{:S(2)}) collective-permute-start(bf16[64,2048]{1,0:T(8,128)(2,1)S(1)} %pad_maximum_fusion.6.refs_1_), channel_id=1, source_target_pairs={{0,4},{4,0},{8,12},{12,8},{16,20},{20,16},{24,28},{28,24},{1,5},{5... | collective-permute-start | bytes 786440 | tf_op jit(solution)/shard_map/ppermute | solution.py:22
  30.0 8.6 %collective-permute-start.7 = (bf16[64,2048]{1,0:T(8,128)(2,1)S(1)}, bf16[64,2048]{1,0:T(8,128)(2,1)S(1)}, u32[]{:S(2)}, u32[]{:S(2)}) collective-permute-start(bf16[64,2048]{1,0:T(8,128)(2,1)S(1)} %pad_maximum_fusion.5.refs_0_), channel_id=1, source_target_pairs={{0,4},{4,0},{8,12},{12,8},{16,20},{20,16},{24,28},{28,24},{1,5},{5... | collective-permute-start | bytes 786440 | tf_op jit(solution)/shard_map/ppermute | solution.py:22
  34.4 12.8 %collective-permute-start.18 = (bf16[128,2048]{1,0:T(8,128)(2,1)S(1)}, bf16[128,2048]{1,0:T(8,128)(2,1)S(1)}, u32[]{:S(2)}, u32[]{:S(2)}) collective-permute-start(bf16[128,2048]{1,0:T(8,128)(2,1)S(1)} %pad_maximum_fusion.2), channel_id=1, source_target_pairs={{0,2},{1,3},{2,0},{3,1},{4,6},{5,7},{6,4},{7,5},{8,10},{9,11},{10,... | collective-permute-start | bytes 1572872 | tf_op jit(solution)/shard_map/ppermute | solution.py:31
  38.5 9.2 %collective-permute-start.17 = (bf16[128,2048]{1,0:T(8,128)(2,1)S(1)}, bf16[128,2048]{1,0:T(8,128)(2,1)S(1)}, u32[]{:S(2)}, u32[]{:S(2)}) collective-permute-start(bf16[128,2048]{1,0:T(8,128)(2,1)S(1)} %pad_maximum_fusion.1), channel_id=1, source_target_pairs={{0,1},{1,0},{2,3},{3,2},{4,5},{5,4},{6,7},{7,6},{8,9},{9,8},{10,11... | collective-permute-start | bytes 1572872 | tf_op jit(solution)/shard_map/ppermute | solution.py:31
  40.0 3.2 %collective-permute-start.11 = (bf16[64,2048]{1,0:T(8,128)(2,1)S(1)}, bf16[64,2048]{1,0:T(8,128)(2,1)S(1)}, u32[]{:S(2)}, u32[]{:S(2)}) collective-permute-start(bf16[64,2048]{1,0:T(8,128)(2,1)S(1)} %collective-permute-done.9.refs_0_), channel_id=1, source_target_pairs={{0,4},{4,0},{8,12},{12,8},{16,20},{20,16},{24,28},{28,24},{1,5},{5... | collective-permute-start | bytes 786440 | tf_op jit(solution)/shard_map/ppermute | solution.py:22
  40.1 3.1 %collective-permute-start.12 = (bf16[64,2048]{1,0:T(8,128)(2,1)S(1)}, bf16[64,2048]{1,0:T(8,128)(2,1)S(1)}, u32[]{:S(2)}, u32[]{:S(2)}) collective-permute-start(bf16[64,2048]{1,0:T(8,128)(2,1)S(1)} %collective-permute-done.10.refs_1_), channel_id=1, source_target_pairs={{0,4},{4,0},{8,12},{12,8},{16,20},{20,16},{24,28},{28,24},{1,5},{5... | collective-permute-start | bytes 786440 | tf_op jit(solution)/shard_map/ppermute | solution.py:22
  40.6 12.3 %collective-permute-start.13 = (bf16[2,3,256,128]{3,2,1,0:T(8,128)(2,1)S(1)}, bf16[2,3,256,128]{3,2,1,0:T(8,128)(2,1)S(1)}, u32[]{:S(2)}, u32[]{:S(2)}) collective-permute-start(bf16[2,3,256,128]{3,2,1,0:T(8,128)(2,1)S(1)} %project.6), channel_id=1, source_target_pairs={{0,8},{4,12},{24,16},{28,20},{1,9},{5,13},{25,17},{29,21},{2,10},{... | collective-permute-start | bytes 1179656 | tf_op jit(solution)/shard_map/ppermute | solution.py:185
  47.7 5.3 %collective-permute-start.19 = (bf16[128,2048]{1,0:T(8,128)(2,1)S(1)}, bf16[128,2048]{1,0:T(8,128)(2,1)S(1)}, u32[]{:S(2)}, u32[]{:S(2)}) collective-permute-start(bf16[128,2048]{1,0:T(8,128)(2,1)S(1)} %collective-permute-done.17.refs_0_), channel_id=1, source_target_pairs={{0,4},{4,0},{8,12},{12,8},{16,20},{20,16},{24,28},{28,24},{1,5},{5... | collective-permute-start | bytes 1572872 | tf_op jit(solution)/shard_map/ppermute | solution.py:22
  47.8 5.3 %collective-permute-start.20 = (bf16[128,2048]{1,0:T(8,128)(2,1)S(1)}, bf16[128,2048]{1,0:T(8,128)(2,1)S(1)}, u32[]{:S(2)}, u32[]{:S(2)}) collective-permute-start(bf16[128,2048]{1,0:T(8,128)(2,1)S(1)} %collective-permute-done.18.refs_1_), channel_id=1, source_target_pairs={{0,4},{4,0},{8,12},{12,8},{16,20},{20,16},{24,28},{28,24},{1,5},{5... | collective-permute-start | bytes 1572872 | tf_op jit(solution)/shard_map/ppermute | solution.py:22
  48.3 14.1 %collective-permute-start.14 = (bf16[2,3,256,128]{3,2,1,0:T(8,128)(2,1)S(1)}, bf16[2,3,256,128]{3,2,1,0:T(8,128)(2,1)S(1)}, u32[]{:S(2)}, u32[]{:S(2)}) collective-permute-start(bf16[2,3,256,128]{3,2,1,0:T(8,128)(2,1)S(1)} %project.8), channel_id=1, source_target_pairs={{0,8},{4,12},{24,16},{28,20},{1,9},{5,13},{25,17},{29,21},{2,10},{... | collective-permute-start | bytes 1179656 | tf_op jit(solution)/shard_map/ppermute | solution.py:185
  57.6 16.0 %collective-permute-start.23 = (bf16[3,512,128]{2,1,0:T(8,128)(2,1)S(1)}, bf16[3,512,128]{2,1,0:T(8,128)(2,1)S(1)}, u32[]{:S(2)}, u32[]{:S(2)}) collective-permute-start(bf16[3,512,128]{2,1,0:T(8,128)(2,1)S(1)} %get-tuple-element.48), channel_id=1, source_target_pairs={{0,8},{4,12},{24,16},{28,20},{1,9},{5,13},{25,17},{29,21},{2,10},{... | collective-permute-start | bytes 1179656 | tf_op jit(solution)/shard_map/ppermute | solution.py:185
  62.6 11.9 %collective-permute-start.15 = (bf16[3,512,128]{2,1,0:T(8,128)(2,1)S(1)}, bf16[3,512,128]{2,1,0:T(8,128)(2,1)S(1)}, u32[]{:S(2)}, u32[]{:S(2)}) collective-permute-start(bf16[3,512,128]{2,1,0:T(8,128)(2,1)S(1)} %pad_maximum_fusion.3), channel_id=1, source_target_pairs={{8,16},{12,20},{16,8},{20,12},{9,17},{13,21},{17,9},{21,13},{10,18... | collective-permute-start | bytes 1179656 | tf_op jit(solution)/shard_map/ppermute | solution.py:185
  66.2 16.9 %collective-permute-start.21 = (bf16[3,512,128]{2,1,0:T(8,128)(2,1)S(1)}, bf16[3,512,128]{2,1,0:T(8,128)(2,1)S(1)}, u32[]{:S(2)}, u32[]{:S(2)}) collective-permute-start(bf16[3,512,128]{2,1,0:T(8,128)(2,1)S(1)} %get-tuple-element.49), channel_id=1, source_target_pairs={{0,8},{4,12},{24,16},{28,20},{1,9},{5,13},{25,17},{29,21},{2,10},{... | collective-permute-start | bytes 1179656 | tf_op jit(solution)/shard_map/ppermute | solution.py:185
  73.7 11.1 %collective-permute-start.24 = (bf16[3,512,128]{2,1,0:T(8,128)(2,1)S(1)}, bf16[3,512,128]{2,1,0:T(8,128)(2,1)S(1)}, u32[]{:S(2)}, u32[]{:S(2)}) collective-permute-start(bf16[3,512,128]{2,1,0:T(8,128)(2,1)S(1)} %add_convert_fusion.1), channel_id=1, source_target_pairs={{8,16},{12,20},{16,8},{20,12},{9,17},{13,21},{17,9},{21,13},{10,18... | collective-permute-start | bytes 1179656 | tf_op jit(solution)/shard_map/ppermute | solution.py:185
  74.6 17.0 %collective-permute-start.16 = (bf16[3,512,128]{2,1,0:T(8,128)(2,1)S(1)}, bf16[3,512,128]{2,1,0:T(8,128)(2,1)S(1)}, u32[]{:S(2)}, u32[]{:S(2)}) collective-permute-start(bf16[3,512,128]{2,1,0:T(8,128)(2,1)S(1)} %add_convert_fusion.3), channel_id=1, source_target_pairs={{0,8},{4,12},{8,0},{12,4},{16,24},{20,28},{24,16},{28,20},{1,9},{5... | collective-permute-start | bytes 1179656 | tf_op jit(solution)/shard_map/ppermute | solution.py:185
  84.1 7.5 %collective-permute-start.26 = (bf16[2,1024,128]{2,1,0:T(8,128)(2,1)}, bf16[2,1024,128]{2,1,0:T(8,128)(2,1)S(1)}, u32[]{:S(2)}, u32[]{:S(2)}) collective-permute-start(bf16[2,1024,128]{2,1,0:T(8,128)(2,1)} %fusion), channel_id=1, source_target_pairs={{8,16},{12,20},{16,8},{20,12},{9,17},{13,21},{17,9},{21,13},{10,18... | collective-permute-start | bytes 1572872 | tf_op jit(solution)/shard_map/ppermute | solution.py:185
  85.7 11.3 %collective-permute-start.25 = (bf16[3,512,128]{2,1,0:T(8,128)(2,1)}, bf16[3,512,128]{2,1,0:T(8,128)(2,1)S(1)}, u32[]{:S(2)}, u32[]{:S(2)}) collective-permute-start(bf16[3,512,128]{2,1,0:T(8,128)(2,1)} %add_convert_fusion), channel_id=1, source_target_pairs={{0,8},{4,12},{8,0},{12,4},{16,24},{20,28},{24,16},{28,20},{1,9},{5... | collective-permute-start | bytes 1179656 | tf_op jit(solution)/shard_map/ppermute | solution.py:185
  90.4 9.4 %collective-permute-start.22 = (bf16[1,1024,128]{2,1,0:T(8,128)(2,1)}, bf16[1,1024,128]{2,1,0:T(8,128)(2,1)S(1)}, u32[]{:S(2)}, u32[]{:S(2)}) collective-permute-start(bf16[1,1024,128]{2,1,0:T(8,128)(2,1)} %fusion.1), channel_id=1, source_target_pairs={{8,16},{12,20},{16,8},{20,12},{9,17},{13,21},{17,9},{21,13},{10,18... | collective-permute-start | bytes 786440 | tf_op jit(solution)/shard_map/ppermute | solution.py:185
  100.6 6.1 %collective-permute-start.29 = (bf16[2,128,128]{2,1,0:T(8,128)(2,1)S(1)}, bf16[2,128,128]{2,1,0:T(8,128)(2,1)S(1)}, u32[]{:S(2)}, u32[]{:S(2)}) collective-permute-start(bf16[2,128,128]{2,1,0:T(8,128)(2,1)S(1)} %get-tuple-element.60), channel_id=1, source_target_pairs={{0,24},{4,28},{8,16},{12,20},{16,8},{20,12},{24,0},{28,4},{1,25},{... | collective-permute-start | bytes 196616 | tf_op jit(solution)/shard_map/ppermute | solution.py:27
  102.0 6.2 %collective-permute-start.28 = (bf16[2,128,128]{2,1,0:T(8,128)(2,1)S(1)}, bf16[2,128,128]{2,1,0:T(8,128)(2,1)S(1)}, u32[]{:S(2)}, u32[]{:S(2)}) collective-permute-start(bf16[2,128,128]{2,1,0:T(8,128)(2,1)S(1)} %get-tuple-element.59), channel_id=1, source_target_pairs={{0,16},{4,20},{8,24},{12,28},{16,0},{20,4},{24,8},{28,12},{1,17},{... | collective-permute-start | bytes 196616 | tf_op jit(solution)/shard_map/ppermute | solution.py:27
  105.1 4.3 %collective-permute-start.27 = (bf16[2,128,128]{2,1,0:T(8,128)(2,1)S(1)}, bf16[2,128,128]{2,1,0:T(8,128)(2,1)S(1)}, u32[]{:S(2)}, u32[]{:S(2)}) collective-permute-start(bf16[2,128,128]{2,1,0:T(8,128)(2,1)S(1)} %get-tuple-element.58), channel_id=1, source_target_pairs={{0,8},{4,12},{8,0},{12,4},{16,24},{20,28},{24,16},{28,20},{1,9},{5... | collective-permute-start | bytes 196616 | tf_op jit(solution)/shard_map/ppermute | solution.py:27
  109.4 1.4 %collective-permute-start.30 = (bf16[4,128,128]{2,1,0:T(8,128)(2,1)S(1)}, bf16[4,128,128]{2,1,0:T(8,128)(2,1)S(1)}, u32[]{:S(2)}, u32[]{:S(2)}) collective-permute-start(bf16[4,128,128]{2,1,0:T(8,128)(2,1)S(1)} %pad_maximum_fusion.7), channel_id=1, source_target_pairs={{0,4},{4,0},{8,12},{12,8},{16,20},{20,16},{24,28},{28,24},{1,5},{5... | collective-permute-start | bytes 393224 | tf_op jit(solution)/shard_map/ppermute | solution.py:22

commit v6 on v5

--- a/solution.py
+++ b/solution.py
@@ -147,7 +147,7 @@
         )(*xs, pltpu.with_memory_space_constraint(w, pltpu.VMEM))
 
     pairs = [*range(0, planes, 2)]
-    return [*call(False, pairs[1:]), *call(True, pairs[:1])] if merged else call(False, pairs)
+    return [*call(False, pairs[1:]), *call(merged, pairs[:1])]
 
 
 def add(*blocks):

time: 113 us -> 113 us (level)
    pallas_call x5 -> x6, Pallas kernels: 10.4 us -> 10.5 us  [call(): pl.pallas_call(lambda *refs: project_kernel(planes, len(xs), merged, pair...]
  transfers between devices with their start and end apart: 31 -> 31, of which waited for: 15 -> 13; matrix products, arithmetic and copies ran while one was open for 9% -> 9% of each run, Pallas kernels for 15% -> 15%
where the time goes in v6:
time: 113 us; the launch traced here: 112 us
  starting transfers between devices  46.6 us (41%)
  waiting for transfers between devices  33.9 us (30%)
  Pallas kernels  18.8 us (17%)
  other arithmetic  6.74 us (6%)
  local copies, waits for them, and re-layouts  5.78 us (5%)
    ppermute x10, starting transfers between devices, exchange(): return lax.ppermute(block, 'ctx', route) if route else None  27 us
    ppermute x10, waiting for transfers between devices, exchange(): return lax.ppermute(block, 'ctx', route) if route else None  13.7 us
    ppermute x7, waiting for transfers between devices, to_column(): return lax.ppermute(block, 'ch', [(j, j ^ distance) for j in range(n_ch)])  11.6 us
    pallas_call x6, Pallas kernels, call(): pl.pallas_call(lambda *refs: project_kernel(planes, len(xs), merged, pair...  10.5 us
    ppermute x6, starting transfers between devices, to_plane(): return lax.ppermute(block, 'ctx', route)  9.33 us
    ppermute x7, starting transfers between devices, to_column(): return lax.ppermute(block, 'ch', [(j, j ^ distance) for j in range(n_ch)])  8.17 us
    ppermute x6, waiting for transfers between devices, to_plane(): return lax.ppermute(block, 'ctx', route)  7.32 us
    pallas_call x1, Pallas kernels, stage(): pl.pallas_call(lambda *refs: stage_kernel(planes, *refs), in_specs=[pl.Bl...  3.39 us
  transfers between devices with their start and end apart: 31, of which 13 were waited for; matrix products, arithmetic and copies ran while one was open for 9% of the time, Pallas kernels for 15%

profile of v6, /device:TPU:0, one launch (start us, length us, event | category | flops | bytes accessed | tf_op | source)
XLA Modules:
  0.0 112.4 jit_solution(4533608574480592)
XLA Ops:
  0.0 0.5 collective-permute-start.6
  0.5 1.1 dynamic-slice_bitcast_fusion
  1.5 3.5 %collective-permute-start = (bf16[32,2048]{1,0:T(8,128)(2,1)S(1)}, bf16[32,2048]{1,0:T(8,128)(2,1)S(1)}, u32[]{:S(2)}, u32[]{:S(2)}) collective-permute-start(bf16[32,2048]{1,0:T(8,128)(2,1)S(1)} %get-tuple-element.75), channel_id=1, source_target_pairs={{0,3},{1,2},{2,1},{3,0},{4,7},{5,6},{6,5},{7,4},{8,11},{9,10},{10,... | collective-permute-start | bytes 393224 | tf_op jit(solution)/shard_map/ppermute | solution.py:31
  5.1 0.5 collective-permute-start.1
  5.6 0.1 collective-permute-start.2
  5.7 0.8 constant_dynamic-slice_fusion.5
  6.9 2.2 %multiply_reduce_fusion = f32[8,128,128]{2,1,0:T(8,128)S(1)} fusion(f32[128,128]{1,0:T(8,128)S(1)} %maximum_convert_fusion, f32[8,16]{1,0:T(8,128)S(1)} %get-tuple-element.77, f32[8,16]{1,0:T(8,128)S(1)} %get-tuple-element.76), kind=kLoop, calls=%fused_computation | loop fusion | flops 6160384 | bytes 590848 | tf_op jit(solution)/shard_map/reduce_sum | solution.py:235
  9.1 0.1 exponential_multiply_fusion
  9.3 2.7 %collective-permute-done.1 = bf16[32,2048]{1,0:T(8,128)(2,1)S(1)} collective-permute-done((bf16[32,2048]{1,0:T(8,128)(2,1)S(1)}, bf16[32,2048]{1,0:T(8,128)(2,1)S(1)}, u32[]{:S(2)}, u32[]{:S(2)}) %collective-permute-start.1) | collective-permute-done | bytes 131104 | tf_op jit(solution)/shard_map/ppermute | solution.py:31
  12.0 0.3 collective-permute-done.2
  12.3 1.0 fusion.13
  13.3 1.6 %collective-permute-start.3 = (bf16[32,2048]{1,0:T(8,128)(2,1)S(1)}, bf16[32,2048]{1,0:T(8,128)(2,1)S(1)}, u32[]{:S(2)}, u32[]{:S(2)}) collective-permute-start(bf16[32,2048]{1,0:T(8,128)(2,1)S(1)} %get-tuple-element.63), channel_id=1, source_target_pairs={{0,8},{4,12},{8,0},{12,4},{16,24},{20,28},{24,16},{28,20},{1,9},{5... | collective-permute-start | bytes 393224 | tf_op jit(solution)/shard_map/ppermute | solution.py:27
  14.9 2.6 %collective-permute-start.4 = (bf16[32,2048]{1,0:T(8,128)(2,1)S(1)}, bf16[32,2048]{1,0:T(8,128)(2,1)S(1)}, u32[]{:S(2)}, u32[]{:S(2)}) collective-permute-start(bf16[32,2048]{1,0:T(8,128)(2,1)S(1)} %get-tuple-element.62), channel_id=1, source_target_pairs={{0,16},{4,20},{8,24},{12,28},{16,0},{20,4},{24,8},{28,12},{1,17},{... | collective-permute-start | bytes 393224 | tf_op jit(solution)/shard_map/ppermute | solution.py:27
  17.5 0.2 collective-permute-start.5
  17.7 0.8 dynamic-slice_bitcast_fusion.3.refs_7_
  18.5 2.8 %copy-done.1 = bf16[1024,3,1024]{2,0,1:T(8,128)(2,1)S(1)} copy-done((bf16[1024,3,1024]{2,0,1:T(8,128)(2,1)S(1)}, bf16[1024,3,1024]{2,0,1:T(8,128)(2,1)}, u32[]{:S(2)}) %copy-start.1) | copy-done | bytes 6291480
  21.3 3.4 %stage.1.refs_4_ = bf16[3,2048,512]{2,1,0:T(8,128)(2,1)S(1)} custom-call(s32[2]{0:T(128)S(1)} %pad_add_fusion.2.refs_0_, bf16[3,1024,1024]{2,1,0:T(8,128)(2,1)S(1)} %bitcast.43, bf16[3,1024,1024]{2,1,0:T(8,128)(2,1)} %collective-permute-done.6.refs_2_), custom_call_target="tpu_custom_call" | custom-call | tf_op jit(solution)/shard_map/stage/pallas_call | solution.py:88
  24.7 3.1 %collective-permute-done.4 = bf16[32,2048]{1,0:T(8,128)(2,1)S(1)} collective-permute-done((bf16[32,2048]{1,0:T(8,128)(2,1)S(1)}, bf16[32,2048]{1,0:T(8,128)(2,1)S(1)}, u32[]{:S(2)}, u32[]{:S(2)}) %collective-permute-start.4) | collective-permute-done | bytes 131104 | tf_op jit(solution)/shard_map/ppermute | solution.py:27
  27.9 1.5 %collective-permute-start.10 = (bf16[64,2048]{1,0:T(8,128)(2,1)S(1)}, bf16[64,2048]{1,0:T(8,128)(2,1)S(1)}, u32[]{:S(2)}, u32[]{:S(2)}) collective-permute-start(bf16[64,2048]{1,0:T(8,128)(2,1)S(1)} %pad_maximum_fusion.6.refs_1_), channel_id=1, source_target_pairs={{0,2},{1,3},{2,0},{3,1},{4,6},{5,7},{6,4},{7,5},{8,10},{9,11},{10,... | collective-permute-start | bytes 786440 | tf_op jit(solution)/shard_map/ppermute | solution.py:31
  29.4 0.5 collective-permute-start.9
  30.0 0.5 collective-permute-start.8
  30.5 3.9 %collective-permute-done.10.refs_1_ = bf16[64,2048]{1,0:T(8,128)(2,1)S(1)} collective-permute-done((bf16[64,2048]{1,0:T(8,128)(2,1)S(1)}, bf16[64,2048]{1,0:T(8,128)(2,1)S(1)}, u32[]{:S(2)}, u32[]{:S(2)}) %collective-permute-start.10) | collective-permute-done | bytes 262176 | tf_op jit(solution)/shard_map/ppermute | solution.py:31
  34.4 1.9 %collective-permute-start.17 = (bf16[128,2048]{1,0:T(8,128)(2,1)S(1)}, bf16[128,2048]{1,0:T(8,128)(2,1)S(1)}, u32[]{:S(2)}, u32[]{:S(2)}) collective-permute-start(bf16[128,2048]{1,0:T(8,128)(2,1)S(1)} %pad_maximum_fusion.1), channel_id=1, source_target_pairs={{0,1},{1,0},{2,3},{3,2},{4,5},{5,4},{6,7},{7,6},{8,9},{9,8},{10,11... | collective-permute-start | bytes 1572872 | tf_op jit(solution)/shard_map/ppermute | solution.py:31
  36.4 1.9 %collective-permute-done.9.refs_0_ = bf16[64,2048]{1,0:T(8,128)(2,1)S(1)} collective-permute-done((bf16[64,2048]{1,0:T(8,128)(2,1)S(1)}, bf16[64,2048]{1,0:T(8,128)(2,1)S(1)}, u32[]{:S(2)}, u32[]{:S(2)}) %collective-permute-start.9) | collective-permute-done | bytes 262176 | tf_op jit(solution)/shard_map/ppermute | solution.py:31
  38.4 1.4 %project.7 = bf16[2,3,256,128]{3,2,1,0:T(8,128)(2,1)S(1)} custom-call(bf16[64,2048]{1,0:T(8,128)(2,1)S(1)} %pad_maximum_fusion.5.refs_0_, bf16[64,2048]{1,0:T(8,128)(2,1)S(1)} %pad_maximum_fusion.6.refs_1_, bf16[64,2048]{1,0:T(8,128)(2,1)S(1)} %collective-permute-done.7.refs_2_, bf16[64,2048]{1,0:T(8,128)(2,1)S(1)} %collective-permute-done.8.refs_3_, ...), custom_call_target="tpu_custom_call" | custom-call | tf_op jit(solution)/shard_map/project/pallas_call | solution.py:138
  40.0 0.5 collective-permute-start.12
  40.5 2.9 %collective-permute-start.13 = (bf16[2,3,256,128]{3,2,1,0:T(8,128)(2,1)S(1)}, bf16[2,3,256,128]{3,2,1,0:T(8,128)(2,1)S(1)}, u32[]{:S(2)}, u32[]{:S(2)}) collective-permute-start(bf16[2,3,256,128]{3,2,1,0:T(8,128)(2,1)S(1)} %project.7), channel_id=1, source_target_pairs={{0,8},{4,12},{24,16},{28,20},{1,9},{5,13},{25,17},{29,21},{2,10},{... | collective-permute-start | bytes 1179656 | tf_op jit(solution)/shard_map/ppermute | solution.py:185
  43.4 1.4 %project.9 = bf16[2,3,256,128]{3,2,1,0:T(8,128)(2,1)S(1)} custom-call(bf16[64,2048]{1,0:T(8,128)(2,1)S(1)} %collective-permute-done.9.refs_0_, bf16[64,2048]{1,0:T(8,128)(2,1)S(1)} %collective-permute-done.10.refs_1_, bf16[64,2048]{1,0:T(8,128)(2,1)S(1)} %collective-permute-done.11.refs_2_, bf16[64,2048]{1,0:T(8,128)(2,1)S(1)} %collective-permute-done.12.refs_3_, ...), custom_call_target="tpu_custom_call" | custom-call | tf_op jit(solution)/shard_map/project/pallas_call | solution.py:138
  44.8 2.3 %collective-permute-done.17.refs_0_ = bf16[128,2048]{1,0:T(8,128)(2,1)S(1)} collective-permute-done((bf16[128,2048]{1,0:T(8,128)(2,1)S(1)}, bf16[128,2048]{1,0:T(8,128)(2,1)S(1)}, u32[]{:S(2)}, u32[]{:S(2)}) %collective-permute-start.17) | collective-permute-done | bytes 524320 | tf_op jit(solution)/shard_map/ppermute | solution.py:31
  47.1 0.5 collective-permute-done.18.refs_1_
  47.6 0.5 collective-permute-start.20
  48.1 4.6 %collective-permute-start.14 = (bf16[2,3,256,128]{3,2,1,0:T(8,128)(2,1)S(1)}, bf16[2,3,256,128]{3,2,1,0:T(8,128)(2,1)S(1)}, u32[]{:S(2)}, u32[]{:S(2)}) collective-permute-start(bf16[2,3,256,128]{3,2,1,0:T(8,128)(2,1)S(1)} %project.9), channel_id=1, source_target_pairs={{0,8},{4,12},{24,16},{28,20},{1,9},{5,13},{25,17},{29,21},{2,10},{... | collective-permute-start | bytes 1179656 | tf_op jit(solution)/shard_map/ppermute | solution.py:185
  52.7 0.1 fusion.4
  52.9 2.3 %project.10 = (bf16[3,512,128]{2,1,0:T(8,128)(2,1)S(1)}, bf16[3,512,128]{2,1,0:T(8,128)(2,1)S(1)}) custom-call(bf16[128,2048]{1,0:T(8,128)(2,1)S(1)} %collective-permute-done.17.refs_0_, bf16[128,2048]{1,0:T(8,128)(2,1)S(1)} %collective-permute-done.18.refs_1_, bf16[128,2048]{1,0:T(8,128)(2,1)S(1)} %collective-permute-done.19.refs_2_, ...), custom_call_target="tpu_custom_call" | custom-call | tf_op jit(solution)/shard_map/project/pallas_call | solution.py:138
  55.2 3.6 %collective-permute-start.23 = (bf16[3,512,128]{2,1,0:T(8,128)(2,1)S(1)}, bf16[3,512,128]{2,1,0:T(8,128)(2,1)S(1)}, u32[]{:S(2)}, u32[]{:S(2)}) collective-permute-start(bf16[3,512,128]{2,1,0:T(8,128)(2,1)S(1)} %get-tuple-element.48), channel_id=1, source_target_pairs={{0,8},{4,12},{24,16},{28,20},{1,9},{5,13},{25,17},{29,21},{2,10},{... | collective-permute-start | bytes 1179656 | tf_op jit(solution)/shard_map/ppermute | solution.py:185
  58.8 3.3 %collective-permute-done.14 = bf16[2,3,256,128]{3,2,1,0:T(8,128)(2,1)S(1)} collective-permute-done((bf16[2,3,256,128]{3,2,1,0:T(8,128)(2,1)S(1)}, bf16[2,3,256,128]{3,2,1,0:T(8,128)(2,1)S(1)}, u32[]{:S(2)}, u32[]{:S(2)}) %collective-permute-start.14) | collective-permute-done | bytes 393248 | tf_op jit(solution)/shard_map/ppermute | solution.py:185
  62.2 0.1 fusion.5
  62.3 0.7 collective-permute-start.15
  63.0 1.5 %project.6 = (bf16[3,256,128]{2,1,0:T(8,128)(2,1)S(1)}, bf16[3,256,128]{2,1,0:T(8,128)(2,1)S(1)}) custom-call(bf16[64,2048]{1,0:T(8,128)(2,1)S(1)} %pad_maximum_fusion.5.refs_0_, bf16[64,2048]{1,0:T(8,128)(2,1)S(1)} %pad_maximum_fusion.6.refs_1_, bf16[64,2048]{1,0:T(8,128)(2,1)S(1)} %collective-permute-done.7.refs_2_, ...), custom_call_target="tpu_custom_call" | custom-call | tf_op jit(solution)/shard_map/project/pallas_call | solution.py:138
  64.5 1.5 %project.8 = (bf16[3,256,128]{2,1,0:T(8,128)(2,1)S(1)}, bf16[3,256,128]{2,1,0:T(8,128)(2,1)S(1)}) custom-call(bf16[64,2048]{1,0:T(8,128)(2,1)S(1)} %collective-permute-done.9.refs_0_, bf16[64,2048]{1,0:T(8,128)(2,1)S(1)} %collective-permute-done.10.refs_1_, bf16[64,2048]{1,0:T(8,128)(2,1)S(1)} %collective-permute-done.11.refs_2_, ...), custom_call_target="tpu_custom_call" | custom-call | tf_op jit(solution)/shard_map/project/pallas_call | solution.py:138
  66.0 7.4 %collective-permute-start.21 = (bf16[3,512,128]{2,1,0:T(8,128)(2,1)S(1)}, bf16[3,512,128]{2,1,0:T(8,128)(2,1)S(1)}, u32[]{:S(2)}, u32[]{:S(2)}) collective-permute-start(bf16[3,512,128]{2,1,0:T(8,128)(2,1)S(1)} %get-tuple-element.49), channel_id=1, source_target_pairs={{0,8},{4,12},{24,16},{28,20},{1,9},{5,13},{25,17},{29,21},{2,10},{... | collective-permute-start | bytes 1179656 | tf_op jit(solution)/shard_map/ppermute | solution.py:185
  73.5 0.1 add_convert_fusion.1
  73.6 0.7 collective-permute-start.24
  74.3 0.1 add_convert_fusion.3
  74.4 1.8 %collective-permute-start.16 = (bf16[3,512,128]{2,1,0:T(8,128)(2,1)S(1)}, bf16[3,512,128]{2,1,0:T(8,128)(2,1)S(1)}, u32[]{:S(2)}, u32[]{:S(2)}) collective-permute-start(bf16[3,512,128]{2,1,0:T(8,128)(2,1)S(1)} %add_convert_fusion.3), channel_id=1, source_target_pairs={{0,8},{4,12},{8,0},{12,4},{16,24},{20,28},{24,16},{28,20},{1,9},{5... | collective-permute-start | bytes 1179656 | tf_op jit(solution)/shard_map/ppermute | solution.py:185
  76.2 2.4 %project.11 = (bf16[3,512,128]{2,1,0:T(8,128)(2,1)S(1)}, bf16[3,512,128]{2,1,0:T(8,128)(2,1)S(1)}) custom-call(bf16[128,2048]{1,0:T(8,128)(2,1)S(1)} %collective-permute-done.17.refs_0_, bf16[128,2048]{1,0:T(8,128)(2,1)S(1)} %collective-permute-done.18.refs_1_, bf16[128,2048]{1,0:T(8,128)(2,1)S(1)} %collective-permute-done.19.refs_2_, ...), custom_call_target="tpu_custom_call" | custom-call | tf_op jit(solution)/shard_map/project/pallas_call | solution.py:138
  78.5 4.5 %collective-permute-done.21 = bf16[3,512,128]{2,1,0:T(8,128)(2,1)S(1)} collective-permute-done((bf16[3,512,128]{2,1,0:T(8,128)(2,1)S(1)}, bf16[3,512,128]{2,1,0:T(8,128)(2,1)S(1)}, u32[]{:S(2)}, u32[]{:S(2)}) %collective-permute-start.21) | collective-permute-done | bytes 393248 | tf_op jit(solution)/shard_map/ppermute | solution.py:185
  83.0 0.1 add_convert_fusion.2
  83.1 0.8 fusion
  84.0 0.7 collective-permute-start.26
  84.7 0.9 add_convert_fusion
  85.5 3.9 %collective-permute-start.25 = (bf16[3,512,128]{2,1,0:T(8,128)(2,1)}, bf16[3,512,128]{2,1,0:T(8,128)(2,1)S(1)}, u32[]{:S(2)}, u32[]{:S(2)}) collective-permute-start(bf16[3,512,128]{2,1,0:T(8,128)(2,1)} %add_convert_fusion), channel_id=1, source_target_pairs={{0,8},{4,12},{8,0},{12,4},{16,24},{20,28},{24,16},{28,20},{1,9},{5... | collective-permute-start | bytes 1179656 | tf_op jit(solution)/shard_map/ppermute | solution.py:185
  89.5 0.7 fusion.1
  90.2 0.7 collective-permute-start.22
  91.0 0.4 collective-permute-done.16.refs_2_
  91.4 5.5 %collective-permute-done.25.refs_5_ = bf16[3,512,128]{2,1,0:T(8,128)(2,1)S(1)} collective-permute-done((bf16[3,512,128]{2,1,0:T(8,128)(2,1)}, bf16[3,512,128]{2,1,0:T(8,128)(2,1)S(1)}, u32[]{:S(2)}, u32[]{:S(2)}) %collective-permute-start.25) | collective-permute-done | bytes 393248 | tf_op jit(solution)/shard_map/ppermute | solution.py:185
  96.9 2.8 %convolve.1.refs_7_ = f32[1024,128]{1,0:T(8,128)S(1)} custom-call(s32[3]{0:T(128)S(1)} %pad_add_fusion.1.refs_0_, bf16[3,512,128]{2,1,0:T(8,128)(2,1)S(1)} %constant_dynamic-update-slice_fusion.refs_1_, bf16[3,512,128]{2,1,0:T(8,128)(2,1)S(1)} %collective-permute-done.16.refs_2_, bf16[2,1024,128]{2,1,0:T(8,128)(2,1)S(1)} %collective-permute-done.26.refs_3_, ...), custom_call_target="tpu_custom_call" | custom-call | tf_op jit(solution)/shard_map/convolve/pallas_call | solution.py:333
  99.7 0.8 gate.1
  100.5 2.4 %collective-permute-start.27 = (bf16[2,128,128]{2,1,0:T(8,128)(2,1)S(1)}, bf16[2,128,128]{2,1,0:T(8,128)(2,1)S(1)}, u32[]{:S(2)}, u32[]{:S(2)}) collective-permute-start(bf16[2,128,128]{2,1,0:T(8,128)(2,1)S(1)} %get-tuple-element.58), channel_id=1, source_target_pairs={{0,8},{4,12},{8,0},{12,4},{16,24},{20,28},{24,16},{28,20},{1,9},{5... | collective-permute-start | bytes 196616 | tf_op jit(solution)/shard_map/ppermute | solution.py:27
  103.0 0.4 collective-permute-start.28
  103.4 2.0 %collective-permute-start.29 = (bf16[2,128,128]{2,1,0:T(8,128)(2,1)S(1)}, bf16[2,128,128]{2,1,0:T(8,128)(2,1)S(1)}, u32[]{:S(2)}, u32[]{:S(2)}) collective-permute-start(bf16[2,128,128]{2,1,0:T(8,128)(2,1)S(1)} %get-tuple-element.60), channel_id=1, source_target_pairs={{0,24},{4,28},{8,16},{12,20},{16,8},{20,12},{24,0},{28,4},{1,25},{... | collective-permute-start | bytes 196616 | tf_op jit(solution)/shard_map/ppermute | solution.py:27
  105.4 4.2 %collective-permute-done.29.refs_4_ = bf16[2,128,128]{2,1,0:T(8,128)(2,1)S(1)} collective-permute-done((bf16[2,128,128]{2,1,0:T(8,128)(2,1)S(1)}, bf16[2,128,128]{2,1,0:T(8,128)(2,1)S(1)}, u32[]{:S(2)}, u32[]{:S(2)}) %collective-permute-start.29) | collective-permute-done | bytes 65568 | tf_op jit(solution)/shard_map/ppermute | solution.py:27
  109.8 1.3 %collective-permute-done.30.refs_5_ = bf16[4,128,128]{2,1,0:T(8,128)(2,1)S(1)} collective-permute-done((bf16[4,128,128]{2,1,0:T(8,128)(2,1)S(1)}, bf16[4,128,128]{2,1,0:T(8,128)(2,1)S(1)}, u32[]{:S(2)}, u32[]{:S(2)}) %collective-permute-start.30) | collective-permute-done | bytes 131104 | tf_op jit(solution)/shard_map/ppermute | solution.py:22
  111.1 1.3 %collect_columns.1 = bf16[128,1024]{1,0:T(8,128)(2,1)} custom-call(s32[2]{0:T(128)S(1)} %pad_add_fusion.refs_0_, bf16[2,128,128]{2,1,0:T(8,128)(2,1)S(1)} %get-tuple-element.57.refs_1_, bf16[2,128,128]{2,1,0:T(8,128)(2,1)S(1)} %collective-permute-done.27.refs_2_, bf16[2,128,128]{2,1,0:T(8,128)(2,1)S(1)} %collective-permute-done.28.refs_3_, ...), custom_call_target="tpu_custom_call" | custom-call | tf_op jit(solution)/shard_map/collect_columns/pallas_call | solution.py:440
  (54 shorter events, 1.2 us)
Async XLA Ops:
  0.0 18.5 %copy-start = (f32[3,3,1024]{2,1,0:T(4,128)S(1)}, f32[3,3,1024]{2,1,0:T(4,128)}, u32[]{:S(2)}) copy-start(f32[3,3,1024]{2,1,0:T(4,128)} %param.8) | copy-start | bytes 110596
  0.0 18.5 %collective-permute-start.6 = (bf16[3,1024,1024]{2,1,0:T(8,128)(2,1)}, bf16[3,1024,1024]{2,1,0:T(8,128)(2,1)}, u32[]{:S(2)}, u32[]{:S(2)}) collective-permute-start(bf16[3,1024,1024]{2,1,0:T(8,128)(2,1)} %bitcast.42), channel_id=1, source_target_pairs={{0,4},{4,0},{8,12},{12,8},{16,20},{20,16},{24,28},{28,24},{1,5},{5... | collective-permute-start | bytes 18874376 | tf_op jit(solution)/shard_map/ppermute | solution.py:22
  1.5 7.8 %collective-permute-start = (bf16[32,2048]{1,0:T(8,128)(2,1)S(1)}, bf16[32,2048]{1,0:T(8,128)(2,1)S(1)}, u32[]{:S(2)}, u32[]{:S(2)}) collective-permute-start(bf16[32,2048]{1,0:T(8,128)(2,1)S(1)} %get-tuple-element.75), channel_id=1, source_target_pairs={{0,3},{1,2},{2,1},{3,0},{4,7},{5,6},{6,5},{7,4},{8,11},{9,10},{10,... | collective-permute-start | bytes 393224 | tf_op jit(solution)/shard_map/ppermute | solution.py:31
  5.1 6.9 %collective-permute-start.1 = (bf16[32,2048]{1,0:T(8,128)(2,1)S(1)}, bf16[32,2048]{1,0:T(8,128)(2,1)S(1)}, u32[]{:S(2)}, u32[]{:S(2)}) collective-permute-start(bf16[32,2048]{1,0:T(8,128)(2,1)S(1)} %get-tuple-element.74), channel_id=1, source_target_pairs={{0,2},{1,3},{2,0},{3,1},{4,6},{5,7},{6,4},{7,5},{8,10},{9,11},{10,... | collective-permute-start | bytes 393224 | tf_op jit(solution)/shard_map/ppermute | solution.py:31
  5.6 6.7 %collective-permute-start.2 = (bf16[32,2048]{1,0:T(8,128)(2,1)S(1)}, bf16[32,2048]{1,0:T(8,128)(2,1)S(1)}, u32[]{:S(2)}, u32[]{:S(2)}) collective-permute-start(bf16[32,2048]{1,0:T(8,128)(2,1)S(1)} %get-tuple-element.73), channel_id=1, source_target_pairs={{0,1},{1,0},{2,3},{3,2},{4,5},{5,4},{6,7},{7,6},{8,9},{9,8},{10,11... | collective-permute-start | bytes 393224 | tf_op jit(solution)/shard_map/ppermute | solution.py:31
  13.3 11.4 %collective-permute-start.3 = (bf16[32,2048]{1,0:T(8,128)(2,1)S(1)}, bf16[32,2048]{1,0:T(8,128)(2,1)S(1)}, u32[]{:S(2)}, u32[]{:S(2)}) collective-permute-start(bf16[32,2048]{1,0:T(8,128)(2,1)S(1)} %get-tuple-element.63), channel_id=1, source_target_pairs={{0,8},{4,12},{8,0},{12,4},{16,24},{20,28},{24,16},{28,20},{1,9},{5... | collective-permute-start | bytes 393224 | tf_op jit(solution)/shard_map/ppermute | solution.py:27
  14.9 12.9 %collective-permute-start.4 = (bf16[32,2048]{1,0:T(8,128)(2,1)S(1)}, bf16[32,2048]{1,0:T(8,128)(2,1)S(1)}, u32[]{:S(2)}, u32[]{:S(2)}) collective-permute-start(bf16[32,2048]{1,0:T(8,128)(2,1)S(1)} %get-tuple-element.62), channel_id=1, source_target_pairs={{0,16},{4,20},{8,24},{12,28},{16,0},{20,4},{24,8},{28,12},{1,17},{... | collective-permute-start | bytes 393224 | tf_op jit(solution)/shard_map/ppermute | solution.py:27
  17.5 10.3 %collective-permute-start.5 = (bf16[32,2048]{1,0:T(8,128)(2,1)S(1)}, bf16[32,2048]{1,0:T(8,128)(2,1)S(1)}, u32[]{:S(2)}, u32[]{:S(2)}) collective-permute-start(bf16[32,2048]{1,0:T(8,128)(2,1)S(1)} %get-tuple-element.61), channel_id=1, source_target_pairs={{0,24},{4,28},{8,16},{12,20},{16,8},{20,12},{24,0},{28,4},{1,25},{... | collective-permute-start | bytes 393224 | tf_op jit(solution)/shard_map/ppermute | solution.py:27
  18.5 2.8 %copy-start.1 = (bf16[1024,3,1024]{2,0,1:T(8,128)(2,1)S(1)}, bf16[1024,3,1024]{2,0,1:T(8,128)(2,1)}, u32[]{:S(2)}) copy-start(bf16[1024,3,1024]{2,0,1:T(8,128)(2,1)} %param.7) | copy-start | bytes 18874372
  27.9 6.4 %collective-permute-start.10 = (bf16[64,2048]{1,0:T(8,128)(2,1)S(1)}, bf16[64,2048]{1,0:T(8,128)(2,1)S(1)}, u32[]{:S(2)}, u32[]{:S(2)}) collective-permute-start(bf16[64,2048]{1,0:T(8,128)(2,1)S(1)} %pad_maximum_fusion.6.refs_1_), channel_id=1, source_target_pairs={{0,2},{1,3},{2,0},{3,1},{4,6},{5,7},{6,4},{7,5},{8,10},{9,11},{10,... | collective-permute-start | bytes 786440 | tf_op jit(solution)/shard_map/ppermute | solution.py:31
  29.4 8.8 %collective-permute-start.9 = (bf16[64,2048]{1,0:T(8,128)(2,1)S(1)}, bf16[64,2048]{1,0:T(8,128)(2,1)S(1)}, u32[]{:S(2)}, u32[]{:S(2)}) collective-permute-start(bf16[64,2048]{1,0:T(8,128)(2,1)S(1)} %pad_maximum_fusion.5.refs_0_), channel_id=1, source_target_pairs={{0,1},{1,0},{2,3},{3,2},{4,5},{5,4},{6,7},{7,6},{8,9},{9,8},{10,11... | collective-permute-start | bytes 786440 | tf_op jit(solution)/shard_map/ppermute | solution.py:31
  29.9 8.5 %collective-permute-start.7 = (bf16[64,2048]{1,0:T(8,128)(2,1)S(1)}, bf16[64,2048]{1,0:T(8,128)(2,1)S(1)}, u32[]{:S(2)}, u32[]{:S(2)}) collective-permute-start(bf16[64,2048]{1,0:T(8,128)(2,1)S(1)} %pad_maximum_fusion.5.refs_0_), channel_id=1, source_target_pairs={{0,4},{4,0},{8,12},{12,8},{16,20},{20,16},{24,28},{28,24},{1,5},{5... | collective-permute-start | bytes 786440 | tf_op jit(solution)/shard_map/ppermute | solution.py:22
  30.0 8.5 %collective-permute-start.8 = (bf16[64,2048]{1,0:T(8,128)(2,1)S(1)}, bf16[64,2048]{1,0:T(8,128)(2,1)S(1)}, u32[]{:S(2)}, u32[]{:S(2)}) collective-permute-start(bf16[64,2048]{1,0:T(8,128)(2,1)S(1)} %pad_maximum_fusion.6.refs_1_), channel_id=1, source_target_pairs={{0,4},{4,0},{8,12},{12,8},{16,20},{20,16},{24,28},{28,24},{1,5},{5... | collective-permute-start | bytes 786440 | tf_op jit(solution)/shard_map/ppermute | solution.py:22
  34.4 12.7 %collective-permute-start.17 = (bf16[128,2048]{1,0:T(8,128)(2,1)S(1)}, bf16[128,2048]{1,0:T(8,128)(2,1)S(1)}, u32[]{:S(2)}, u32[]{:S(2)}) collective-permute-start(bf16[128,2048]{1,0:T(8,128)(2,1)S(1)} %pad_maximum_fusion.1), channel_id=1, source_target_pairs={{0,1},{1,0},{2,3},{3,2},{4,5},{5,4},{6,7},{7,6},{8,9},{9,8},{10,11... | collective-permute-start | bytes 1572872 | tf_op jit(solution)/shard_map/ppermute | solution.py:31
  38.3 9.2 %collective-permute-start.18 = (bf16[128,2048]{1,0:T(8,128)(2,1)S(1)}, bf16[128,2048]{1,0:T(8,128)(2,1)S(1)}, u32[]{:S(2)}, u32[]{:S(2)}) collective-permute-start(bf16[128,2048]{1,0:T(8,128)(2,1)S(1)} %pad_maximum_fusion.2), channel_id=1, source_target_pairs={{0,2},{1,3},{2,0},{3,1},{4,6},{5,7},{6,4},{7,5},{8,10},{9,11},{10,... | collective-permute-start | bytes 1572872 | tf_op jit(solution)/shard_map/ppermute | solution.py:31
  39.9 3.5 %collective-permute-start.11 = (bf16[64,2048]{1,0:T(8,128)(2,1)S(1)}, bf16[64,2048]{1,0:T(8,128)(2,1)S(1)}, u32[]{:S(2)}, u32[]{:S(2)}) collective-permute-start(bf16[64,2048]{1,0:T(8,128)(2,1)S(1)} %collective-permute-done.9.refs_0_), channel_id=1, source_target_pairs={{0,4},{4,0},{8,12},{12,8},{16,20},{20,16},{24,28},{28,24},{1,5},{5... | collective-permute-start | bytes 786440 | tf_op jit(solution)/shard_map/ppermute | solution.py:22
  40.0 3.4 %collective-permute-start.12 = (bf16[64,2048]{1,0:T(8,128)(2,1)S(1)}, bf16[64,2048]{1,0:T(8,128)(2,1)S(1)}, u32[]{:S(2)}, u32[]{:S(2)}) collective-permute-start(bf16[64,2048]{1,0:T(8,128)(2,1)S(1)} %collective-permute-done.10.refs_1_), channel_id=1, source_target_pairs={{0,4},{4,0},{8,12},{12,8},{16,20},{20,16},{24,28},{28,24},{1,5},{5... | collective-permute-start | bytes 786440 | tf_op jit(solution)/shard_map/ppermute | solution.py:22
  40.5 12.3 %collective-permute-start.13 = (bf16[2,3,256,128]{3,2,1,0:T(8,128)(2,1)S(1)}, bf16[2,3,256,128]{3,2,1,0:T(8,128)(2,1)S(1)}, u32[]{:S(2)}, u32[]{:S(2)}) collective-permute-start(bf16[2,3,256,128]{3,2,1,0:T(8,128)(2,1)S(1)} %project.7), channel_id=1, source_target_pairs={{0,8},{4,12},{24,16},{28,20},{1,9},{5,13},{25,17},{29,21},{2,10},{... | collective-permute-start | bytes 1179656 | tf_op jit(solution)/shard_map/ppermute | solution.py:185
  47.6 5.3 %collective-permute-start.19 = (bf16[128,2048]{1,0:T(8,128)(2,1)S(1)}, bf16[128,2048]{1,0:T(8,128)(2,1)S(1)}, u32[]{:S(2)}, u32[]{:S(2)}) collective-permute-start(bf16[128,2048]{1,0:T(8,128)(2,1)S(1)} %collective-permute-done.17.refs_0_), channel_id=1, source_target_pairs={{0,4},{4,0},{8,12},{12,8},{16,20},{20,16},{24,28},{28,24},{1,5},{5... | collective-permute-start | bytes 1572872 | tf_op jit(solution)/shard_map/ppermute | solution.py:22
  47.6 5.3 %collective-permute-start.20 = (bf16[128,2048]{1,0:T(8,128)(2,1)S(1)}, bf16[128,2048]{1,0:T(8,128)(2,1)S(1)}, u32[]{:S(2)}, u32[]{:S(2)}) collective-permute-start(bf16[128,2048]{1,0:T(8,128)(2,1)S(1)} %collective-permute-done.18.refs_1_), channel_id=1, source_target_pairs={{0,4},{4,0},{8,12},{12,8},{16,20},{20,16},{24,28},{28,24},{1,5},{5... | collective-permute-start | bytes 1572872 | tf_op jit(solution)/shard_map/ppermute | solution.py:22
  48.1 14.1 %collective-permute-start.14 = (bf16[2,3,256,128]{3,2,1,0:T(8,128)(2,1)S(1)}, bf16[2,3,256,128]{3,2,1,0:T(8,128)(2,1)S(1)}, u32[]{:S(2)}, u32[]{:S(2)}) collective-permute-start(bf16[2,3,256,128]{3,2,1,0:T(8,128)(2,1)S(1)} %project.9), channel_id=1, source_target_pairs={{0,8},{4,12},{24,16},{28,20},{1,9},{5,13},{25,17},{29,21},{2,10},{... | collective-permute-start | bytes 1179656 | tf_op jit(solution)/shard_map/ppermute | solution.py:185
  55.2 18.3 %collective-permute-start.23 = (bf16[3,512,128]{2,1,0:T(8,128)(2,1)S(1)}, bf16[3,512,128]{2,1,0:T(8,128)(2,1)S(1)}, u32[]{:S(2)}, u32[]{:S(2)}) collective-permute-start(bf16[3,512,128]{2,1,0:T(8,128)(2,1)S(1)} %get-tuple-element.48), channel_id=1, source_target_pairs={{0,8},{4,12},{24,16},{28,20},{1,9},{5,13},{25,17},{29,21},{2,10},{... | collective-permute-start | bytes 1179656 | tf_op jit(solution)/shard_map/ppermute | solution.py:185
  62.3 12.0 %collective-permute-start.15 = (bf16[3,512,128]{2,1,0:T(8,128)(2,1)S(1)}, bf16[3,512,128]{2,1,0:T(8,128)(2,1)S(1)}, u32[]{:S(2)}, u32[]{:S(2)}) collective-permute-start(bf16[3,512,128]{2,1,0:T(8,128)(2,1)S(1)} %pad_maximum_fusion.3), channel_id=1, source_target_pairs={{8,16},{12,20},{16,8},{20,12},{9,17},{13,21},{17,9},{21,13},{10,18... | collective-permute-start | bytes 1179656 | tf_op jit(solution)/shard_map/ppermute | solution.py:185
  66.0 17.0 %collective-permute-start.21 = (bf16[3,512,128]{2,1,0:T(8,128)(2,1)S(1)}, bf16[3,512,128]{2,1,0:T(8,128)(2,1)S(1)}, u32[]{:S(2)}, u32[]{:S(2)}) collective-permute-start(bf16[3,512,128]{2,1,0:T(8,128)(2,1)S(1)} %get-tuple-element.49), channel_id=1, source_target_pairs={{0,8},{4,12},{24,16},{28,20},{1,9},{5,13},{25,17},{29,21},{2,10},{... | collective-permute-start | bytes 1179656 | tf_op jit(solution)/shard_map/ppermute | solution.py:185
  73.6 11.1 %collective-permute-start.24 = (bf16[3,512,128]{2,1,0:T(8,128)(2,1)S(1)}, bf16[3,512,128]{2,1,0:T(8,128)(2,1)S(1)}, u32[]{:S(2)}, u32[]{:S(2)}) collective-permute-start(bf16[3,512,128]{2,1,0:T(8,128)(2,1)S(1)} %add_convert_fusion.1), channel_id=1, source_target_pairs={{8,16},{12,20},{16,8},{20,12},{9,17},{13,21},{17,9},{21,13},{10,18... | collective-permute-start | bytes 1179656 | tf_op jit(solution)/shard_map/ppermute | solution.py:185
  74.4 17.0 %collective-permute-start.16 = (bf16[3,512,128]{2,1,0:T(8,128)(2,1)S(1)}, bf16[3,512,128]{2,1,0:T(8,128)(2,1)S(1)}, u32[]{:S(2)}, u32[]{:S(2)}) collective-permute-start(bf16[3,512,128]{2,1,0:T(8,128)(2,1)S(1)} %add_convert_fusion.3), channel_id=1, source_target_pairs={{0,8},{4,12},{8,0},{12,4},{16,24},{20,28},{24,16},{28,20},{1,9},{5... | collective-permute-start | bytes 1179656 | tf_op jit(solution)/shard_map/ppermute | solution.py:185
  84.0 7.4 %collective-permute-start.26 = (bf16[2,1024,128]{2,1,0:T(8,128)(2,1)}, bf16[2,1024,128]{2,1,0:T(8,128)(2,1)S(1)}, u32[]{:S(2)}, u32[]{:S(2)}) collective-permute-start(bf16[2,1024,128]{2,1,0:T(8,128)(2,1)} %fusion), channel_id=1, source_target_pairs={{8,16},{12,20},{16,8},{20,12},{9,17},{13,21},{17,9},{21,13},{10,18... | collective-permute-start | bytes 1572872 | tf_op jit(solution)/shard_map/ppermute | solution.py:185
  85.5 11.3 %collective-permute-start.25 = (bf16[3,512,128]{2,1,0:T(8,128)(2,1)}, bf16[3,512,128]{2,1,0:T(8,128)(2,1)S(1)}, u32[]{:S(2)}, u32[]{:S(2)}) collective-permute-start(bf16[3,512,128]{2,1,0:T(8,128)(2,1)} %add_convert_fusion), channel_id=1, source_target_pairs={{0,8},{4,12},{8,0},{12,4},{16,24},{20,28},{24,16},{28,20},{1,9},{5... | collective-permute-start | bytes 1179656 | tf_op jit(solution)/shard_map/ppermute | solution.py:185
  90.2 9.6 %collective-permute-start.22 = (bf16[1,1024,128]{2,1,0:T(8,128)(2,1)}, bf16[1,1024,128]{2,1,0:T(8,128)(2,1)S(1)}, u32[]{:S(2)}, u32[]{:S(2)}) collective-permute-start(bf16[1,1024,128]{2,1,0:T(8,128)(2,1)} %fusion.1), channel_id=1, source_target_pairs={{8,16},{12,20},{16,8},{20,12},{9,17},{13,21},{17,9},{21,13},{10,18... | collective-permute-start | bytes 786440 | tf_op jit(solution)/shard_map/ppermute | solution.py:185
  100.5 9.1 %collective-permute-start.27 = (bf16[2,128,128]{2,1,0:T(8,128)(2,1)S(1)}, bf16[2,128,128]{2,1,0:T(8,128)(2,1)S(1)}, u32[]{:S(2)}, u32[]{:S(2)}) collective-permute-start(bf16[2,128,128]{2,1,0:T(8,128)(2,1)S(1)} %get-tuple-element.58), channel_id=1, source_target_pairs={{0,8},{4,12},{8,0},{12,4},{16,24},{20,28},{24,16},{28,20},{1,9},{5... | collective-permute-start | bytes 196616 | tf_op jit(solution)/shard_map/ppermute | solution.py:27
  103.0 6.6 %collective-permute-start.28 = (bf16[2,128,128]{2,1,0:T(8,128)(2,1)S(1)}, bf16[2,128,128]{2,1,0:T(8,128)(2,1)S(1)}, u32[]{:S(2)}, u32[]{:S(2)}) collective-permute-start(bf16[2,128,128]{2,1,0:T(8,128)(2,1)S(1)} %get-tuple-element.59), channel_id=1, source_target_pairs={{0,16},{4,20},{8,24},{12,28},{16,0},{20,4},{24,8},{28,12},{1,17},{... | collective-permute-start | bytes 196616 | tf_op jit(solution)/shard_map/ppermute | solution.py:27
  103.4 6.2 %collective-permute-start.29 = (bf16[2,128,128]{2,1,0:T(8,128)(2,1)S(1)}, bf16[2,128,128]{2,1,0:T(8,128)(2,1)S(1)}, u32[]{:S(2)}, u32[]{:S(2)}) collective-permute-start(bf16[2,128,128]{2,1,0:T(8,128)(2,1)S(1)} %get-tuple-element.60), channel_id=1, source_target_pairs={{0,24},{4,28},{8,16},{12,20},{16,8},{20,12},{24,0},{28,4},{1,25},{... | collective-permute-start | bytes 196616 | tf_op jit(solution)/shard_map/ppermute | solution.py:27
  109.7 1.4 %collective-permute-start.30 = (bf16[4,128,128]{2,1,0:T(8,128)(2,1)S(1)}, bf16[4,128,128]{2,1,0:T(8,128)(2,1)S(1)}, u32[]{:S(2)}, u32[]{:S(2)}) collective-permute-start(bf16[4,128,128]{2,1,0:T(8,128)(2,1)S(1)} %pad_maximum_fusion.7), channel_id=1, source_target_pairs={{0,4},{4,0},{8,12},{12,8},{16,20},{20,16},{24,28},{28,24},{1,5},{5... | collective-permute-start | bytes 393224 | tf_op jit(solution)/shard_map/ppermute | solution.py:22
